TPU v7x, 256 devices: a whole 4x4x8 slice. The times are simulated.
256 devices in a mesh: dp: 32 (over x, z_hi, core), tensor: 8 (over z_lo, y).
Axes of the slice: x: 4, y: 4, z: 8 (z_hi: 4, z_lo: 2; z = z_hi * 2 + z_lo), core: 2. Of those that a mesh axis runs over, the one named last changes fastest.
Arguments:
- acts: bfloat16 [16384, 4096], P('dp'), may hold values from -6 to 6
- output_grad: bfloat16 [16384, 4096], P('dp'), may hold values from -16 to 16
- gate_act: bfloat16 [16384, 14336], P('dp', 'tensor'), may hold values from -8 to 8
- down_weight: bfloat16 [14336, 4096], P('tensor', 'dp'), may hold values from -0.09375 to 0.09375
- proj_in: bfloat16 [64, 4096], replicated, may hold values from -0.09375 to 0.09375
- proj_out: bfloat16 [64, 14336], P(None, 'tensor'), may hold values from -0.046875 to 0.046875
- query: bfloat16 [1024, 4096], P('tensor', 'dp'), may hold values from -6 to 6
Outputs:
- gram: float32 [4096, 4096], P('dp', 'tensor')
- scores: float32 [64, 1024], P('dp', 'tensor')
All inputs are finite; a program needn't handle non-finite values.
Results may differ from a plain program's by a relative error of at most 0.0057.
Values may be sent and summed in bfloat16 or wider, within the bound.
No kernel may reach another device: no remote copies, remote signals or barrier semaphores. Data moves between devices by JAX's collectives and lax.ppermute only.
A program may use at most 128 MiB of HBM per device.

v0:
```python
import jax
import jax.numpy as jnp
from jax import lax
from jax.sharding import PartitionSpec as P

SEQ = 256


def outer_sum(out_side, in_side, examples):
    out_three = out_side.reshape(out_side.shape[0], examples, SEQ)
    in_three = in_side.reshape(in_side.shape[0], examples, SEQ)
    sketch = jnp.einsum("iel,jel->eij", out_three, in_three, precision=lax.Precision.HIGHEST)
    return sketch.reshape(examples, out_side.shape[0] * in_side.shape[0])


def body(acts, output_grad, gate_act, down_weight, proj_in, proj_out, query):
    tok_rows = acts.shape[0]
    examples = tok_rows // SEQ
    contract_last = (((1,), (1,)), ((), ()))
    contract_first = (((0,), (0,)), ((), ()))
    hidden_grad = lax.dot_general(
        output_grad,
        lax.all_gather(down_weight, "dp", axis=1, tiled=True),
        contract_last,
        preferred_element_type=jnp.float32,
    )
    up_grad = (hidden_grad * jax.nn.silu(gate_act.astype(jnp.float32))).astype(jnp.bfloat16)
    in_proj = lax.dot_general(proj_in, acts, contract_last, preferred_element_type=jnp.float32)
    out_part = lax.dot_general(proj_out, up_grad, contract_last, preferred_element_type=jnp.float32)
    out_proj = lax.psum(out_part, "tensor")
    sketch_full = outer_sum(out_proj, in_proj, examples)
    sketches = sketch_full.astype(jnp.bfloat16)
    sketch_width = sketches.shape[1]
    dp_count = lax.axis_size("dp")
    tensor_count = lax.axis_size("tensor")
    row_count = sketch_width // dp_count
    col_count = sketch_width // tensor_count
    row_start = lax.axis_index("dp") * row_count
    col_start = lax.axis_index("tensor") * col_count
    row_ids = row_start + lax.broadcasted_iota(jnp.int32, (row_count, col_count), 0)
    col_ids = col_start + lax.broadcasted_iota(jnp.int32, (row_count, col_count), 1)
    diagonal_mask = (row_ids == col_ids).astype(jnp.float32)
    wide = sketches.astype(jnp.float32)
    trace = lax.psum(jnp.sum(wide * wide), "dp")
    piece = lax.all_gather(sketches, "dp", axis=0, tiled=True)
    row_part = lax.dynamic_slice_in_dim(piece, row_start, row_count, 1)
    col_part = lax.dynamic_slice_in_dim(piece, col_start, col_count, 1)
    raw_gram = lax.dot_general(
        row_part, col_part, contract_first, preferred_element_type=jnp.float32
    )
    gram = raw_gram * (sketch_width / trace) + 0.1 * diagonal_mask
    raw_scores = lax.dot_general(
        sketches,
        lax.all_gather(query, "dp", axis=1, tiled=True),
        contract_last,
        preferred_element_type=jnp.float32,
    )
    scores = raw_scores / jnp.sqrt(trace / (examples * dp_count))
    return (gram, scores)


def solution(mesh):
    placed = (
        P("dp", None),
        P("dp", None),
        P("dp", "tensor"),
        P("tensor", "dp"),
        P(),
        P(None, "tensor"),
        P("tensor", "dp"),
    )
    return jax.shard_map(
        body,
        mesh=mesh,
        in_specs=placed,
        out_specs=(P("dp", "tensor"), P("dp", "tensor")),
        check_vma=False,
    )
```

profile of v0, /device:TPU:1, one launch (start us, length us, event | category | flops | bytes accessed | tf_op | source)
XLA Modules:
  0.0 350.9 jit_solution(17679257131715822224)
XLA Ops:
  7.2 0.0 copy-start
  7.2 0.0 all-gather.4.cloned.1.call-start
  7.2 0.7 all-gather.4.cloned.1.call-update
  7.9 0.0 all-reduce.2.cloned.1.call-start
  8.0 125.1 %all-gather.4.cloned.1.call-done = bf16[1792,4096]{1,0:T(8,128)(2,1)} async-done(((bf16[1792,128]{1,0:T(8,128)(2,1)}), bf16[1792,4096]{1,0:T(8,128)(2,1)}) %all-gather.4.cloned.1.call-update) | async-done | bytes 14680080 | tf_op jit(solution)/shard_map/all_gather | solution.py:23
  133.1 15.7 %fusion.5 = f32[512,64]{0,1:T(8,128)S(1)} fusion(bf16[64,1792]{1,0:T(8,128)(2,1)} %param.12, bf16[512,1792]{1,0:T(8,128)(2,1)} %param.9, bf16[512,4096]{1,0:T(8,128)(2,1)} %param.8, bf16[1792,4096]{1,0:T(8,128)(2,1)} %all-gather.4.cloned.1.call-done), kind=kOutput, calls=%fused_computation.7 | convolution fusion | flops 7640055808 | bytes 21069824 | tf_op jit(solution)/shard_map/dot_general | solution.py:29
  148.9 0.7 copy.22
  149.5 0.0 all-reduce.2.cloned.1.call-update
  149.5 0.0 all-gather.6.cloned.1.call-start
  149.6 0.7 all-gather.6.cloned.1.call-update
  150.3 0.0 copy-done
  150.3 3.6 %fusion.14 = f32[64,512]{1,0:T(8,128)S(1)} fusion(bf16[64,4096]{1,0:T(8,128)(2,1)S(1)} %copy-done, bf16[512,4096]{1,0:T(8,128)(2,1)} %param.7), kind=kOutput, calls=%fused_computation.23 | convolution fusion | flops 268435456 | bytes 4849664 | tf_op jit(solution)/shard_map/dot_general | solution.py:28
  153.9 67.2 %all-reduce.2.cloned.1.call-done = f32[64,2,256]{2,0,1:T(8,128)} async-done(((f32[64,2,256]{2,0,1:T(8,128)}), f32[64,2,256]{2,0,1:T(8,128)}) %all-reduce.2.cloned.1.call-update) | async-done | bytes 131088 | tf_op jit(solution)/shard_map/psum | solution.py:30
  221.1 1.8 multiply_reduce_fusion
  222.8 75.4 %psum.15 = f32[]{:T(128)} all-reduce(f32[]{:T(128)} %get-tuple-element.2), channel_id=1, replica_groups=mesh['dp'=32,'tensor'=8] {'dp'}, use_global_device_ids=true, to_apply=%region_2.3 | all-reduce | flops 1 | bytes 8 | tf_op jit(solution)/shard_map/psum | solution.py:44
  298.3 0.1 reshape.14
  298.4 0.1 convert_element_type.21
  299.8 41.3 %all-gather = bf16[32,2,4096]{2,1,0:T(2,128)(2,1)S(1)} all-gather(bf16[1,2,4096]{2,1,0:T(2,128)(2,1)S(1)} %reshape.14), channel_id=1, replica_groups=mesh['dp'=32,'tensor'=8] {'dp'}, dimensions={0}, use_global_device_ids=true | all-gather | bytes 540672 | tf_op jit(solution)/shard_map/all_gather | solution.py:45
  341.1 0.2 reshape.15
  341.3 0.9 fusion.7
  342.2 0.0 all-gather.6.cloned.1.call-done
  342.2 2.2 convolution_divide_fusion
  (2 shorter events, 0.0 us)
Async XLA Ops:
  7.2 143.2 %copy-start = (bf16[64,4096]{1,0:T(8,128)(2,1)S(1)}, bf16[64,4096]{1,0:T(8,128)(2,1)}, u32[]{:S(2)}) copy-start(bf16[64,4096]{1,0:T(8,128)(2,1)} %param.11) | copy-start | bytes 1572868
  7.2 125.9 %all-gather.4.cloned.1.call-start = ((), (), s32[]{:S(2)}) async-start(), calls=%async_computation | async-start | bytes 15138816 | tf_op jit(solution)/shard_map/all_gather | solution.py:23
  7.9 213.1 %all-reduce.2.cloned.1.call-start = ((), (), s32[]{:S(2)}) async-start(), calls=%async_computation.1 | async-start | bytes 262144 | tf_op jit(solution)/shard_map/psum | solution.py:30
  149.5 192.7 %all-gather.6.cloned.1.call-start = ((), (), s32[]{:S(2)}) async-start(), calls=%async_computation.2 | async-start | bytes 1081344 | tf_op jit(solution)/shard_map/all_gather | solution.py:54
Sparse Core Ops, SparseCore 0:
  10.5 122.5 all-gather.3
  149.7 71.3 all-reduce.1
  223.8 56.8 all-gather.5
where the time goes:
time: 351 us
  waiting for transfers between devices  194 us (55%)
  blocking collectives  117 us (33%)
  matrix products  24.2 us (7%)
  between operations  15.2 us (4%)
    all_gather x1, waiting for transfers between devices, body(): lax.all_gather(down_weight, 'dp', axis=1, tiled=True)  125 us
    psum x1, blocking collectives, body(): trace = lax.psum(jnp.sum(wide * wide), 'dp')  75.4 us
    psum x1, waiting for transfers between devices, body(): out_proj = lax.psum(out_part, 'tensor')  67.2 us
    all_gather x1, blocking collectives, body(): piece = lax.all_gather(sketches, 'dp', axis=0, tiled=True)  41.3 us
    dot_general x1, matrix products, body(): lax.dot_general(proj_out, up_grad, contract_last, preferred_element_type=...  15.7 us
  transfers between devices with their start and end apart: 3, of which 2 were waited for; matrix products, arithmetic and copies ran while one was open for 2% of the time, Pallas kernels for 0%

commit v1 on v0

v1 whole, which is shorter than its diff:
```python
import jax
import jax.numpy as jnp
from jax import lax
from jax.experimental import pallas as pl
from jax.experimental.pallas import tpu as pltpu
from jax.sharding import PartitionSpec as P

SEQ = 256
SIDE = 4
LANES = 128
F_TILE = 256
LAST = (((1,), (1,)), ((), ()))


def dp_id(x, z, c):
    return ((x % SIDE) * SIDE + z % SIDE) * 2 + c


PLACES = [(x, z, c) for x in range(SIDE) for z in range(SIDE) for c in range(2)]
SAME_CORE = [[dp_id(x, z, c) for x in range(SIDE) for z in range(SIDE)] for c in range(2)]


def dp_move(value, where):
    return lax.ppermute(value, "dp", [(dp_id(*s), dp_id(*where(*s))) for s in PLACES])


def x_step(value):
    return dp_move(value, lambda x, z, c: (x + 1 - 2 * c, z, c))


def z_step(value):
    return dp_move(value, lambda x, z, c: (x, z + 1 - 2 * c, c))


def core_swap(value):
    return dp_move(value, lambda x, z, c: (x, z, 1 - c))


def tensor_swap(value, bit):
    return lax.ppermute(value, "tensor", [(t, t ^ bit) for t in range(8)])


def after(value, *others):
    return lax.optimization_barrier((value,) + others)[0]


def part_kernel(count, has_total, table, *refs):
    grads, weights, rest = refs[:count], refs[count:2 * count], refs[2 * count:]
    left = jnp.concatenate([g[...] for g in grads], axis=1)
    right = jnp.concatenate([w[...] for w in weights], axis=1)
    value = lax.dot_general(left, right, LAST, preferred_element_type=jnp.float32)
    if has_total:
        value = value + rest[0][...]
    rest[-1][...] = value


def grad_spec(rows, k):
    return pl.BlockSpec((rows, LANES), lambda f, table: (0, table[k]))


def add_part(table, grad, pieces, total):
    count = len(pieces)
    rows = grad.shape[0]
    hidden = 1792
    total_spec = pl.BlockSpec((rows, F_TILE), lambda f, table: (0, f))
    in_specs = [grad_spec(rows, k) for k in range(count)]
    in_specs += [pl.BlockSpec((F_TILE, LANES), lambda f, table: (f, 0))] * count
    args = [grad] * count + pieces
    if total is not None:
        in_specs.append(total_spec)
        args.append(total)
    return pl.pallas_call(
        lambda *refs: part_kernel(count, total is not None, *refs),
        out_shape=jax.ShapeDtypeStruct((rows, hidden), jnp.float32),
        grid_spec=pltpu.PrefetchScalarGridSpec(
            num_scalar_prefetch=1, grid=(hidden // F_TILE,), in_specs=in_specs, out_specs=total_spec
        ),
        cost_estimate=pl.CostEstimate(
            flops=2 * rows * hidden * LANES * count,
            bytes_accessed=count * (rows + hidden) * LANES * 2 + 8 * rows * hidden,
            transcendentals=0,
        ),
    )(table, *args)


def sketch_kernel(count, table, *refs):
    grads, weights = refs[:count], refs[count:2 * count]
    total, gate, proj_out, in_proj, out, out_side = refs[2 * count:]
    f = pl.program_id(0)
    left = jnp.concatenate([g[...] for g in grads], axis=1)
    right = jnp.concatenate([w[...] for w in weights], axis=1)
    hidden_grad = total[...] + lax.dot_general(left, right, LAST, preferred_element_type=jnp.float32)
    v = gate[...].astype(jnp.float32)
    up_grad = (hidden_grad * (v / (1.0 + jnp.exp(-v)))).astype(jnp.bfloat16)
    part = lax.dot_general(proj_out[...], up_grad, LAST, preferred_element_type=jnp.float32)

    @pl.when(f == 0)
    def _():
        out_side[...] = part

    @pl.when(f > 0)
    def _():
        out_side[...] += part

    @pl.when(f == pl.num_programs(0) - 1)
    def _():
        for e in range(2):
            tokens = pl.ds(e * SEQ, SEQ)
            sketch = lax.dot_general(
                out_side[:, tokens], in_proj[:, tokens], LAST,
                preferred_element_type=jnp.float32, precision=lax.Precision.HIGHEST,
            )
            out[e * 32:(e + 1) * 32, :] = jnp.concatenate([sketch[:32], sketch[32:]], axis=1)


def sketch_part(table, grad, pieces, total, gate, proj_out, in_proj):
    count = len(pieces)
    rows, hidden = gate.shape
    in_specs = [grad_spec(rows, k) for k in range(count)]
    in_specs += [pl.BlockSpec((F_TILE, LANES), lambda f, table: (f, 0))] * count
    in_specs += [
        pl.BlockSpec((rows, F_TILE), lambda f, table: (0, f)),
        pl.BlockSpec((rows, F_TILE), lambda f, table: (0, f)),
        pl.BlockSpec((64, F_TILE), lambda f, table: (0, f)),
        pl.BlockSpec((64, rows), lambda f, table: (0, 0)),
    ]
    return pl.pallas_call(
        lambda *refs: sketch_kernel(count, *refs),
        out_shape=jax.ShapeDtypeStruct((64, LANES), jnp.float32),
        grid_spec=pltpu.PrefetchScalarGridSpec(
            num_scalar_prefetch=1, grid=(hidden // F_TILE,), in_specs=in_specs,
            out_specs=pl.BlockSpec((64, LANES), lambda f, table: (0, 0)),
            scratch_shapes=[pltpu.VMEM((64, rows), jnp.float32)],
        ),
        cost_estimate=pl.CostEstimate(
            flops=2 * rows * hidden * (LANES * count + 64),
            bytes_accessed=count * (rows + hidden) * LANES * 2 + 6 * rows * hidden,
            transcendentals=rows * hidden,
        ),
    )(table, *([grad] * count), *pieces, total, gate, proj_out, in_proj)


def split3(value):
    high = value.astype(jnp.bfloat16)
    rest = value - high.astype(jnp.float32)
    mid = rest.astype(jnp.bfloat16)
    low = (rest - mid.astype(jnp.float32)).astype(jnp.bfloat16)
    return high, mid, low


def send_kernel(place, mine, other, queries, order, payload, raw_scores, wide, left):
    wide[...] = (mine[...] + other[...]).astype(jnp.bfloat16).astype(jnp.float32)
    whole = wide[...]
    squares = jnp.sum(jnp.sum(whole * whole, axis=0, keepdims=True), axis=1, keepdims=True)
    parts = [v.astype(jnp.float32) for v in split3(jnp.broadcast_to(squares, (1, LANES)))]
    tails = [[parts[0], parts[1]], [parts[2], jnp.zeros((1, LANES), jnp.float32)]]
    first_col = place[0] * 4
    cols = [[wide[pl.ds(e * 32 + first_col + r, 1), :] for r in range(4)] for e in range(2)]
    for p in range(16):
        rows = []
        for e in range(2):
            rows += cols[e] + [wide[e * 32 + 2 * p:e * 32 + 2 * p + 2, :]] + tails[e]
        payload[p] = jnp.concatenate(rows, axis=0).astype(jnp.bfloat16)
    left[...] = jnp.zeros_like(left)
    for k in range(32):
        for e in range(2):
            left[e:e + 1, k * LANES:(k + 1) * LANES] = wide[pl.ds(e * 32 + order[k], 1), :]
    raw_scores[...] = lax.dot_general(
        left[...].astype(jnp.bfloat16), queries[...], LAST, preferred_element_type=jnp.float32
    )


def send_part(place, mine, other, queries, order):
    smem, vmem = pl.BlockSpec(memory_space=pltpu.SMEM), pl.BlockSpec(memory_space=pltpu.VMEM)
    return pl.pallas_call(
        send_kernel,
        out_shape=(
            jax.ShapeDtypeStruct((16, 16, LANES), jnp.bfloat16),
            jax.ShapeDtypeStruct((8, LANES), jnp.float32),
        ),
        in_specs=[smem, vmem, vmem, vmem, smem],
        out_specs=(vmem, vmem),
        scratch_shapes=[pltpu.VMEM((64, LANES), jnp.float32), pltpu.VMEM((8, 4096), jnp.float32)],
    )(place, mine, other, queries, order)


def gram_kernel(place, mine, other, raw_scores, gram, scores):
    t, dp = place[0], place[1]
    odd = (dp % 2) == 1
    blocks = [mine[...].astype(jnp.float32), other[...].astype(jnp.float32)]

    def stack(r):
        return jnp.concatenate([b[:, e * 8 + r, :] for b in blocks for e in range(2)], axis=0)

    trace = jnp.zeros((1, LANES), jnp.float32)
    for b in blocks:
        for r in (15, 14, 7, 6):
            trace = trace + jnp.sum(b[:, r, :], axis=0, keepdims=True)
    row_part = jnp.where(odd, stack(5), stack(4)).astype(jnp.bfloat16)
    for r in range(4):
        raw = lax.dot_general(
            row_part, stack(r).astype(jnp.bfloat16), (((0,), (0,)), ((), ())),
            preferred_element_type=jnp.float32,
        )
        rows = dp * LANES + lax.broadcasted_iota(jnp.int32, raw.shape, 0)
        cols = t * 512 + r * LANES + lax.broadcasted_iota(jnp.int32, raw.shape, 1)
        gram[:, r * LANES:(r + 1) * LANES] = raw * (4096.0 / trace) + jnp.where(rows == cols, 0.1, 0.0)
    scores[...] = raw_scores[:2, :] / jnp.sqrt(trace / 64.0)


def gram_part(place, mine, other, raw_scores):
    smem, vmem = pl.BlockSpec(memory_space=pltpu.SMEM), pl.BlockSpec(memory_space=pltpu.VMEM)
    return pl.pallas_call(
        gram_kernel,
        out_shape=(
            jax.ShapeDtypeStruct((LANES, 512), jnp.float32),
            jax.ShapeDtypeStruct((2, LANES), jnp.float32),
        ),
        in_specs=[smem, vmem, vmem, vmem],
        out_specs=(vmem, vmem),
    )(place, mine, other, raw_scores)


def body(acts, output_grad, gate_act, down_weight, proj_in, proj_out, query):
    dp, tensor = lax.axis_index("dp"), lax.axis_index("tensor")
    x, z, c = dp // 8, (dp // 2) % SIDE, dp % 2
    sign = 1 - 2 * c
    hidden = down_weight.shape[0]

    block = jnp.concatenate([down_weight, query], axis=0)
    held = {(0, 0): block}
    for b in range(1, SIDE):
        held[0, b] = z_step(held[0, b - 1])
    sends = []
    for a, b in ((1, 0), (2, 0), (1, 1), (3, 0), (2, 1), (1, 2), (3, 1), (2, 2), (1, 3), (3, 2), (2, 3), (3, 3)):
        source = held[a - 1, b]
        if len(sends) >= 2:
            source = after(source, sends[-2])
        held[a, b] = x_step(source)
        sends.append(held[a, b])

    in_proj = lax.dot_general(proj_in, acts, LAST, preferred_element_type=jnp.float32)
    proj_out = jnp.concatenate([proj_out.reshape(32, 2, hidden)[:, k] for k in range(2)], axis=0)

    groups = [[(a, b) for a in range(SIDE)] for b in range(SIDE)]
    groups[-1].remove((3, 3))
    groups.append([(3, 3)])
    total, query_parts, order = None, [], []
    for group in groups:
        own = [held[key] for key in group]
        pieces = own + [core_swap(piece) for piece in own]
        table = jnp.stack(
            [dp_id(x - sign * a, z - sign * b, c) for a, b in group]
            + [dp_id(x + sign * a, z + sign * b, 1 - c) for a, b in group]
        ).astype(jnp.int32)
        order.append(table)
        query_parts += [piece[hidden:] for piece in pieces]
        if group is groups[-1]:
            sketch = sketch_part(table, output_grad, pieces, total, gate_act, proj_out, in_proj)
        else:
            total = add_part(table, output_grad, pieces, total)
    queries = jnp.concatenate(query_parts, axis=1)
    order = jnp.concatenate(order)

    sketch = sketch + tensor_swap(sketch, 4)
    sketch = sketch + tensor_swap(sketch, 1)
    place = jnp.stack([tensor, dp]).astype(jnp.int32)
    payload, raw_scores = send_part(place, sketch, tensor_swap(sketch, 2), queries, order)
    mine = lax.all_to_all(payload, "dp", 0, 0, axis_index_groups=SAME_CORE)
    return gram_part(place, mine, core_swap(mine), raw_scores)


def solution(mesh):
    placed = (
        P("dp", None),
        P("dp", None),
        P("dp", "tensor"),
        P("tensor", "dp"),
        P(),
        P(None, "tensor"),
        P("tensor", "dp"),
    )
    return jax.shard_map(
        body,
        mesh=mesh,
        in_specs=placed,
        out_specs=(P("dp", "tensor"), P("dp", "tensor")),
        check_vma=False,
    )
```

time: 351 us -> 186 us (0.53)
  waiting for transfers between devices: 194 us -> 33 us
  blocking collectives: 117 us -> 14.7 us
  starting transfers between devices: 0.12 us -> 53.1 us
  Pallas kernels: 0 us -> 49.3 us
  local copies, waits for them, and re-layouts: 1.07 us -> 24.8 us
  matrix products: 24.2 us -> 4.23 us
  between operations: 15.2 us -> 1.01 us
    all_gather x2 -> x0, waiting for transfers between devices: 125 us -> none  [the longest x1 125 us: body(): lax.all_gather(down_weight, 'dp', axis=1, tiled=True)]
    psum x1 -> x0, blocking collectives: 75.4 us -> none  [body(): trace = lax.psum(jnp.sum(wide * wide), 'dp')]
    psum x1 -> x0, waiting for transfers between devices: 67.2 us -> none  [body(): out_proj = lax.psum(out_part, 'tensor')]
    ppermute x0 -> x35, starting transfers between devices: none -> 53.1 us  [the longest x32 48.6 us: dp_move(): lax.ppermute(value, 'dp', [(dp_id(*s), dp_id(*where(*s))) for s in PLACES])]
    pallas_call x0 -> x7, Pallas kernels: none -> 49.3 us  [the longest x4 36.6 us: add_part(): pl.pallas_call(lambda *refs: part_kernel(count, total is not None, *refs)...]
    all_gather x1 -> x0, blocking collectives: 41.3 us -> none  [body(): piece = lax.all_gather(sketches, 'dp', axis=0, tiled=True)]
    ppermute x0 -> x35, waiting for transfers between devices: none -> 33 us  [the longest x32 29.7 us: dp_move(): lax.ppermute(value, 'dp', [(dp_id(*s), dp_id(*where(*s))) for s in PLACES])]
    dot_general x5 -> x1, matrix products: 24.2 us -> 4.23 us  [body(): lax.dot_general(proj_in, acts, LAST, preferred_element_type=jnp.float32)]
  transfers between devices with their start and end apart: 3 -> 35, of which waited for: 2 -> 10; matrix products, arithmetic and copies ran while one was open for 2% -> 14% of each run, Pallas kernels for 0% -> 20%
where the time goes in v1:
time: 186 us; the launch traced here: 183 us
  starting transfers between devices  53.1 us (29%)
  Pallas kernels  49.3 us (27%)
  waiting for transfers between devices  33 us (18%)
  local copies, waits for them, and re-layouts  24.8 us (13%)
  blocking collectives  14.7 us (8%)
  matrix products  4.23 us (2%)
  other arithmetic  2.62 us (1%)
    ppermute x32, starting transfers between devices, dp_move(): lax.ppermute(value, 'dp', [(dp_id(*s), dp_id(*where(*s))) for s in PLACES])  48.6 us
    pallas_call x4, Pallas kernels, add_part(): pl.pallas_call(lambda *refs: part_kernel(count, total is not None, *refs)...  36.6 us
    ppermute x32, waiting for transfers between devices, dp_move(): lax.ppermute(value, 'dp', [(dp_id(*s), dp_id(*where(*s))) for s in PLACES])  29.7 us
    unnamed x72, local copies, waits for them, and re-layouts  19.4 us
    all_to_all x1, blocking collectives, body(): mine = lax.all_to_all(payload, 'dp', 0, 0, axis_index_groups=SAME_CORE)  14.7 us
    pallas_call x1, Pallas kernels, sketch_part(): pl.pallas_call(lambda *refs: sketch_kernel(count, *refs), out_shape=jax.S...  8.57 us
    ppermute x3, starting transfers between devices, tensor_swap(): return lax.ppermute(value, 'tensor', [(t, t ^ bit) for t in range(8)])  4.58 us
    dot_general x1, matrix products, body(): lax.dot_general(proj_in, acts, LAST, preferred_element_type=jnp.float32)  4.23 us
  transfers between devices with their start and end apart: 35, of which 10 were waited for; matrix products, arithmetic and copies ran while one was open for 14% of the time, Pallas kernels for 20%

profile of v1, /device:TPU:1, one launch (start us, length us, event | category | flops | bytes accessed | tf_op | source)
XLA Modules:
  0.0 182.9 jit_solution(3633161357685346277)
XLA Ops:
  0.6 1.1 constant_dynamic-update-slice_fusion.1
  1.8 0.8 constant_dynamic-update-slice_fusion.33
  2.5 3.4 %collective-permute-start.3 = (bf16[1920,128]{1,0:T(8,128)(2,1)S(1)}, bf16[1920,128]{1,0:T(8,128)(2,1)}, u32[]{:S(2)}, u32[]{:S(2)}) collective-permute-start(bf16[1920,128]{1,0:T(8,128)(2,1)S(1)} %get-tuple-element.29.refs_9_), channel_id=1, source_target_pairs={{0,64},{8,200},{16,80},{24,216},{32,96},{40,232},{48,112},{56,248}... | collective-permute-start | bytes 1474568 | tf_op jit(solution)/shard_map/ppermute | solution.py:24
  6.0 6.0 %collective-permute-start = (bf16[1920,128]{1,0:T(8,128)(2,1)S(1)}, bf16[1920,128]{1,0:T(8,128)(2,1)S(1)}, u32[]{:S(2)}, u32[]{:S(2)}) collective-permute-start(bf16[1920,128]{1,0:T(8,128)(2,1)S(1)} %get-tuple-element.29.refs_9_), channel_id=1, source_target_pairs={{0,16},{8,56},{16,32},{24,8},{32,48},{40,24},{48,0},{56,40},{64,80... | collective-permute-start | bytes 1474568 | tf_op jit(solution)/shard_map/ppermute | solution.py:24
  12.0 1.0 reshape.8
  13.4 9.6 %collective-permute-done.refs_9_ = bf16[1920,128]{1,0:T(8,128)(2,1)S(1)} collective-permute-done((bf16[1920,128]{1,0:T(8,128)(2,1)S(1)}, bf16[1920,128]{1,0:T(8,128)(2,1)S(1)}, u32[]{:S(2)}, u32[]{:S(2)}) %collective-permute-start) | collective-permute-done | bytes 491552 | tf_op jit(solution)/shard_map/ppermute | solution.py:24
  23.0 2.4 %collective-permute-start.9 = (bf16[1920,128]{1,0:T(8,128)(2,1)}, bf16[1920,128]{1,0:T(8,128)(2,1)}, u32[]{:S(2)}, u32[]{:S(2)}) collective-permute-start(bf16[1920,128]{1,0:T(8,128)(2,1)} %collective-permute-done.3.refs_10_), channel_id=1, source_target_pairs={{0,64},{8,200},{16,80},{24,216},{32,96},{40,232},{48,112},{56,248}... | collective-permute-start | bytes 1474568 | tf_op jit(solution)/shard_map/ppermute | solution.py:24
  25.4 0.7 pad_maximum_fusion.refs_7_
  26.7 4.2 %fusion.1.refs_8_ = f32[64,512]{1,0:T(8,128)} fusion(bf16[64,4096]{1,0:T(8,128)(2,1)S(1)} %copy-done, bf16[512,4096]{1,0:T(8,128)(2,1)} %param.7), kind=kOutput, calls=%fused_computation.40 | convolution fusion | flops 268435456 | bytes 4849664 | tf_op jit(solution)/shard_map/dot_general | solution.py:242
  31.0 4.0 %collective-permute-start.1 = (bf16[1920,128]{1,0:T(8,128)(2,1)S(1)}, bf16[1920,128]{1,0:T(8,128)(2,1)S(1)}, u32[]{:S(2)}, u32[]{:S(2)}) collective-permute-start(bf16[1920,128]{1,0:T(8,128)(2,1)S(1)} %collective-permute-done.refs_9_), channel_id=1, source_target_pairs={{0,16},{8,56},{16,32},{24,8},{32,48},{40,24},{48,0},{56,40},{64,80... | collective-permute-start | bytes 1474568 | tf_op jit(solution)/shard_map/ppermute | solution.py:24
  35.0 1.2 collective-permute-done.9.refs_11_
  36.1 1.1 collective-permute-start.10
  37.3 1.2 collective-permute-start.5
  39.0 0.7 stack.159.refs_0_
  40.9 0.7 concatenate.16.order
  41.6 0.7 stack.132.refs_0_
  42.3 0.8 constant_dynamic-update-slice_fusion.32
  43.1 0.8 constant_dynamic-update-slice_fusion.31
  44.3 3.0 %collective-permute-start.29 = (bf16[1920,128]{1,0:T(8,128)(2,1)}, bf16[1920,128]{1,0:T(8,128)(2,1)S(1)}, u32[]{:S(2)}, u32[]{:S(2)}) collective-permute-start(bf16[1920,128]{1,0:T(8,128)(2,1)} %collective-permute-done.9.refs_11_), channel_id=1, source_target_pairs={{0,8},{8,0},{16,24},{24,16},{32,40},{40,32},{48,56},{56,48},{64,72... | collective-permute-start | bytes 1474568 | tf_op jit(solution)/shard_map/ppermute | solution.py:24
  47.3 2.4 %collective-permute-done.5.refs_11_ = bf16[1920,128]{1,0:T(8,128)(2,1)} collective-permute-done((bf16[1920,128]{1,0:T(8,128)(2,1)S(1)}, bf16[1920,128]{1,0:T(8,128)(2,1)}, u32[]{:S(2)}, u32[]{:S(2)}) %collective-permute-start.5) | collective-permute-done | bytes 491552 | tf_op jit(solution)/shard_map/ppermute | solution.py:24
  49.7 4.2 %collective-permute-start.2 = (bf16[1920,128]{1,0:T(8,128)(2,1)}, bf16[1920,128]{1,0:T(8,128)(2,1)S(1)}, u32[]{:S(2)}, u32[]{:S(2)}) collective-permute-start(bf16[1920,128]{1,0:T(8,128)(2,1)} %copy-done.9), channel_id=1, source_target_pairs={{0,16},{8,56},{16,32},{24,8},{32,48},{40,24},{48,0},{56,40},{64,80... | collective-permute-start | bytes 1474568 | tf_op jit(solution)/shard_map/ppermute | solution.py:24
  53.9 1.9 %collective-permute-start.6 = (bf16[1920,128]{1,0:T(8,128)(2,1)}, bf16[1920,128]{1,0:T(8,128)(2,1)}, u32[]{:S(2)}, u32[]{:S(2)}) collective-permute-start(bf16[1920,128]{1,0:T(8,128)(2,1)} %collective-permute-done.5.refs_11_), channel_id=1, source_target_pairs={{0,64},{8,200},{16,80},{24,216},{32,96},{40,232},{48,112},{56,248}... | collective-permute-start | bytes 1474568 | tf_op jit(solution)/shard_map/ppermute | solution.py:24
  55.8 0.8 constant_dynamic-update-slice_fusion.30
  56.6 0.6 collective-permute-start.11
  57.7 0.8 constant_dynamic-update-slice_fusion.29
  58.9 8.6 %collective-permute-done.11.refs_10_ = bf16[1920,128]{1,0:T(8,128)(2,1)} collective-permute-done((bf16[1920,128]{1,0:T(8,128)(2,1)}, bf16[1920,128]{1,0:T(8,128)(2,1)}, u32[]{:S(2)}, u32[]{:S(2)}) %collective-permute-start.11) | collective-permute-done | bytes 491552 | tf_op jit(solution)/shard_map/ppermute | solution.py:24
  67.5 4.9 %collective-permute-start.24 = (bf16[1920,128]{1,0:T(8,128)(2,1)S(1)}, bf16[1920,128]{1,0:T(8,128)(2,1)}, u32[]{:S(2)}, u32[]{:S(2)}) collective-permute-start(bf16[1920,128]{1,0:T(8,128)(2,1)S(1)} %collective-permute-done.4.refs_10_), channel_id=1, source_target_pairs={{0,8},{8,0},{16,24},{24,16},{32,40},{40,32},{48,56},{56,48},{64,72... | collective-permute-start | bytes 1474568 | tf_op jit(solution)/shard_map/ppermute | solution.py:24
  72.7 0.8 constant_dynamic-update-slice_fusion.23
  73.5 0.8 constant_dynamic-update-slice_fusion.22
  75.1 8.7 %shard_map.86.refs_17_ = f32[512,1792]{1,0:T(8,128)} custom-call(s32[8]{0:T(128)} %stack.159.refs_0_, bf16[512,4096]{1,0:T(8,128)(2,1)} %refs_2_.9, bf16[512,4096]{1,0:T(8,128)(2,1)} %refs_2_.9, bf16[512,4096]{1,0:T(8,128)(2,1)} %refs_2_.9, bf16[512,4096]{1,0:T(8,128)(2,1)} %refs_2_.9, bf16[512,4096]{1,0:T(8,128)(2,1)} %refs_2_.9, ...), custom_call_target="tpu_custom_call" | custom-call | flops 1879048192 | bytes 12058624 | tf_op jit(solution)/shard_map/pallas_call | solution.py:72
  84.3 0.8 constant_dynamic-update-slice_fusion.20
  85.3 0.8 constant_dynamic-update-slice_fusion.19
  86.6 2.9 %collective-permute-start.13 = (bf16[1920,128]{1,0:T(8,128)(2,1)}, bf16[1920,128]{1,0:T(8,128)(2,1)}, u32[]{:S(2)}, u32[]{:S(2)}) collective-permute-start(bf16[1920,128]{1,0:T(8,128)(2,1)} %collective-permute-done.12.refs_11_), channel_id=1, source_target_pairs={{0,64},{8,200},{16,80},{24,216},{32,96},{40,232},{48,112},{56,248}... | collective-permute-start | bytes 1474568 | tf_op jit(solution)/shard_map/ppermute | solution.py:24
  89.5 1.6 collective-permute-start.8
  91.1 0.8 constant_dynamic-update-slice_fusion.18
  91.9 0.8 constant_dynamic-update-slice_fusion.17
  92.7 0.8 constant_dynamic-update-slice_fusion.16
  93.5 0.8 constant_dynamic-update-slice_fusion.15
  94.2 9.5 %shard_map.87.refs_17_ = f32[512,1792]{1,0:T(8,128)} custom-call(s32[8]{0:T(128)} %stack.150.refs_0_, bf16[512,4096]{1,0:T(8,128)(2,1)} %refs_2_.9, bf16[512,4096]{1,0:T(8,128)(2,1)} %refs_2_.9, bf16[512,4096]{1,0:T(8,128)(2,1)} %refs_2_.9, bf16[512,4096]{1,0:T(8,128)(2,1)} %refs_2_.9, bf16[512,4096]{1,0:T(8,128)(2,1)} %refs_2_.9, ...), custom_call_target="tpu_custom_call" | custom-call | flops 1879048192 | bytes 12058624 | tf_op jit(solution)/shard_map/pallas_call | solution.py:72
  103.9 0.8 constant_dynamic-update-slice_fusion.14
  105.2 0.8 constant_dynamic-update-slice_fusion.13
  106.4 0.8 constant_dynamic-update-slice_fusion.12
  107.6 6.6 %collective-permute-done.14.refs_3_ = bf16[1920,128]{1,0:T(8,128)(2,1)} collective-permute-done((bf16[1920,128]{1,0:T(8,128)(2,1)S(1)}, bf16[1920,128]{1,0:T(8,128)(2,1)}, u32[]{:S(2)}, u32[]{:S(2)}) %collective-permute-start.14) | collective-permute-done | bytes 491552 | tf_op jit(solution)/shard_map/ppermute | solution.py:24
  114.2 2.5 %collective-permute-start.15 = (bf16[1920,128]{1,0:T(8,128)(2,1)}, bf16[1920,128]{1,0:T(8,128)(2,1)}, u32[]{:S(2)}, u32[]{:S(2)}) collective-permute-start(bf16[1920,128]{1,0:T(8,128)(2,1)} %collective-permute-done.14.refs_3_), channel_id=1, source_target_pairs={{0,8},{8,0},{16,24},{24,16},{32,40},{40,32},{48,56},{56,48},{64,72... | collective-permute-start | bytes 1474568 | tf_op jit(solution)/shard_map/ppermute | solution.py:24
  116.7 9.4 %shard_map.88.refs_13_ = f32[512,1792]{1,0:T(8,128)} custom-call(s32[8]{0:T(128)} %stack.141.refs_0_, bf16[512,4096]{1,0:T(8,128)(2,1)} %refs_2_.9, bf16[512,4096]{1,0:T(8,128)(2,1)} %refs_2_.9, bf16[512,4096]{1,0:T(8,128)(2,1)} %refs_2_.9, bf16[512,4096]{1,0:T(8,128)(2,1)} %refs_2_.9, bf16[512,4096]{1,0:T(8,128)(2,1)} %refs_2_.9, ...), custom_call_target="tpu_custom_call" | custom-call | flops 1879048192 | bytes 12058624 | tf_op jit(solution)/shard_map/pallas_call | solution.py:72
  126.3 0.8 copy-done.5
  127.0 8.9 %shard_map.89.refs_5_ = f32[512,1792]{1,0:T(8,128)} custom-call(s32[6]{0:T(128)} %stack.132.refs_0_, bf16[512,4096]{1,0:T(8,128)(2,1)} %refs_2_.9, bf16[512,4096]{1,0:T(8,128)(2,1)} %refs_2_.9, bf16[512,4096]{1,0:T(8,128)(2,1)} %refs_2_.9, bf16[512,4096]{1,0:T(8,128)(2,1)} %refs_2_.9, bf16[512,4096]{1,0:T(8,128)(2,1)} %refs_2_.9, bf16[512,4096]{1,0:T(8,128)(2,1)} %refs_2_.9, ...), custom_call_target="tpu_custom_call" | custom-call | flops 1409286144 | bytes 10878976 | tf_op jit(solution)/shard_map/pallas_call | solution.py:72
  136.0 0.8 constant_dynamic-update-slice_fusion.6
  136.8 0.8 constant_dynamic-update-slice_fusion.5
  137.5 8.6 %shard_map.90 = f32[64,128]{1,0:T(8,128)} custom-call(s32[2]{0:T(128)} %pad_add_fusion.1.refs_0_, bf16[512,4096]{1,0:T(8,128)(2,1)} %refs_2_.9, bf16[512,4096]{1,0:T(8,128)(2,1)} %refs_2_.9, bf16[1920,128]{1,0:T(8,128)(2,1)} %collective-permute-done.14.refs_3_, bf16[1920,128]{1,0:T(8,128)(2,1)} %collective-permute-done.15.refs_4_, ...), custom_call_target="tpu_custom_call" | custom-call | flops 587202560 | bytes 6684672 | tf_op jit(solution)/shard_map/pallas_call | solution.py:127
  146.4 0.8 constant_dynamic-update-slice_fusion.4
  147.2 1.9 %collective-permute-done.31 = f32[64,128]{1,0:T(8,128)S(1)} collective-permute-done((f32[64,128]{1,0:T(8,128)}, f32[64,128]{1,0:T(8,128)S(1)}, u32[]{:S(2)}, u32[]{:S(2)}) %collective-permute-start.31) | collective-permute-done | bytes 32800 | tf_op jit(solution)/shard_map/ppermute | solution.py:40
  149.1 0.8 add.418
  149.8 1.3 collective-permute-start.32
  151.1 0.8 constant_dynamic-update-slice_fusion.3
  151.9 0.7 collective-permute-done.32
  152.6 3.0 %collective-permute-start.33 = (f32[64,128]{1,0:T(8,128)S(1)}, f32[64,128]{1,0:T(8,128)S(1)}, u32[]{:S(2)}, u32[]{:S(2)}) collective-permute-start(f32[64,128]{1,0:T(8,128)S(1)} %add.419.mine), channel_id=1, source_target_pairs={{0,2},{1,3},{2,0},{3,1},{4,6},{5,7},{6,4},{7,5},{8,10},{9,11},{10,... | collective-permute-start | bytes 98312 | tf_op jit(solution)/shard_map/ppermute | solution.py:40
  155.6 0.8 constant_dynamic-update-slice_fusion.2.queries
  156.4 0.7 collective-permute-done.33.other
  158.0 2.3 %shard_map.91 = (bf16[16,16,128]{2,1,0:T(8,128)(2,1)}, f32[8,128]{1,0:T(8,128)}) custom-call(s32[2]{0:T(128)} %pad_add_fusion.place, f32[64,128]{1,0:T(8,128)} %copy-done.17, f32[64,128]{1,0:T(8,128)} %copy-done.19, bf16[128,4096]{1,0:T(8,128)(2,1)} %copy-done.2, s32[32]{0:T(128)} %concatenate.16.order), custom_call_target="tpu_custom_call" | custom-call | tf_op jit(solution)/shard_map/pallas_call | solution.py:175
  160.3 14.7 %all_to_all.5.mine = bf16[16,16,128]{2,1,0:T(8,128)(2,1)S(1)} all-to-all(bf16[16,16,128]{2,1,0:T(8,128)(2,1)} %get-tuple-element.24), channel_id=1, replica_groups={{0,16,32,48,64,80,96,112,128,144,160,176,192,208,224,240},{8,24,40,56,7..., dimensions={0} | all-to-all | bytes 131072 | tf_op jit(solution)/shard_map/all_to_all | solution.py:269
  175.0 4.5 %collective-permute-start.34 = (bf16[16,16,128]{2,1,0:T(8,128)(2,1)S(1)}, bf16[16,16,128]{2,1,0:T(8,128)(2,1)S(1)}, u32[]{:S(2)}, u32[]{:S(2)}) collective-permute-start(bf16[16,16,128]{2,1,0:T(8,128)(2,1)S(1)} %all_to_all.5.mine), channel_id=1, source_target_pairs={{0,8},{8,0},{16,24},{24,16},{32,40},{40,32},{48,56},{56,48},{64,72... | collective-permute-start | bytes 196616 | tf_op jit(solution)/shard_map/ppermute | solution.py:24
  179.5 0.9 collective-permute-done.34.other
  181.0 1.8 %shard_map.92 = (f32[128,512]{1,0:T(8,128)}, f32[2,128]{1,0:T(2,128)}) custom-call(s32[2]{0:T(128)} %pad_add_fusion.place, bf16[16,16,128]{2,1,0:T(8,128)(2,1)} %copy-done.16, bf16[16,16,128]{2,1,0:T(8,128)(2,1)} %copy-done.18, f32[8,128]{1,0:T(8,128)} %get-tuple-element.25.raw_scores), custom_call_target="tpu_custom_call" | custom-call | tf_op jit(solution)/shard_map/pallas_call | solution.py:213
  (101 shorter events, 9.9 us)
Async XLA Ops:
  0.6 26.1 %copy-start = (bf16[64,4096]{1,0:T(8,128)(2,1)S(1)}, bf16[64,4096]{1,0:T(8,128)(2,1)}, u32[]{:S(2)}) copy-start(bf16[64,4096]{1,0:T(8,128)(2,1)} %param.11) | copy-start | bytes 1572868
  2.5 56.0 %copy-start.1 = (bf16[1920,128]{1,0:T(8,128)(2,1)}, bf16[1920,128]{1,0:T(8,128)(2,1)S(1)}, u32[]{:S(2)}) copy-start(bf16[1920,128]{1,0:T(8,128)(2,1)S(1)} %get-tuple-element.29.refs_9_) | copy-start | bytes 1474564
  2.5 10.8 %collective-permute-start.3 = (bf16[1920,128]{1,0:T(8,128)(2,1)S(1)}, bf16[1920,128]{1,0:T(8,128)(2,1)}, u32[]{:S(2)}, u32[]{:S(2)}) collective-permute-start(bf16[1920,128]{1,0:T(8,128)(2,1)S(1)} %get-tuple-element.29.refs_9_), channel_id=1, source_target_pairs={{0,64},{8,200},{16,80},{24,216},{32,96},{40,232},{48,112},{56,248}... | collective-permute-start | bytes 1474568 | tf_op jit(solution)/shard_map/ppermute | solution.py:24
  5.9 50.6 %collective-permute-start.27 = (bf16[1920,128]{1,0:T(8,128)(2,1)S(1)}, bf16[1920,128]{1,0:T(8,128)(2,1)}, u32[]{:S(2)}, u32[]{:S(2)}) collective-permute-start(bf16[1920,128]{1,0:T(8,128)(2,1)S(1)} %get-tuple-element.29.refs_9_), channel_id=1, source_target_pairs={{0,8},{8,0},{16,24},{24,16},{32,40},{40,32},{48,56},{56,48},{64,72... | collective-permute-start | bytes 1474568 | tf_op jit(solution)/shard_map/ppermute | solution.py:24
  6.0 17.0 %collective-permute-start = (bf16[1920,128]{1,0:T(8,128)(2,1)S(1)}, bf16[1920,128]{1,0:T(8,128)(2,1)S(1)}, u32[]{:S(2)}, u32[]{:S(2)}) collective-permute-start(bf16[1920,128]{1,0:T(8,128)(2,1)S(1)} %get-tuple-element.29.refs_9_), channel_id=1, source_target_pairs={{0,16},{8,56},{16,32},{24,8},{32,48},{40,24},{48,0},{56,40},{64,80... | collective-permute-start | bytes 1474568 | tf_op jit(solution)/shard_map/ppermute | solution.py:24
  23.0 60.8 %copy-start.7 = (bf16[1920,128]{1,0:T(8,128)(2,1)}, bf16[1920,128]{1,0:T(8,128)(2,1)S(1)}, u32[]{:S(2)}) copy-start(bf16[1920,128]{1,0:T(8,128)(2,1)S(1)} %collective-permute-done.refs_9_) | copy-start | bytes 1474564
  23.0 14.3 %collective-permute-start.4 = (bf16[1920,128]{1,0:T(8,128)(2,1)S(1)}, bf16[1920,128]{1,0:T(8,128)(2,1)S(1)}, u32[]{:S(2)}, u32[]{:S(2)}) collective-permute-start(bf16[1920,128]{1,0:T(8,128)(2,1)S(1)} %collective-permute-done.refs_9_), channel_id=1, source_target_pairs={{0,64},{8,200},{16,80},{24,216},{32,96},{40,232},{48,112},{56,248}... | collective-permute-start | bytes 1474568 | tf_op jit(solution)/shard_map/ppermute | solution.py:24
  23.0 13.1 %collective-permute-start.9 = (bf16[1920,128]{1,0:T(8,128)(2,1)}, bf16[1920,128]{1,0:T(8,128)(2,1)}, u32[]{:S(2)}, u32[]{:S(2)}) collective-permute-start(bf16[1920,128]{1,0:T(8,128)(2,1)} %collective-permute-done.3.refs_10_), channel_id=1, source_target_pairs={{0,64},{8,200},{16,80},{24,216},{32,96},{40,232},{48,112},{56,248}... | collective-permute-start | bytes 1474568 | tf_op jit(solution)/shard_map/ppermute | solution.py:24
  31.0 13.3 %collective-permute-start.1 = (bf16[1920,128]{1,0:T(8,128)(2,1)S(1)}, bf16[1920,128]{1,0:T(8,128)(2,1)S(1)}, u32[]{:S(2)}, u32[]{:S(2)}) collective-permute-start(bf16[1920,128]{1,0:T(8,128)(2,1)S(1)} %collective-permute-done.refs_9_), channel_id=1, source_target_pairs={{0,16},{8,56},{16,32},{24,8},{32,48},{40,24},{48,0},{56,40},{64,80... | collective-permute-start | bytes 1474568 | tf_op jit(solution)/shard_map/ppermute | solution.py:24
  36.1 17.8 %collective-permute-start.10 = (bf16[1920,128]{1,0:T(8,128)(2,1)}, bf16[1920,128]{1,0:T(8,128)(2,1)}, u32[]{:S(2)}, u32[]{:S(2)}) collective-permute-start(bf16[1920,128]{1,0:T(8,128)(2,1)} %collective-permute-done.9.refs_11_), channel_id=1, source_target_pairs={{0,64},{8,200},{16,80},{24,216},{32,96},{40,232},{48,112},{56,248}... | collective-permute-start | bytes 1474568 | tf_op jit(solution)/shard_map/ppermute | solution.py:24
  37.3 46.6 %copy-start.8 = (bf16[1920,128]{1,0:T(8,128)(2,1)}, bf16[1920,128]{1,0:T(8,128)(2,1)S(1)}, u32[]{:S(2)}) copy-start(bf16[1920,128]{1,0:T(8,128)(2,1)S(1)} %collective-permute-done.4.refs_10_) | copy-start | bytes 1474564
  37.3 12.4 %collective-permute-start.5 = (bf16[1920,128]{1,0:T(8,128)(2,1)S(1)}, bf16[1920,128]{1,0:T(8,128)(2,1)}, u32[]{:S(2)}, u32[]{:S(2)}) collective-permute-start(bf16[1920,128]{1,0:T(8,128)(2,1)S(1)} %collective-permute-done.4.refs_10_), channel_id=1, source_target_pairs={{0,64},{8,200},{16,80},{24,216},{32,96},{40,232},{48,112},{56,248}... | collective-permute-start | bytes 1474568 | tf_op jit(solution)/shard_map/ppermute | solution.py:24
  42.3 14.9 %collective-permute-start.28 = (bf16[1920,128]{1,0:T(8,128)(2,1)}, bf16[1920,128]{1,0:T(8,128)(2,1)S(1)}, u32[]{:S(2)}, u32[]{:S(2)}) collective-permute-start(bf16[1920,128]{1,0:T(8,128)(2,1)} %collective-permute-done.3.refs_10_), channel_id=1, source_target_pairs={{0,8},{8,0},{16,24},{24,16},{32,40},{40,32},{48,56},{56,48},{64,72... | collective-permute-start | bytes 1474568 | tf_op jit(solution)/shard_map/ppermute | solution.py:24
  44.3 3.0 %copy-start.9 = (bf16[1920,128]{1,0:T(8,128)(2,1)}, bf16[1920,128]{1,0:T(8,128)(2,1)S(1)}, u32[]{:S(2)}) copy-start(bf16[1920,128]{1,0:T(8,128)(2,1)S(1)} %collective-permute-done.1.refs_9_) | copy-start | bytes 1474564
  44.3 14.2 %collective-permute-start.29 = (bf16[1920,128]{1,0:T(8,128)(2,1)}, bf16[1920,128]{1,0:T(8,128)(2,1)S(1)}, u32[]{:S(2)}, u32[]{:S(2)}) collective-permute-start(bf16[1920,128]{1,0:T(8,128)(2,1)} %collective-permute-done.9.refs_11_), channel_id=1, source_target_pairs={{0,8},{8,0},{16,24},{24,16},{32,40},{40,32},{48,56},{56,48},{64,72... | collective-permute-start | bytes 1474568 | tf_op jit(solution)/shard_map/ppermute | solution.py:24
  49.7 22.7 %collective-permute-start.2 = (bf16[1920,128]{1,0:T(8,128)(2,1)}, bf16[1920,128]{1,0:T(8,128)(2,1)S(1)}, u32[]{:S(2)}, u32[]{:S(2)}) collective-permute-start(bf16[1920,128]{1,0:T(8,128)(2,1)} %copy-done.9), channel_id=1, source_target_pairs={{0,16},{8,56},{16,32},{24,8},{32,48},{40,24},{48,0},{56,40},{64,80... | collective-permute-start | bytes 1474568 | tf_op jit(solution)/shard_map/ppermute | solution.py:24
  53.9 18.6 %collective-permute-start.6 = (bf16[1920,128]{1,0:T(8,128)(2,1)}, bf16[1920,128]{1,0:T(8,128)(2,1)}, u32[]{:S(2)}, u32[]{:S(2)}) collective-permute-start(bf16[1920,128]{1,0:T(8,128)(2,1)} %collective-permute-done.5.refs_11_), channel_id=1, source_target_pairs={{0,64},{8,200},{16,80},{24,216},{32,96},{40,232},{48,112},{56,248}... | collective-permute-start | bytes 1474568 | tf_op jit(solution)/shard_map/ppermute | solution.py:24
  56.6 10.9 %collective-permute-start.11 = (bf16[1920,128]{1,0:T(8,128)(2,1)}, bf16[1920,128]{1,0:T(8,128)(2,1)}, u32[]{:S(2)}, u32[]{:S(2)}) collective-permute-start(bf16[1920,128]{1,0:T(8,128)(2,1)} %copy-done.9), channel_id=1, source_target_pairs={{0,64},{8,200},{16,80},{24,216},{32,96},{40,232},{48,112},{56,248}... | collective-permute-start | bytes 1474568 | tf_op jit(solution)/shard_map/ppermute | solution.py:24
  57.2 1.3 copy-start.11
  57.2 15.3 %collective-permute-start.30 = (bf16[1920,128]{1,0:T(8,128)(2,1)}, bf16[1920,128]{1,0:T(8,128)(2,1)S(1)}, u32[]{:S(2)}, u32[]{:S(2)}) collective-permute-start(bf16[1920,128]{1,0:T(8,128)(2,1)} %collective-permute-done.10.refs_12_), channel_id=1, source_target_pairs={{0,8},{8,0},{16,24},{24,16},{32,40},{40,32},{48,56},{56,48},{64,72... | collective-permute-start | bytes 1474568 | tf_op jit(solution)/shard_map/ppermute | solution.py:24
  58.5 15.7 %copy-start.12 = (bf16[1920,128]{1,0:T(8,128)(2,1)}, bf16[1920,128]{1,0:T(8,128)(2,1)S(1)}, u32[]{:S(2)}) copy-start(bf16[1920,128]{1,0:T(8,128)(2,1)S(1)} %collective-permute-done.29.refs_15_) | copy-start | bytes 1474564
  58.6 15.7 %collective-permute-start.23 = (bf16[1920,128]{1,0:T(8,128)(2,1)S(1)}, bf16[1920,128]{1,0:T(8,128)(2,1)S(1)}, u32[]{:S(2)}, u32[]{:S(2)}) collective-permute-start(bf16[1920,128]{1,0:T(8,128)(2,1)S(1)} %collective-permute-done.refs_9_), channel_id=1, source_target_pairs={{0,8},{8,0},{16,24},{24,16},{32,40},{40,32},{48,56},{56,48},{64,72... | collective-permute-start | bytes 1474568 | tf_op jit(solution)/shard_map/ppermute | solution.py:24
  67.5 16.4 %collective-permute-start.24 = (bf16[1920,128]{1,0:T(8,128)(2,1)S(1)}, bf16[1920,128]{1,0:T(8,128)(2,1)}, u32[]{:S(2)}, u32[]{:S(2)}) collective-permute-start(bf16[1920,128]{1,0:T(8,128)(2,1)S(1)} %collective-permute-done.4.refs_10_), channel_id=1, source_target_pairs={{0,8},{8,0},{16,24},{24,16},{32,40},{40,32},{48,56},{56,48},{64,72... | collective-permute-start | bytes 1474568 | tf_op jit(solution)/shard_map/ppermute | solution.py:24
  72.4 35.2 %copy-start.3 = (bf16[1920,128]{1,0:T(8,128)(2,1)}, bf16[1920,128]{1,0:T(8,128)(2,1)S(1)}, u32[]{:S(2)}) copy-start(bf16[1920,128]{1,0:T(8,128)(2,1)S(1)} %collective-permute-done.2.refs_7_) | copy-start | bytes 1474564
  72.4 12.7 %collective-permute-start.25 = (bf16[1920,128]{1,0:T(8,128)(2,1)}, bf16[1920,128]{1,0:T(8,128)(2,1)}, u32[]{:S(2)}, u32[]{:S(2)}) collective-permute-start(bf16[1920,128]{1,0:T(8,128)(2,1)} %collective-permute-done.5.refs_11_), channel_id=1, source_target_pairs={{0,8},{8,0},{16,24},{24,16},{32,40},{40,32},{48,56},{56,48},{64,72... | collective-permute-start | bytes 1474568 | tf_op jit(solution)/shard_map/ppermute | solution.py:24
  72.5 13.6 %collective-permute-start.12 = (bf16[1920,128]{1,0:T(8,128)(2,1)}, bf16[1920,128]{1,0:T(8,128)(2,1)}, u32[]{:S(2)}, u32[]{:S(2)}) collective-permute-start(bf16[1920,128]{1,0:T(8,128)(2,1)} %collective-permute-done.11.refs_10_), channel_id=1, source_target_pairs={{0,64},{8,200},{16,80},{24,216},{32,96},{40,232},{48,112},{56,248}... | collective-permute-start | bytes 1474568 | tf_op jit(solution)/shard_map/ppermute | solution.py:24
  72.5 2.2 %copy-start.13 = (bf16[1920,128]{1,0:T(8,128)(2,1)}, bf16[1920,128]{1,0:T(8,128)(2,1)S(1)}, u32[]{:S(2)}) copy-start(bf16[1920,128]{1,0:T(8,128)(2,1)S(1)} %collective-permute-done.30.refs_16_) | copy-start | bytes 1474564
  72.5 14.1 %collective-permute-start.7 = (bf16[1920,128]{1,0:T(8,128)(2,1)S(1)}, bf16[1920,128]{1,0:T(8,128)(2,1)S(1)}, u32[]{:S(2)}, u32[]{:S(2)}) collective-permute-start(bf16[1920,128]{1,0:T(8,128)(2,1)S(1)} %collective-permute-done.2.refs_7_), channel_id=1, source_target_pairs={{0,64},{8,200},{16,80},{24,216},{32,96},{40,232},{48,112},{56,248}... | collective-permute-start | bytes 1474568 | tf_op jit(solution)/shard_map/ppermute | solution.py:24
  74.2 0.8 copy-start.10
  74.3 15.3 %collective-permute-start.26 = (bf16[1920,128]{1,0:T(8,128)(2,1)}, bf16[1920,128]{1,0:T(8,128)(2,1)}, u32[]{:S(2)}, u32[]{:S(2)}) collective-permute-start(bf16[1920,128]{1,0:T(8,128)(2,1)} %collective-permute-done.6.refs_12_), channel_id=1, source_target_pairs={{0,8},{8,0},{16,24},{24,16},{32,40},{40,32},{48,56},{56,48},{64,72... | collective-permute-start | bytes 1474568 | tf_op jit(solution)/shard_map/ppermute | solution.py:24
  83.8 20.8 %collective-permute-start.19 = (bf16[1920,128]{1,0:T(8,128)(2,1)}, bf16[1920,128]{1,0:T(8,128)(2,1)}, u32[]{:S(2)}, u32[]{:S(2)}) collective-permute-start(bf16[1920,128]{1,0:T(8,128)(2,1)} %copy-done.9), channel_id=1, source_target_pairs={{0,8},{8,0},{16,24},{24,16},{32,40},{40,32},{48,56},{56,48},{64,72... | collective-permute-start | bytes 1474568 | tf_op jit(solution)/shard_map/ppermute | solution.py:24
  85.1 41.1 %collective-permute-start.16 = (bf16[1920,128]{1,0:T(8,128)(2,1)S(1)}, bf16[1920,128]{1,0:T(8,128)(2,1)S(1)}, u32[]{:S(2)}, u32[]{:S(2)}) collective-permute-start(bf16[1920,128]{1,0:T(8,128)(2,1)S(1)} %collective-permute-done.2.refs_7_), channel_id=1, source_target_pairs={{0,8},{8,0},{16,24},{24,16},{32,40},{40,32},{48,56},{56,48},{64,72... | collective-permute-start | bytes 1474568 | tf_op jit(solution)/shard_map/ppermute | solution.py:24
  86.1 20.0 %collective-permute-start.20 = (bf16[1920,128]{1,0:T(8,128)(2,1)}, bf16[1920,128]{1,0:T(8,128)(2,1)}, u32[]{:S(2)}, u32[]{:S(2)}) collective-permute-start(bf16[1920,128]{1,0:T(8,128)(2,1)} %collective-permute-done.11.refs_10_), channel_id=1, source_target_pairs={{0,8},{8,0},{16,24},{24,16},{32,40},{40,32},{48,56},{56,48},{64,72... | collective-permute-start | bytes 1474568 | tf_op jit(solution)/shard_map/ppermute | solution.py:24
  86.6 39.6 %copy-start.4 = (bf16[1920,128]{1,0:T(8,128)(2,1)}, bf16[1920,128]{1,0:T(8,128)(2,1)S(1)}, u32[]{:S(2)}) copy-start(bf16[1920,128]{1,0:T(8,128)(2,1)S(1)} %collective-permute-done.7.refs_8_) | copy-start | bytes 1474564
  86.6 17.1 %collective-permute-start.13 = (bf16[1920,128]{1,0:T(8,128)(2,1)}, bf16[1920,128]{1,0:T(8,128)(2,1)}, u32[]{:S(2)}, u32[]{:S(2)}) collective-permute-start(bf16[1920,128]{1,0:T(8,128)(2,1)} %collective-permute-done.12.refs_11_), channel_id=1, source_target_pairs={{0,64},{8,200},{16,80},{24,216},{32,96},{40,232},{48,112},{56,248}... | collective-permute-start | bytes 1474568 | tf_op jit(solution)/shard_map/ppermute | solution.py:24
  89.5 16.4 %collective-permute-start.8 = (bf16[1920,128]{1,0:T(8,128)(2,1)S(1)}, bf16[1920,128]{1,0:T(8,128)(2,1)S(1)}, u32[]{:S(2)}, u32[]{:S(2)}) collective-permute-start(bf16[1920,128]{1,0:T(8,128)(2,1)S(1)} %collective-permute-done.7.refs_8_), channel_id=1, source_target_pairs={{0,64},{8,200},{16,80},{24,216},{32,96},{40,232},{48,112},{56,248}... | collective-permute-start | bytes 1474568 | tf_op jit(solution)/shard_map/ppermute | solution.py:24
  103.7 3.4 %collective-permute-start.21 = (bf16[1920,128]{1,0:T(8,128)(2,1)}, bf16[1920,128]{1,0:T(8,128)(2,1)S(1)}, u32[]{:S(2)}, u32[]{:S(2)}) collective-permute-start(bf16[1920,128]{1,0:T(8,128)(2,1)} %collective-permute-done.12.refs_11_), channel_id=1, source_target_pairs={{0,8},{8,0},{16,24},{24,16},{32,40},{40,32},{48,56},{56,48},{64,72... | collective-permute-start | bytes 1474568 | tf_op jit(solution)/shard_map/ppermute | solution.py:24
  104.6 2.9 %collective-permute-start.22 = (bf16[1920,128]{1,0:T(8,128)(2,1)}, bf16[1920,128]{1,0:T(8,128)(2,1)S(1)}, u32[]{:S(2)}, u32[]{:S(2)}) collective-permute-start(bf16[1920,128]{1,0:T(8,128)(2,1)} %collective-permute-done.13.refs_12_), channel_id=1, source_target_pairs={{0,8},{8,0},{16,24},{24,16},{32,40},{40,32},{48,56},{56,48},{64,72... | collective-permute-start | bytes 1474568 | tf_op jit(solution)/shard_map/ppermute | solution.py:24
  106.0 20.2 %copy-start.6 = (bf16[1920,128]{1,0:T(8,128)(2,1)}, bf16[1920,128]{1,0:T(8,128)(2,1)S(1)}, u32[]{:S(2)}) copy-start(bf16[1920,128]{1,0:T(8,128)(2,1)S(1)} %collective-permute-done.8.refs_9_) | copy-start | bytes 1474564
  106.0 20.3 %collective-permute-start.17 = (bf16[1920,128]{1,0:T(8,128)(2,1)S(1)}, bf16[1920,128]{1,0:T(8,128)(2,1)}, u32[]{:S(2)}, u32[]{:S(2)}) collective-permute-start(bf16[1920,128]{1,0:T(8,128)(2,1)S(1)} %collective-permute-done.7.refs_8_), channel_id=1, source_target_pairs={{0,8},{8,0},{16,24},{24,16},{32,40},{40,32},{48,56},{56,48},{64,72... | collective-permute-start | bytes 1474568 | tf_op jit(solution)/shard_map/ppermute | solution.py:24
  106.1 8.1 %collective-permute-start.14 = (bf16[1920,128]{1,0:T(8,128)(2,1)S(1)}, bf16[1920,128]{1,0:T(8,128)(2,1)}, u32[]{:S(2)}, u32[]{:S(2)}) collective-permute-start(bf16[1920,128]{1,0:T(8,128)(2,1)S(1)} %collective-permute-done.8.refs_9_), channel_id=1, source_target_pairs={{0,64},{8,200},{16,80},{24,216},{32,96},{40,232},{48,112},{56,248}... | collective-permute-start | bytes 1474568 | tf_op jit(solution)/shard_map/ppermute | solution.py:24
  107.2 7.1 %copy-start.14 = (bf16[1920,128]{1,0:T(8,128)(2,1)}, bf16[1920,128]{1,0:T(8,128)(2,1)S(1)}, u32[]{:S(2)}) copy-start(bf16[1920,128]{1,0:T(8,128)(2,1)S(1)} %collective-permute-done.21.refs_15_) | copy-start | bytes 1474564
  107.2 19.1 %collective-permute-start.18 = (bf16[1920,128]{1,0:T(8,128)(2,1)S(1)}, bf16[1920,128]{1,0:T(8,128)(2,1)}, u32[]{:S(2)}, u32[]{:S(2)}) collective-permute-start(bf16[1920,128]{1,0:T(8,128)(2,1)S(1)} %collective-permute-done.8.refs_9_), channel_id=1, source_target_pairs={{0,8},{8,0},{16,24},{24,16},{32,40},{40,32},{48,56},{56,48},{64,72... | collective-permute-start | bytes 1474568 | tf_op jit(solution)/shard_map/ppermute | solution.py:24
  107.6 6.7 %copy-start.15 = (bf16[1920,128]{1,0:T(8,128)(2,1)}, bf16[1920,128]{1,0:T(8,128)(2,1)S(1)}, u32[]{:S(2)}) copy-start(bf16[1920,128]{1,0:T(8,128)(2,1)S(1)} %collective-permute-done.22.refs_16_) | copy-start | bytes 1474564
  114.2 23.3 %collective-permute-start.15 = (bf16[1920,128]{1,0:T(8,128)(2,1)}, bf16[1920,128]{1,0:T(8,128)(2,1)}, u32[]{:S(2)}, u32[]{:S(2)}) collective-permute-start(bf16[1920,128]{1,0:T(8,128)(2,1)} %collective-permute-done.14.refs_3_), channel_id=1, source_target_pairs={{0,8},{8,0},{16,24},{24,16},{32,40},{40,32},{48,56},{56,48},{64,72... | collective-permute-start | bytes 1474568 | tf_op jit(solution)/shard_map/ppermute | solution.py:24
  126.2 0.8 copy-start.5
  146.1 3.0 %collective-permute-start.31 = (f32[64,128]{1,0:T(8,128)}, f32[64,128]{1,0:T(8,128)S(1)}, u32[]{:S(2)}, u32[]{:S(2)}) collective-permute-start(f32[64,128]{1,0:T(8,128)} %shard_map.90), channel_id=1, source_target_pairs={{0,4},{1,5},{2,6},{3,7},{4,0},{5,1},{6,2},{7,3},{8,12},{9,13},{10,... | collective-permute-start | bytes 98312 | tf_op jit(solution)/shard_map/ppermute | solution.py:40
  149.8 2.8 %collective-permute-start.32 = (f32[64,128]{1,0:T(8,128)S(1)}, f32[64,128]{1,0:T(8,128)S(1)}, u32[]{:S(2)}, u32[]{:S(2)}) collective-permute-start(f32[64,128]{1,0:T(8,128)S(1)} %add.418), channel_id=1, source_target_pairs={{0,1},{1,0},{2,3},{3,2},{4,5},{5,4},{6,7},{7,6},{8,9},{9,8},{10,11... | collective-permute-start | bytes 98312 | tf_op jit(solution)/shard_map/ppermute | solution.py:40
  152.6 4.4 %copy-start.17 = (f32[64,128]{1,0:T(8,128)}, f32[64,128]{1,0:T(8,128)S(1)}, u32[]{:S(2)}) copy-start(f32[64,128]{1,0:T(8,128)S(1)} %add.419.mine) | copy-start | bytes 98308
  152.6 4.4 %collective-permute-start.33 = (f32[64,128]{1,0:T(8,128)S(1)}, f32[64,128]{1,0:T(8,128)S(1)}, u32[]{:S(2)}, u32[]{:S(2)}) collective-permute-start(f32[64,128]{1,0:T(8,128)S(1)} %add.419.mine), channel_id=1, source_target_pairs={{0,2},{1,3},{2,0},{3,1},{4,6},{5,7},{6,4},{7,5},{8,10},{9,11},{10,... | collective-permute-start | bytes 98312 | tf_op jit(solution)/shard_map/ppermute | solution.py:40
  156.4 1.0 copy-start.2
  157.4 0.6 copy-start.19
  175.0 5.4 %copy-start.16 = (bf16[16,16,128]{2,1,0:T(8,128)(2,1)}, bf16[16,16,128]{2,1,0:T(8,128)(2,1)S(1)}, u32[]{:S(2)}) copy-start(bf16[16,16,128]{2,1,0:T(8,128)(2,1)S(1)} %all_to_all.5.mine) | copy-start | bytes 196612
  175.0 5.4 %collective-permute-start.34 = (bf16[16,16,128]{2,1,0:T(8,128)(2,1)S(1)}, bf16[16,16,128]{2,1,0:T(8,128)(2,1)S(1)}, u32[]{:S(2)}, u32[]{:S(2)}) collective-permute-start(bf16[16,16,128]{2,1,0:T(8,128)(2,1)S(1)} %all_to_all.5.mine), channel_id=1, source_target_pairs={{0,8},{8,0},{16,24},{24,16},{32,40},{40,32},{48,56},{56,48},{64,72... | collective-permute-start | bytes 196616 | tf_op jit(solution)/shard_map/ppermute | solution.py:24
  180.4 0.6 copy-start.18

commit v2 on v1

v2 whole, which is shorter than its diff:
```python
import jax
import jax.numpy as jnp
from jax import lax
from jax.experimental import pallas as pl
from jax.experimental.pallas import tpu as pltpu
from jax.sharding import PartitionSpec as P

SEQ = 256
SIDE = 4
LANES = 128
HALF = 896
VMEM_BYTES = 56 << 20
LAST = (((1,), (1,)), ((), ()))


def dp_id(x, z, c):
    return ((x % SIDE) * SIDE + z % SIDE) * 2 + c


PLACES = [(x, z, c) for x in range(SIDE) for z in range(SIDE) for c in range(2)]
SAME_CORE = [[dp_id(x, z, c) for x in range(SIDE) for z in range(SIDE)] for c in range(2)]


FROM = (0, -1, 1, -2)
X_ORDER = [
    (1, 0), (2, 0), (3, 0), (1, 1), (2, 1), (1, 2), (2, 2), (3, 1), (1, 3), (3, 2), (2, 3), (3, 3),
]
IN_FLIGHT = 3
ARRIVAL = [(0, 0), (0, 1), (0, 2), (1, 0), (2, 0), (3, 0), (1, 1), (2, 1), (1, 2), (2, 2), (3, 1), (0, 3)]
ARRIVAL += [(1, 3), (3, 2), (2, 3), (3, 3)]


def dp_move(value, where):
    return lax.ppermute(value, "dp", [(dp_id(*s), dp_id(*where(*s))) for s in PLACES])


def x_step(value, way):
    return dp_move(value, lambda x, z, c: (x + way * (1 - 2 * c), z, c))


def z_step(value, way):
    return dp_move(value, lambda x, z, c: (x, z + way * (1 - 2 * c), c))


def core_swap(value):
    return dp_move(value, lambda x, z, c: (x, z, 1 - c))


def tensor_swap(value, bit):
    return lax.ppermute(value, "tensor", [(t, t ^ bit) for t in range(8)])


def after(value, *others):
    return lax.optimization_barrier((value,) + others)[0]


def piece_copies(table, grads, pieces, first, weight, grad, queries, sem):
    made = []
    for p, piece in enumerate(pieces):
        k = first + 2 * p
        made.append((piece.at[:, :HALF], weight.at[k:k + 2]))
        made.append((piece.at[:, HALF:], queries.at[k:k + 2]))
    for k in range(first, first + 2 * len(pieces)):
        span = pl.ds(pl.multiple_of(table[k] * LANES, LANES), LANES)
        made += [(grads[side].at[:, span], grad.at[side, k]) for side in range(2)]
    return [pltpu.make_async_copy(x, y, sem) for x, y in made]


def start(copies):
    for copy in copies:
        copy.start()


def finish(copies):
    for copy in copies:
        copy.wait()


def product(weight, grad, span, e):
    left = jnp.concatenate([weight[k] for k in span], axis=1)
    rows = slice((e % 2) * SEQ, (e % 2 + 1) * SEQ)
    right = jnp.concatenate([grad[e // 2, k, rows, :] for k in span], axis=1)
    return lax.dot_general(left, right, LAST, preferred_element_type=jnp.float32)


def early_kernel(count, table, *refs):
    grads, pieces = refs[:2], refs[2:2 + count]
    out, queries, weight, grad, total, sems, out_sem = refs[2 + count:]
    groups = count // SIDE
    moving = [
        piece_copies(
            table, grads, pieces[SIDE * b:SIDE * b + SIDE], 2 * SIDE * b, weight, grad, queries, sems.at[b]
        )
        for b in range(groups)
    ]
    start(moving[0])
    start(moving[1])
    for b in range(groups):
        finish(moving[b])
        if b + 2 < groups:
            start(moving[b + 2])

        @pl.when(table[0] >= 0)
        def _():
            for e in range(4):
                value = product(weight, grad, range(2 * SIDE * b, 2 * SIDE * (b + 1)), e)
                total[e] = value if b == 0 else value + total[e]
    write = pltpu.make_async_copy(total, out, out_sem)
    write.start()
    write.wait()


def late_kernel(count, table, *refs):
    grads, pieces = refs[:2], refs[2:2 + count]
    held, gate_own, gate_other, proj_out, in_own, in_other = refs[2 + count:8 + count]
    out_own, out_other, queries, weight, grad, total, value, gate, sem, total_sem = refs[8 + count:]
    moving = piece_copies(table, grads, pieces, 0, weight, grad, queries, sem)
    later = [pltpu.make_async_copy(held, total, total_sem)]
    later += [pltpu.make_async_copy(ref, gate.at[n], total_sem) for n, ref in enumerate((gate_own, gate_other))]
    start(moving)
    start(later)
    finish(moving)

    @pl.when(table[0] >= 0)
    def _():
        for e in range(4):
            value[e] = product(weight, grad, range(2 * count), e)

    finish(later)
    sides = []
    for e in range(4):
        v = gate[e // 2, :, (e % 2) * SEQ:(e % 2 + 1) * SEQ].astype(jnp.float32)
        up_grad = ((value[e] + total[e]) * (v / (1.0 + jnp.exp(-v)))).astype(jnp.bfloat16)
        sides.append(jnp.dot(proj_out[...], up_grad, preferred_element_type=jnp.float32))
    for e, out_side in enumerate(sides):
        in_side = (in_own, in_other)[e // 2][:, (e % 2) * SEQ:(e % 2 + 1) * SEQ]
        sketch = lax.dot_general(
            out_side, in_side, LAST, preferred_element_type=jnp.float32, precision=lax.Precision.HIGHEST
        )
        out = (out_own, out_other)[e // 2]
        out[(e % 2) * 32:(e % 2 + 1) * 32, :] = jnp.concatenate([sketch[:32], sketch[32:]], axis=1)


def grad_part(table, grads, pieces, tail=None):
    count = len(pieces)
    rows = grads[0].shape[0]
    smem, vmem, anywhere = [pl.BlockSpec(memory_space=m) for m in (pltpu.SMEM, pltpu.VMEM, pl.ANY)]
    total = ((4, HALF, SEQ), jnp.float32)
    queries = jax.ShapeDtypeStruct((2 * count, 64, LANES), jnp.bfloat16)
    scratch = [
        pltpu.VMEM((2 * count, HALF, LANES), jnp.bfloat16),
        pltpu.VMEM((2, 2 * count, rows, LANES), jnp.bfloat16),
        pltpu.VMEM(*total),
    ]
    if tail:
        kernel = late_kernel
        shapes, out_specs = [jax.ShapeDtypeStruct((64, LANES), jnp.float32)] * 2, [vmem] * 3
        in_specs = [anywhere] * (5 + count) + [vmem] * 3
        scratch += [pltpu.VMEM(*total), pltpu.VMEM((2, HALF, rows), jnp.bfloat16)]
        scratch += [pltpu.SemaphoreType.DMA, pltpu.SemaphoreType.DMA]
    else:
        kernel = early_kernel
        shapes, out_specs = [jax.ShapeDtypeStruct(*total)], [anywhere, vmem]
        in_specs = [anywhere] * (2 + count)
        scratch += [pltpu.SemaphoreType.DMA((count // SIDE,)), pltpu.SemaphoreType.DMA]
    return pl.pallas_call(
        lambda *refs: kernel(count, *refs),
        out_shape=shapes + [queries],
        in_specs=[smem] + in_specs,
        out_specs=out_specs,
        scratch_shapes=scratch,
        compiler_params=pltpu.CompilerParams(vmem_limit_bytes=VMEM_BYTES),
        cost_estimate=pl.CostEstimate(
            flops=8 * rows * HALF * count * LANES, bytes_accessed=count << 20, transcendentals=0
        ),
    )(table, *grads, *pieces, *(tail or ()))


def split3(value):
    high = value.astype(jnp.bfloat16)
    rest = value - high.astype(jnp.float32)
    mid = rest.astype(jnp.bfloat16)
    low = (rest - mid.astype(jnp.float32)).astype(jnp.bfloat16)
    return high, mid, low


def send_kernel(parts_count, place, order, parts, *refs):
    own_queries, other_queries = refs[:parts_count], refs[parts_count:2 * parts_count]
    payload, raw_scores, wide, left = refs[2 * parts_count:]
    sketch = parts[0]
    for k in range(1, 8):
        sketch = sketch + parts[k]
    wide[...] = sketch.astype(jnp.bfloat16).astype(jnp.float32)
    whole = wide[...]
    squares = jnp.sum(jnp.sum(whole * whole, axis=0, keepdims=True), axis=1, keepdims=True)
    parts = [v.astype(jnp.float32) for v in split3(jnp.broadcast_to(squares, (1, LANES)))]
    tails = [[parts[0], parts[1]], [parts[2], jnp.zeros((1, LANES), jnp.float32)]]
    first_col = place[0] * 4
    cols = [[wide[pl.ds(e * 32 + first_col + r, 1), :] for r in range(4)] for e in range(2)]
    for p in range(16):
        rows = []
        for e in range(2):
            rows += cols[e] + [wide[e * 32 + 2 * p:e * 32 + 2 * p + 2, :]] + tails[e]
        payload[p] = jnp.concatenate(rows, axis=0).astype(jnp.bfloat16)
    left[...] = jnp.zeros_like(left)
    raw = []
    for q, queries in enumerate((own_queries, other_queries)):
        for k in range(32):
            for e in range(2):
                left[e:e + 1, k * LANES:(k + 1) * LANES] = wide[pl.ds(e * 32 + order[q * 32 + k], 1), :]
        right = jnp.concatenate([part[k] for part in queries for k in range(part.shape[0])], axis=1)
        raw.append(lax.dot_general(
            left[...].astype(jnp.bfloat16), right, LAST, preferred_element_type=jnp.float32
        ))
    even = (place[1] % 2) == 0
    raw_scores[...] = jnp.where(
        even, jnp.concatenate(raw, axis=1), jnp.concatenate(raw[::-1], axis=1)
    )


def send_part(place, sketches, own_queries, other_queries, order):
    smem, vmem = pl.BlockSpec(memory_space=pltpu.SMEM), pl.BlockSpec(memory_space=pltpu.VMEM)
    return pl.pallas_call(
        lambda *refs: send_kernel(len(own_queries), *refs),
        out_shape=(
            jax.ShapeDtypeStruct((16, 16, LANES), jnp.bfloat16),
            jax.ShapeDtypeStruct((8, LANES), jnp.float32),
        ),
        in_specs=[smem, smem] + [vmem] * (1 + 2 * len(own_queries)),
        out_specs=(vmem, vmem),
        scratch_shapes=[pltpu.VMEM((64, LANES), jnp.float32), pltpu.VMEM((8, 4096), jnp.float32)],
    )(place, order, sketches, *own_queries, *other_queries)


def gram_kernel(place, mine, other, raw_scores, gram, scores):
    t, dp = place[0], place[1]
    odd = (dp % 2) == 1
    blocks = [mine[...].astype(jnp.float32), other[...].astype(jnp.float32)]

    def stack(r):
        return jnp.concatenate([b[:, e * 8 + r, :] for b in blocks for e in range(2)], axis=0)

    trace = jnp.zeros((1, LANES), jnp.float32)
    for b in blocks:
        for r in (15, 14, 7, 6):
            trace = trace + jnp.sum(b[:, r, :], axis=0, keepdims=True)
    row_part = jnp.where(odd, stack(5), stack(4)).astype(jnp.bfloat16)
    for r in range(4):
        raw = lax.dot_general(
            row_part, stack(r).astype(jnp.bfloat16), (((0,), (0,)), ((), ())),
            preferred_element_type=jnp.float32,
        )
        rows = dp * LANES + lax.broadcasted_iota(jnp.int32, raw.shape, 0)
        cols = t * 512 + r * LANES + lax.broadcasted_iota(jnp.int32, raw.shape, 1)
        gram[:, r * LANES:(r + 1) * LANES] = raw * (4096.0 / trace) + jnp.where(rows == cols, 0.1, 0.0)
    scores[...] = raw_scores[:2, :] / jnp.sqrt(trace / 64.0)


def gram_part(place, mine, other, raw_scores):
    smem, vmem = pl.BlockSpec(memory_space=pltpu.SMEM), pl.BlockSpec(memory_space=pltpu.VMEM)
    return pl.pallas_call(
        gram_kernel,
        out_shape=(
            jax.ShapeDtypeStruct((LANES, 512), jnp.float32),
            jax.ShapeDtypeStruct((2, LANES), jnp.float32),
        ),
        in_specs=[smem, vmem, vmem, vmem],
        out_specs=(vmem, vmem),
    )(place, mine, other, raw_scores)


def halves(value, c, axis):
    size = value.shape[axis] // 2
    return [lax.dynamic_slice_in_dim(value, h * size, size, axis) for h in (c, 1 - c)]


def gather_pieces(down_weight, query, c):
    pair = (down_weight, query)
    first = jnp.stack([
        jnp.concatenate([halves(v, c, 0)[0] for v in values])
        for values in (pair, [core_swap(v) for v in pair])
    ])
    held = {(0, 0): first}
    held[0, 1], held[0, 2] = z_step(first, 1), z_step(first, -1)
    held[0, 3] = z_step(held[0, 1], 1)
    for n, (a, b) in enumerate(X_ORDER):
        source = held[1 if a == 3 else 0, b]
        if n >= IN_FLIGHT:
            source = after(source, held[X_ORDER[n - IN_FLIGHT]])
        held[a, b] = x_step(source, -1 if a == 2 else 1)
    return held


def body(acts, output_grad, gate_act, down_weight, proj_in, proj_out, query):
    dp, tensor = lax.axis_index("dp"), lax.axis_index("tensor")
    x, z, c = dp // 8, (dp // 2) % SIDE, dp % 2
    hidden = down_weight.shape[0]

    held = gather_pieces(down_weight, query, c)
    grads = (output_grad, core_swap(after(output_grad, held[0, 0])))
    gate_keep, gate_give = halves(gate_act, c, 1)
    gates = (gate_keep.T, core_swap(after(gate_give, held[0, 0])).T)
    in_proj = lax.dot_general(proj_in, acts, LAST, preferred_element_type=jnp.float32)
    in_projs = (in_proj, core_swap(in_proj))
    proj_half = halves(proj_out, c, 1)[0].reshape(32, 2, hidden // 2)
    proj_half = jnp.concatenate([proj_half[:, k] for k in range(2)], axis=0)

    def columns(keys, core):
        sign = 1 - 2 * core
        return jnp.stack([
            dp_id(x + sign * FROM[a], z + sign * FROM[b], k) for a, b in keys for k in (core, 1 - core)
        ]).astype(jnp.int32)

    early, late = ARRIVAL[:12], ARRIVAL[12:]
    total, early_queries = grad_part(columns(early, c), grads, [held[key] for key in early])
    own_part, other_part, late_queries = grad_part(
        columns(late, c), grads, [held[key] for key in late], (total, *gates, proj_half, *in_projs)
    )
    own_queries = [early_queries, late_queries]
    other_queries = [core_swap(part) for part in own_queries]
    order = jnp.concatenate([columns(ARRIVAL, c), columns(ARRIVAL, 1 - c)])
    sketch = own_part + core_swap(other_part)
    sketches = lax.all_to_all(jnp.broadcast_to(sketch[None], (8,) + sketch.shape), "tensor", 0, 0)
    place = jnp.stack([tensor, dp]).astype(jnp.int32)
    payload, raw_scores = send_part(place, sketches, own_queries, other_queries, order)
    mine = lax.all_to_all(payload, "dp", 0, 0, axis_index_groups=SAME_CORE)
    return gram_part(place, mine, core_swap(mine), raw_scores)


def solution(mesh):
    placed = (
        P("dp", None),
        P("dp", None),
        P("dp", "tensor"),
        P("tensor", "dp"),
        P(),
        P(None, "tensor"),
        P("tensor", "dp"),
    )
    return jax.shard_map(
        body,
        mesh=mesh,
        in_specs=placed,
        out_specs=(P("dp", "tensor"), P("dp", "tensor")),
        check_vma=False,
    )
```

time: 186 us -> 138 us (0.74); the launches traced: 183 us -> 137 us
  Pallas kernels: 49.3 us -> 24.9 us
  local copies, waits for them, and re-layouts: 24.8 us -> 12.8 us
  starting transfers between devices: 53.1 us -> 43.5 us
  blocking collectives: 14.7 us -> 17.3 us
    pallas_call x6 -> x3, Pallas kernels: 47.5 us -> 23 us  [the longest x2 20.7 us: grad_part(): pl.pallas_call(lambda *refs: kernel(count, *refs), out_shape=shapes + [qu...]
    unnamed x72 -> x43, local copies, waits for them, and re-layouts: 19.4 us -> 5.17 us
    ppermute x32 -> x24, starting transfers between devices: 48.6 us -> 36.8 us  [dp_move(): lax.ppermute(value, 'dp', [(dp_id(*s), dp_id(*where(*s))) for s in PLACES])]
    all_to_all x0 -> x1, starting transfers between devices: none -> 6.75 us  [body(): lax.all_to_all(jnp.broadcast_to(sketch[None], (8,) + sketch.shape), 'tens...]
    ppermute x3 -> x0, starting transfers between devices: 4.58 us -> none  [tensor_swap(): return lax.ppermute(value, 'tensor', [(t, t ^ bit) for t in range(8)])]
    dynamic_slice x0 -> x6, local copies, waits for them, and re-layouts: none -> 4.22 us  [halves(): lax.dynamic_slice_in_dim(value, h * size, size, axis)]
    all_to_all x0 -> x1, waiting for transfers between devices: none -> 3.73 us  [body(): lax.all_to_all(jnp.broadcast_to(sketch[None], (8,) + sketch.shape), 'tens...]
    ppermute x3 -> x0, waiting for transfers between devices: 3.29 us -> none  [tensor_swap(): return lax.ppermute(value, 'tensor', [(t, t ^ bit) for t in range(8)])]
  transfers between devices with their start and end apart: 35 -> 25, of which waited for: 10 -> 8; matrix products, arithmetic and copies ran while one was open for 14% -> 10% of each run, Pallas kernels for 20% -> 9%
where the time goes in v2:
time: 138 us; the launch traced here: 137 us
  starting transfers between devices  43.5 us (32%)
  waiting for transfers between devices  32 us (23%)
  Pallas kernels  24.9 us (18%)
  blocking collectives  17.3 us (13%)
  local copies, waits for them, and re-layouts  12.8 us (9%)
  matrix products  3.58 us (3%)
  other arithmetic  2.15 us (2%)
    ppermute x24, starting transfers between devices, dp_move(): lax.ppermute(value, 'dp', [(dp_id(*s), dp_id(*where(*s))) for s in PLACES])  36.8 us
    ppermute x24, waiting for transfers between devices, dp_move(): lax.ppermute(value, 'dp', [(dp_id(*s), dp_id(*where(*s))) for s in PLACES])  28.2 us
    pallas_call x2, Pallas kernels, grad_part(): pl.pallas_call(lambda *refs: kernel(count, *refs), out_shape=shapes + [qu...  20.7 us
    all_to_all x1, blocking collectives, body(): mine = lax.all_to_all(payload, 'dp', 0, 0, axis_index_groups=SAME_CORE)  17.3 us
    all_to_all x1, starting transfers between devices, body(): lax.all_to_all(jnp.broadcast_to(sketch[None], (8,) + sketch.shape), 'tens...  6.75 us
    unnamed x43, local copies, waits for them, and re-layouts  5.17 us
    dynamic_slice x6, local copies, waits for them, and re-layouts, halves(): lax.dynamic_slice_in_dim(value, h * size, size, axis)  4.22 us
    all_to_all x1, waiting for transfers between devices, body(): lax.all_to_all(jnp.broadcast_to(sketch[None], (8,) + sketch.shape), 'tens...  3.73 us
  transfers between devices with their start and end apart: 25, of which 8 were waited for; matrix products, arithmetic and copies ran while one was open for 10% of the time, Pallas kernels for 9%

profile of v2, /device:TPU:1, one launch (start us, length us, event | category | flops | bytes accessed | tf_op | source)
XLA Modules:
  0.0 137.2 jit_solution(7035760742061286617)
XLA Ops:
  0.6 0.0 copy-start
  0.6 3.3 %collective-permute-start = (bf16[1792,128]{1,0:T(8,128)(2,1)}, bf16[1792,128]{1,0:T(8,128)(2,1)S(1)}, u32[]{:S(2)}, u32[]{:S(2)}) collective-permute-start(bf16[1792,128]{1,0:T(8,128)(2,1)} %param.10), channel_id=1, source_target_pairs={{0,8},{8,0},{16,24},{24,16},{32,40},{40,32},{48,56},{56,48},{64,72... | collective-permute-start | bytes 1376264 | tf_op jit(solution)/shard_map/ppermute | solution.py:34
  4.0 0.1 collective-permute-start.1
  4.1 0.7 constant_dynamic-slice_fusion.5
  4.8 1.0 constant_dynamic-slice_fusion.6
  5.8 0.0 collective-permute-done
  5.9 0.5 collective-permute-start.2
  6.4 0.7 collective-permute-start.6
  7.2 6.0 %collective-permute-start.3 = (bf16[2,960,128]{2,1,0:T(8,128)(2,1)S(1)}, bf16[2,960,128]{2,1,0:T(8,128)(2,1)S(1)}, u32[]{:S(2)}, u32[]{:S(2)}) collective-permute-start(bf16[2,960,128]{2,1,0:T(8,128)(2,1)S(1)} %pad_maximum_fusion.refs_3_), channel_id=1, source_target_pairs={{0,16},{8,56},{16,32},{24,8},{32,48},{40,24},{48,0},{56,40},{64,80... | collective-permute-start | bytes 1474568 | tf_op jit(solution)/shard_map/ppermute | solution.py:34
  13.2 0.0 collective-permute-start.13
  13.2 2.8 %collective-permute-done.6.refs_6_ = bf16[2,960,128]{2,1,0:T(8,128)(2,1)S(1)} collective-permute-done((bf16[2,960,128]{2,1,0:T(8,128)(2,1)S(1)}, bf16[2,960,128]{2,1,0:T(8,128)(2,1)S(1)}, u32[]{:S(2)}, u32[]{:S(2)}) %collective-permute-start.6) | collective-permute-done | bytes 491552 | tf_op jit(solution)/shard_map/ppermute | solution.py:34
  16.0 1.2 collective-permute-start.7
  17.3 14.3 %collective-permute-done.3.refs_4_ = bf16[2,960,128]{2,1,0:T(8,128)(2,1)S(1)} collective-permute-done((bf16[2,960,128]{2,1,0:T(8,128)(2,1)S(1)}, bf16[2,960,128]{2,1,0:T(8,128)(2,1)S(1)}, u32[]{:S(2)}, u32[]{:S(2)}) %collective-permute-start.3) | collective-permute-done | bytes 491552 | tf_op jit(solution)/shard_map/ppermute | solution.py:34
  31.5 0.1 collective-permute-start.10
  31.6 0.0 collective-permute-done.13.refs_7_
  31.6 1.3 collective-permute-start.14
  33.0 0.0 collective-permute-done.5.refs_5_
  33.0 4.6 %collective-permute-start.4 = (bf16[2,960,128]{2,1,0:T(8,128)(2,1)S(1)}, bf16[2,960,128]{2,1,0:T(8,128)(2,1)}, u32[]{:S(2)}, u32[]{:S(2)}) collective-permute-start(bf16[2,960,128]{2,1,0:T(8,128)(2,1)S(1)} %collective-permute-done.3.refs_4_), channel_id=1, source_target_pairs={{0,16},{8,56},{16,32},{24,8},{32,48},{40,24},{48,0},{56,40},{64,80... | collective-permute-start | bytes 1474568 | tf_op jit(solution)/shard_map/ppermute | solution.py:34
  37.6 0.0 collective-permute-done.7.refs_8_
  37.6 0.8 copy-done.17
  38.4 1.5 %collective-permute-start.8 = (bf16[2,960,128]{2,1,0:T(8,128)(2,1)}, bf16[2,960,128]{2,1,0:T(8,128)(2,1)S(1)}, u32[]{:S(2)}, u32[]{:S(2)}) collective-permute-start(bf16[2,960,128]{2,1,0:T(8,128)(2,1)} %collective-permute-done.5.refs_5_), channel_id=1, source_target_pairs={{0,64},{8,200},{16,80},{24,216},{32,96},{40,232},{48,112},{56,248}... | collective-permute-start | bytes 1474568 | tf_op jit(solution)/shard_map/ppermute | solution.py:34
  39.9 0.9 constant_dynamic-slice_fusion
  40.9 0.2 fusion
  41.1 0.0 collective-permute-done.14.refs_10_
  41.1 1.1 collective-permute-start.15
  42.2 0.4 collective-permute-start.11
  42.6 5.6 %collective-permute-done.4.refs_14_ = bf16[2,960,128]{2,1,0:T(8,128)(2,1)} collective-permute-done((bf16[2,960,128]{2,1,0:T(8,128)(2,1)S(1)}, bf16[2,960,128]{2,1,0:T(8,128)(2,1)}, u32[]{:S(2)}, u32[]{:S(2)}) %collective-permute-start.4) | collective-permute-done | bytes 491552 | tf_op jit(solution)/shard_map/ppermute | solution.py:34
  48.2 0.0 collective-permute-done.8.refs_11_
  48.2 0.8 copy-done.18
  49.0 1.5 %collective-permute-start.9 = (bf16[2,960,128]{2,1,0:T(8,128)(2,1)}, bf16[2,960,128]{2,1,0:T(8,128)(2,1)}, u32[]{:S(2)}, u32[]{:S(2)}) collective-permute-start(bf16[2,960,128]{2,1,0:T(8,128)(2,1)} %collective-permute-done.4.refs_14_), channel_id=1, source_target_pairs={{0,64},{8,200},{16,80},{24,216},{32,96},{40,232},{48,112},{56,248}... | collective-permute-start | bytes 1474568 | tf_op jit(solution)/shard_map/ppermute | solution.py:34
  50.5 1.6 %constant_dynamic-slice_fusion.1 = (bf16[512,896]{1,0:T(8,128)(2,1)S(1)}, bf16[512,896]{1,0:T(8,128)(2,1)S(1)}) fusion(bf16[512,1792]{1,0:T(8,128)(2,1)} %param.9, s32[]{:T(128)S(6)} %select_n.463, s32[]{:T(128)S(6)} %select_n.461), kind=kLoop, calls=%fused_computation.7 | loop fusion | bytes 3670024 | tf_op jit(solution)/shard_map/dynamic_slice | solution.py:274
  52.1 0.5 copy.16
  52.6 4.2 %collective-permute-start.18 = (bf16[512,896]{0,1:T(8,128)(2,1)S(1)}, bf16[512,896]{0,1:T(8,128)(2,1)S(1)}, u32[]{:S(2)}, u32[]{:S(2)}) collective-permute-start(bf16[512,896]{0,1:T(8,128)(2,1)S(1)} %copy.16), channel_id=1, source_target_pairs={{0,8},{8,0},{16,24},{24,16},{32,40},{40,32},{48,56},{56,48},{64,72... | collective-permute-start | bytes 2752520 | tf_op jit(solution)/shard_map/ppermute | solution.py:34
  56.9 0.6 pad_maximum_fusion.1.refs_10_
  57.5 1.4 %copy.15 = bf16[512,896]{0,1:T(8,128)(2,1)} copy(bf16[512,896]{1,0:T(8,128)(2,1)S(1)} %get-tuple-element.39) | data formatting | bytes 1835008
  58.9 0.6 stack.309.refs_0_
  59.5 0.7 stack.313.refs_0_
  60.2 3.6 %fusion.1.refs_11_ = f32[64,512]{1,0:T(8,128)S(1)} fusion(bf16[64,4096]{1,0:T(8,128)(2,1)S(1)} %copy-done, bf16[512,4096]{1,0:T(8,128)(2,1)} %param.7), kind=kOutput, calls=%fused_computation.15 | convolution fusion | flops 268435456 | bytes 4849664 | tf_op jit(solution)/shard_map/dot_general | solution.py:303
  63.8 0.1 collective-permute-start.19
  63.9 0.3 collective-permute-start.16
  64.3 2.8 %collective-permute-start.12 = (bf16[2,960,128]{2,1,0:T(8,128)(2,1)S(1)}, bf16[2,960,128]{2,1,0:T(8,128)(2,1)S(1)}, u32[]{:S(2)}, u32[]{:S(2)}) collective-permute-start(bf16[2,960,128]{2,1,0:T(8,128)(2,1)S(1)} %copy-done.19), channel_id=1, source_target_pairs={{0,64},{8,200},{16,80},{24,216},{32,96},{40,232},{48,112},{56,248}... | collective-permute-start | bytes 1474568 | tf_op jit(solution)/shard_map/ppermute | solution.py:34
  67.1 1.4 collective-permute-start.17
  68.4 11.7 %shard_map.86 = (f32[4,896,256]{2,1,0:T(8,128)}, bf16[24,64,128]{2,1,0:T(8,128)(2,1)}) custom-call(s32[24]{0:T(128)} %stack.313.refs_0_, bf16[512,4096]{1,0:T(8,128)(2,1)} %refs_1_.3, bf16[512,4096]{1,0:T(8,128)(2,1)} %collective-permute-done.2.refs_2_, bf16[2,960,128]{2,1,0:T(8,128)(2,1)} %copy-done.4, bf16[2,960,128]{2,1,0:T(8,128)(2,1)} %copy-done.15, ...), custom_call_target="tpu_custom_call" | custom-call | flops 5637144576 | bytes 12582912 | tf_op jit(solution)/shard_map/pallas_call | solution.py:166
  80.3 3.2 %collective-permute-done.17.refs_6_ = bf16[2,960,128]{2,1,0:T(8,128)(2,1)S(1)} collective-permute-done((bf16[2,960,128]{2,1,0:T(8,128)(2,1)}, bf16[2,960,128]{2,1,0:T(8,128)(2,1)S(1)}, u32[]{:S(2)}, u32[]{:S(2)}) %collective-permute-start.17) | collective-permute-done | bytes 491552 | tf_op jit(solution)/shard_map/ppermute | solution.py:34
  83.5 0.8 copy-done.7
  84.3 9.0 %shard_map.87 = (f32[64,128]{1,0:T(8,128)}, f32[64,128]{1,0:T(8,128)}, bf16[8,64,128]{2,1,0:T(8,128)(2,1)}) custom-call(s32[8]{0:T(128)} %stack.309.refs_0_, bf16[512,4096]{1,0:T(8,128)(2,1)} %refs_1_.3, bf16[512,4096]{1,0:T(8,128)(2,1)} %collective-permute-done.2.refs_2_, bf16[2,960,128]{2,1,0:T(8,128)(2,1)} %collective-permute-done.9.refs_3_, ...), custom_call_target="tpu_custom_call" | custom-call | flops 1879048192 | bytes 4194304 | tf_op jit(solution)/shard_map/pallas_call | solution.py:166
  93.3 1.2 collective-permute-start.20
  94.5 1.1 collective-permute-done.20
  95.6 0.8 add.915
  96.4 0.7 broadcast_in_dim.2
  97.1 6.8 %all-to-all-start = ((f32[8,64,128]{2,1,0:T(8,128)}), f32[8,64,128]{2,1,0:T(8,128)S(1)}, u32[]{:S(2)}, u32[]{:S(2)}) async-start(f32[8,64,128]{2,1,0:T(8,128)} %broadcast_in_dim.2), calls=%async_computation | async-start | bytes 524288 | tf_op jit(solution)/shard_map/all_to_all | solution.py:323
  103.8 0.7 collective-permute-start.21
  104.6 0.1 collective-permute-start.22
  104.7 0.6 concatenate.12.refs_1_
  105.3 0.7 pad_add_fusion.refs_0_.place
  105.9 0.4 collective-permute-done.22.refs_6_
  106.3 3.7 %all-to-all-done.refs_2_ = f32[8,64,128]{2,1,0:T(8,128)S(1)} async-done(((f32[8,64,128]{2,1,0:T(8,128)}), f32[8,64,128]{2,1,0:T(8,128)S(1)}, u32[]{:S(2)}, u32[]{:S(2)}) %all-to-all-start) | async-done | bytes 262176 | tf_op jit(solution)/shard_map/all_to_all | solution.py:323
  110.1 0.7 copy-done.1
  110.8 2.4 %shard_map.88 = (bf16[16,16,128]{2,1,0:T(8,128)(2,1)}, f32[8,128]{1,0:T(8,128)}) custom-call(s32[2]{0:T(128)} %pad_add_fusion.refs_0_.place, s32[64]{0:T(128)} %concatenate.12.refs_1_, f32[8,64,128]{2,1,0:T(8,128)} %copy-done.1, bf16[24,64,128]{2,1,0:T(8,128)(2,1)} %get-tuple-element.34.refs_3_, bf16[8,64,128]{2,1,0:T(8,128)(2,1)} %get-tuple-element.35.refs_4_, ...), custom_call_target="tpu_custom_call" | custom-call | tf_op jit(solution)/shard_map/pallas_call | solution.py:223
  113.1 17.3 %all_to_all.10.mine = bf16[16,16,128]{2,1,0:T(8,128)(2,1)S(1)} all-to-all(bf16[16,16,128]{2,1,0:T(8,128)(2,1)} %get-tuple-element.36), channel_id=1, replica_groups={{0,16,32,48,64,80,96,112,128,144,160,176,192,208,224,240},{8,24,40,56,7..., dimensions={0} | all-to-all | bytes 131072 | tf_op jit(solution)/shard_map/all_to_all | solution.py:326
  130.4 3.4 %collective-permute-start.23 = (bf16[16,16,128]{2,1,0:T(8,128)(2,1)S(1)}, bf16[16,16,128]{2,1,0:T(8,128)(2,1)S(1)}, u32[]{:S(2)}, u32[]{:S(2)}) collective-permute-start(bf16[16,16,128]{2,1,0:T(8,128)(2,1)S(1)} %all_to_all.10.mine), channel_id=1, source_target_pairs={{0,8},{8,0},{16,24},{24,16},{32,40},{40,32},{48,56},{56,48},{64,72... | collective-permute-start | bytes 196616 | tf_op jit(solution)/shard_map/ppermute | solution.py:34
  133.8 0.9 collective-permute-done.23.other
  134.7 0.6 copy-done.13
  135.3 1.8 %shard_map.89 = (f32[128,512]{1,0:T(8,128)}, f32[2,128]{1,0:T(2,128)}) custom-call(s32[2]{0:T(128)} %pad_add_fusion.refs_0_.place, bf16[16,16,128]{2,1,0:T(8,128)(2,1)} %copy-done.10, bf16[16,16,128]{2,1,0:T(8,128)(2,1)} %copy-done.13, f32[8,128]{1,0:T(8,128)} %get-tuple-element.37.raw_scores), custom_call_target="tpu_custom_call" | custom-call | tf_op jit(solution)/shard_map/pallas_call | solution.py:261
  (55 shorter events, 0.3 us)
Async XLA Ops:
  0.6 59.6 %copy-start = (bf16[64,4096]{1,0:T(8,128)(2,1)S(1)}, bf16[64,4096]{1,0:T(8,128)(2,1)}, u32[]{:S(2)}) copy-start(bf16[64,4096]{1,0:T(8,128)(2,1)} %param.11) | copy-start | bytes 1572868
  0.6 5.2 %collective-permute-start = (bf16[1792,128]{1,0:T(8,128)(2,1)}, bf16[1792,128]{1,0:T(8,128)(2,1)S(1)}, u32[]{:S(2)}, u32[]{:S(2)}) collective-permute-start(bf16[1792,128]{1,0:T(8,128)(2,1)} %param.10), channel_id=1, source_target_pairs={{0,8},{8,0},{16,24},{24,16},{32,40},{40,32},{48,56},{56,48},{64,72... | collective-permute-start | bytes 1376264 | tf_op jit(solution)/shard_map/ppermute | solution.py:34
  4.0 1.8 %collective-permute-start.1 = (bf16[128,128]{1,0:T(8,128)(2,1)}, bf16[128,128]{1,0:T(8,128)(2,1)S(1)}, u32[]{:S(2)}, u32[]{:S(2)}) collective-permute-start(bf16[128,128]{1,0:T(8,128)(2,1)} %param.13), channel_id=1, source_target_pairs={{0,8},{8,0},{16,24},{24,16},{32,40},{40,32},{48,56},{56,48},{64,72... | collective-permute-start | bytes 98312 | tf_op jit(solution)/shard_map/ppermute | solution.py:34
  5.9 7.3 %copy-start.4 = (bf16[2,960,128]{2,1,0:T(8,128)(2,1)}, bf16[2,960,128]{2,1,0:T(8,128)(2,1)S(1)}, u32[]{:S(2)}) copy-start(bf16[2,960,128]{2,1,0:T(8,128)(2,1)S(1)} %pad_maximum_fusion.refs_3_) | copy-start | bytes 1474564
  5.9 61.1 %collective-permute-start.2 = (bf16[512,4096]{1,0:T(8,128)(2,1)}, bf16[512,4096]{1,0:T(8,128)(2,1)}, u32[]{:S(2)}, u32[]{:S(2)}) collective-permute-start(bf16[512,4096]{1,0:T(8,128)(2,1)} %refs_1_.3), channel_id=1, source_target_pairs={{0,8},{8,0},{16,24},{24,16},{32,40},{40,32},{48,56},{56,48},{64,72... | collective-permute-start | bytes 12582920 | tf_op jit(solution)/shard_map/ppermute | solution.py:34
  6.4 9.6 %collective-permute-start.6 = (bf16[2,960,128]{2,1,0:T(8,128)(2,1)S(1)}, bf16[2,960,128]{2,1,0:T(8,128)(2,1)S(1)}, u32[]{:S(2)}, u32[]{:S(2)}) collective-permute-start(bf16[2,960,128]{2,1,0:T(8,128)(2,1)S(1)} %pad_maximum_fusion.refs_3_), channel_id=1, source_target_pairs={{0,64},{8,200},{16,80},{24,216},{32,96},{40,232},{48,112},{56,248}... | collective-permute-start | bytes 1474568 | tf_op jit(solution)/shard_map/ppermute | solution.py:34
  7.2 24.3 %collective-permute-start.3 = (bf16[2,960,128]{2,1,0:T(8,128)(2,1)S(1)}, bf16[2,960,128]{2,1,0:T(8,128)(2,1)S(1)}, u32[]{:S(2)}, u32[]{:S(2)}) collective-permute-start(bf16[2,960,128]{2,1,0:T(8,128)(2,1)S(1)} %pad_maximum_fusion.refs_3_), channel_id=1, source_target_pairs={{0,16},{8,56},{16,32},{24,8},{32,48},{40,24},{48,0},{56,40},{64,80... | collective-permute-start | bytes 1474568 | tf_op jit(solution)/shard_map/ppermute | solution.py:34
  13.2 18.4 %collective-permute-start.13 = (bf16[2,960,128]{2,1,0:T(8,128)(2,1)S(1)}, bf16[2,960,128]{2,1,0:T(8,128)(2,1)S(1)}, u32[]{:S(2)}, u32[]{:S(2)}) collective-permute-start(bf16[2,960,128]{2,1,0:T(8,128)(2,1)S(1)} %pad_maximum_fusion.refs_3_), channel_id=1, source_target_pairs={{0,192},{8,72},{16,208},{24,88},{32,224},{40,104},{48,240},{56,120... | collective-permute-start | bytes 1474568 | tf_op jit(solution)/shard_map/ppermute | solution.py:34
  13.2 19.8 %collective-permute-start.5 = (bf16[2,960,128]{2,1,0:T(8,128)(2,1)S(1)}, bf16[2,960,128]{2,1,0:T(8,128)(2,1)}, u32[]{:S(2)}, u32[]{:S(2)}) collective-permute-start(bf16[2,960,128]{2,1,0:T(8,128)(2,1)S(1)} %pad_maximum_fusion.refs_3_), channel_id=1, source_target_pairs={{0,48},{8,24},{16,0},{24,40},{32,16},{40,56},{48,32},{56,8},{64,11... | collective-permute-start | bytes 1474568 | tf_op jit(solution)/shard_map/ppermute | solution.py:34
  16.0 21.6 %copy-start.14 = (bf16[2,960,128]{2,1,0:T(8,128)(2,1)}, bf16[2,960,128]{2,1,0:T(8,128)(2,1)S(1)}, u32[]{:S(2)}) copy-start(bf16[2,960,128]{2,1,0:T(8,128)(2,1)S(1)} %collective-permute-done.6.refs_6_) | copy-start | bytes 1474564
  16.0 21.6 %collective-permute-start.7 = (bf16[2,960,128]{2,1,0:T(8,128)(2,1)S(1)}, bf16[2,960,128]{2,1,0:T(8,128)(2,1)S(1)}, u32[]{:S(2)}, u32[]{:S(2)}) collective-permute-start(bf16[2,960,128]{2,1,0:T(8,128)(2,1)S(1)} %collective-permute-done.6.refs_6_), channel_id=1, source_target_pairs={{0,64},{8,200},{16,80},{24,216},{32,96},{40,232},{48,112},{56,248}... | collective-permute-start | bytes 1474568 | tf_op jit(solution)/shard_map/ppermute | solution.py:34
  31.5 16.7 %copy-start.15 = (bf16[2,960,128]{2,1,0:T(8,128)(2,1)}, bf16[2,960,128]{2,1,0:T(8,128)(2,1)S(1)}, u32[]{:S(2)}) copy-start(bf16[2,960,128]{2,1,0:T(8,128)(2,1)S(1)} %collective-permute-done.3.refs_4_) | copy-start | bytes 1474564
  31.5 9.6 %collective-permute-start.10 = (bf16[2,960,128]{2,1,0:T(8,128)(2,1)S(1)}, bf16[2,960,128]{2,1,0:T(8,128)(2,1)}, u32[]{:S(2)}, u32[]{:S(2)}) collective-permute-start(bf16[2,960,128]{2,1,0:T(8,128)(2,1)S(1)} %collective-permute-done.3.refs_4_), channel_id=1, source_target_pairs={{0,64},{8,200},{16,80},{24,216},{32,96},{40,232},{48,112},{56,248}... | collective-permute-start | bytes 1474568 | tf_op jit(solution)/shard_map/ppermute | solution.py:34
  31.6 6.0 %copy-start.16 = (bf16[2,960,128]{2,1,0:T(8,128)(2,1)}, bf16[2,960,128]{2,1,0:T(8,128)(2,1)S(1)}, u32[]{:S(2)}) copy-start(bf16[2,960,128]{2,1,0:T(8,128)(2,1)S(1)} %collective-permute-done.13.refs_7_) | copy-start | bytes 1474564
  31.6 9.4 %collective-permute-start.14 = (bf16[2,960,128]{2,1,0:T(8,128)(2,1)S(1)}, bf16[2,960,128]{2,1,0:T(8,128)(2,1)S(1)}, u32[]{:S(2)}, u32[]{:S(2)}) collective-permute-start(bf16[2,960,128]{2,1,0:T(8,128)(2,1)S(1)} %collective-permute-done.3.refs_4_), channel_id=1, source_target_pairs={{0,192},{8,72},{16,208},{24,88},{32,224},{40,104},{48,240},{56,120... | collective-permute-start | bytes 1474568 | tf_op jit(solution)/shard_map/ppermute | solution.py:34
  33.0 15.2 %collective-permute-start.4 = (bf16[2,960,128]{2,1,0:T(8,128)(2,1)S(1)}, bf16[2,960,128]{2,1,0:T(8,128)(2,1)}, u32[]{:S(2)}, u32[]{:S(2)}) collective-permute-start(bf16[2,960,128]{2,1,0:T(8,128)(2,1)S(1)} %collective-permute-done.3.refs_4_), channel_id=1, source_target_pairs={{0,16},{8,56},{16,32},{24,8},{32,48},{40,24},{48,0},{56,40},{64,80... | collective-permute-start | bytes 1474568 | tf_op jit(solution)/shard_map/ppermute | solution.py:34
  37.6 0.8 copy-start.17
  38.4 9.8 %collective-permute-start.8 = (bf16[2,960,128]{2,1,0:T(8,128)(2,1)}, bf16[2,960,128]{2,1,0:T(8,128)(2,1)S(1)}, u32[]{:S(2)}, u32[]{:S(2)}) collective-permute-start(bf16[2,960,128]{2,1,0:T(8,128)(2,1)} %collective-permute-done.5.refs_5_), channel_id=1, source_target_pairs={{0,64},{8,200},{16,80},{24,216},{32,96},{40,232},{48,112},{56,248}... | collective-permute-start | bytes 1474568 | tf_op jit(solution)/shard_map/ppermute | solution.py:34
  41.1 7.1 %copy-start.20 = (bf16[2,960,128]{2,1,0:T(8,128)(2,1)}, bf16[2,960,128]{2,1,0:T(8,128)(2,1)S(1)}, u32[]{:S(2)}) copy-start(bf16[2,960,128]{2,1,0:T(8,128)(2,1)S(1)} %collective-permute-done.14.refs_10_) | copy-start | bytes 1474564
  41.1 22.7 %collective-permute-start.15 = (bf16[2,960,128]{2,1,0:T(8,128)(2,1)}, bf16[2,960,128]{2,1,0:T(8,128)(2,1)}, u32[]{:S(2)}, u32[]{:S(2)}) collective-permute-start(bf16[2,960,128]{2,1,0:T(8,128)(2,1)} %collective-permute-done.10.refs_9_), channel_id=1, source_target_pairs={{0,64},{8,200},{16,80},{24,216},{32,96},{40,232},{48,112},{56,248}... | collective-permute-start | bytes 1474568 | tf_op jit(solution)/shard_map/ppermute | solution.py:34
  42.2 21.7 %collective-permute-start.11 = (bf16[2,960,128]{2,1,0:T(8,128)(2,1)}, bf16[2,960,128]{2,1,0:T(8,128)(2,1)}, u32[]{:S(2)}, u32[]{:S(2)}) collective-permute-start(bf16[2,960,128]{2,1,0:T(8,128)(2,1)} %collective-permute-done.5.refs_5_), channel_id=1, source_target_pairs={{0,192},{8,72},{16,208},{24,88},{32,224},{40,104},{48,240},{56,120... | collective-permute-start | bytes 1474568 | tf_op jit(solution)/shard_map/ppermute | solution.py:34
  48.2 0.8 copy-start.18
  49.0 15.3 %collective-permute-start.9 = (bf16[2,960,128]{2,1,0:T(8,128)(2,1)}, bf16[2,960,128]{2,1,0:T(8,128)(2,1)}, u32[]{:S(2)}, u32[]{:S(2)}) collective-permute-start(bf16[2,960,128]{2,1,0:T(8,128)(2,1)} %collective-permute-done.4.refs_14_), channel_id=1, source_target_pairs={{0,64},{8,200},{16,80},{24,216},{32,96},{40,232},{48,112},{56,248}... | collective-permute-start | bytes 1474568 | tf_op jit(solution)/shard_map/ppermute | solution.py:34
  52.6 27.5 %collective-permute-start.18 = (bf16[512,896]{0,1:T(8,128)(2,1)S(1)}, bf16[512,896]{0,1:T(8,128)(2,1)S(1)}, u32[]{:S(2)}, u32[]{:S(2)}) collective-permute-start(bf16[512,896]{0,1:T(8,128)(2,1)S(1)} %copy.16), channel_id=1, source_target_pairs={{0,8},{8,0},{16,24},{24,16},{32,40},{40,32},{48,56},{56,48},{64,72... | collective-permute-start | bytes 2752520 | tf_op jit(solution)/shard_map/ppermute | solution.py:34
  58.9 5.4 %copy-start.19 = (bf16[2,960,128]{2,1,0:T(8,128)(2,1)S(1)}, bf16[2,960,128]{2,1,0:T(8,128)(2,1)}, u32[]{:S(2)}) copy-start(bf16[2,960,128]{2,1,0:T(8,128)(2,1)} %copy-done.18) | copy-start | bytes 1474564
  63.8 16.4 %copy-start.3 = (f32[64,512]{1,0:T(8,128)}, f32[64,512]{1,0:T(8,128)S(1)}, u32[]{:S(2)}) copy-start(f32[64,512]{1,0:T(8,128)S(1)} %fusion.1.refs_11_) | copy-start | bytes 393220
  63.8 16.3 %collective-permute-start.19 = (f32[64,512]{1,0:T(8,128)S(1)}, f32[64,512]{1,0:T(8,128)S(1)}, u32[]{:S(2)}, u32[]{:S(2)}) collective-permute-start(f32[64,512]{1,0:T(8,128)S(1)} %fusion.1.refs_11_), channel_id=1, source_target_pairs={{0,8},{8,0},{16,24},{24,16},{32,40},{40,32},{48,56},{56,48},{64,72... | collective-permute-start | bytes 393224 | tf_op jit(solution)/shard_map/ppermute | solution.py:34
  63.9 16.3 %collective-permute-start.16 = (bf16[2,960,128]{2,1,0:T(8,128)(2,1)}, bf16[2,960,128]{2,1,0:T(8,128)(2,1)S(1)}, u32[]{:S(2)}, u32[]{:S(2)}) collective-permute-start(bf16[2,960,128]{2,1,0:T(8,128)(2,1)} %collective-permute-done.4.refs_14_), channel_id=1, source_target_pairs={{0,192},{8,72},{16,208},{24,88},{32,224},{40,104},{48,240},{56,120... | collective-permute-start | bytes 1474568 | tf_op jit(solution)/shard_map/ppermute | solution.py:34
  64.3 15.9 %collective-permute-start.12 = (bf16[2,960,128]{2,1,0:T(8,128)(2,1)S(1)}, bf16[2,960,128]{2,1,0:T(8,128)(2,1)S(1)}, u32[]{:S(2)}, u32[]{:S(2)}) collective-permute-start(bf16[2,960,128]{2,1,0:T(8,128)(2,1)S(1)} %copy-done.19), channel_id=1, source_target_pairs={{0,64},{8,200},{16,80},{24,216},{32,96},{40,232},{48,112},{56,248}... | collective-permute-start | bytes 1474568 | tf_op jit(solution)/shard_map/ppermute | solution.py:34
  67.1 16.4 %collective-permute-start.17 = (bf16[2,960,128]{2,1,0:T(8,128)(2,1)}, bf16[2,960,128]{2,1,0:T(8,128)(2,1)S(1)}, u32[]{:S(2)}, u32[]{:S(2)}) collective-permute-start(bf16[2,960,128]{2,1,0:T(8,128)(2,1)} %collective-permute-done.9.refs_3_), channel_id=1, source_target_pairs={{0,64},{8,200},{16,80},{24,216},{32,96},{40,232},{48,112},{56,248}... | collective-permute-start | bytes 1474568 | tf_op jit(solution)/shard_map/ppermute | solution.py:34
  80.2 3.3 %copy-start.11 = (f32[64,512]{1,0:T(8,128)}, f32[64,512]{1,0:T(8,128)S(1)}, u32[]{:S(2)}) copy-start(f32[64,512]{1,0:T(8,128)S(1)} %collective-permute-done.19.refs_12_) | copy-start | bytes 393220
  80.2 3.3 %copy-start.2 = (bf16[512,896]{0,1:T(8,128)(2,1)}, bf16[512,896]{0,1:T(8,128)(2,1)S(1)}, u32[]{:S(2)}) copy-start(bf16[512,896]{0,1:T(8,128)(2,1)S(1)} %collective-permute-done.18) | copy-start | bytes 2752516
  80.2 3.3 %copy-start.5 = (bf16[2,960,128]{2,1,0:T(8,128)(2,1)}, bf16[2,960,128]{2,1,0:T(8,128)(2,1)S(1)}, u32[]{:S(2)}) copy-start(bf16[2,960,128]{2,1,0:T(8,128)(2,1)S(1)} %collective-permute-done.16.refs_5_) | copy-start | bytes 1474564
  80.2 3.3 %copy-start.6 = (bf16[2,960,128]{2,1,0:T(8,128)(2,1)}, bf16[2,960,128]{2,1,0:T(8,128)(2,1)S(1)}, u32[]{:S(2)}) copy-start(bf16[2,960,128]{2,1,0:T(8,128)(2,1)S(1)} %collective-permute-done.12.refs_4_) | copy-start | bytes 1474564
  83.5 0.8 copy-start.7
  84.3 19.5 %copy-start.8 = (bf16[24,64,128]{2,1,0:T(8,128)(2,1)S(1)}, bf16[24,64,128]{2,1,0:T(8,128)(2,1)}, u32[]{:S(2)}) copy-start(bf16[24,64,128]{2,1,0:T(8,128)(2,1)} %get-tuple-element.34.refs_3_) | copy-start | bytes 1179652
  93.3 2.3 %collective-permute-start.20 = (f32[64,128]{1,0:T(8,128)}, f32[64,128]{1,0:T(8,128)S(1)}, u32[]{:S(2)}, u32[]{:S(2)}) collective-permute-start(f32[64,128]{1,0:T(8,128)} %get-tuple-element.33), channel_id=1, source_target_pairs={{0,8},{8,0},{16,24},{24,16},{32,40},{40,32},{48,56},{56,48},{64,72... | collective-permute-start | bytes 98312 | tf_op jit(solution)/shard_map/ppermute | solution.py:34
  97.1 13.0 %all-to-all-start = ((f32[8,64,128]{2,1,0:T(8,128)}), f32[8,64,128]{2,1,0:T(8,128)S(1)}, u32[]{:S(2)}, u32[]{:S(2)}) async-start(f32[8,64,128]{2,1,0:T(8,128)} %broadcast_in_dim.2), calls=%async_computation | async-start | bytes 524288 | tf_op jit(solution)/shard_map/all_to_all | solution.py:323
  103.8 2.5 %collective-permute-start.21 = (bf16[24,64,128]{2,1,0:T(8,128)(2,1)S(1)}, bf16[24,64,128]{2,1,0:T(8,128)(2,1)S(1)}, u32[]{:S(2)}, u32[]{:S(2)}) collective-permute-start(bf16[24,64,128]{2,1,0:T(8,128)(2,1)S(1)} %copy-done.8), channel_id=1, source_target_pairs={{0,8},{8,0},{16,24},{24,16},{32,40},{40,32},{48,56},{56,48},{64,72... | collective-permute-start | bytes 1179656 | tf_op jit(solution)/shard_map/ppermute | solution.py:34
  104.6 1.7 %collective-permute-start.22 = (bf16[8,64,128]{2,1,0:T(8,128)(2,1)}, bf16[8,64,128]{2,1,0:T(8,128)(2,1)S(1)}, u32[]{:S(2)}, u32[]{:S(2)}) collective-permute-start(bf16[8,64,128]{2,1,0:T(8,128)(2,1)} %get-tuple-element.35.refs_4_), channel_id=1, source_target_pairs={{0,8},{8,0},{16,24},{24,16},{32,40},{40,32},{48,56},{56,48},{64,72... | collective-permute-start | bytes 393224 | tf_op jit(solution)/shard_map/ppermute | solution.py:34
  106.3 3.7 %copy-start.12 = (bf16[8,64,128]{2,1,0:T(8,128)(2,1)}, bf16[8,64,128]{2,1,0:T(8,128)(2,1)S(1)}, u32[]{:S(2)}) copy-start(bf16[8,64,128]{2,1,0:T(8,128)(2,1)S(1)} %collective-permute-done.22.refs_6_) | copy-start | bytes 393220
  106.3 3.7 %copy-start.9 = (bf16[24,64,128]{2,1,0:T(8,128)(2,1)}, bf16[24,64,128]{2,1,0:T(8,128)(2,1)S(1)}, u32[]{:S(2)}) copy-start(bf16[24,64,128]{2,1,0:T(8,128)(2,1)S(1)} %collective-permute-done.21.refs_5_) | copy-start | bytes 1179652
  110.1 0.7 copy-start.1
  130.4 4.3 %copy-start.10 = (bf16[16,16,128]{2,1,0:T(8,128)(2,1)}, bf16[16,16,128]{2,1,0:T(8,128)(2,1)S(1)}, u32[]{:S(2)}) copy-start(bf16[16,16,128]{2,1,0:T(8,128)(2,1)S(1)} %all_to_all.10.mine) | copy-start | bytes 196612
  130.4 4.3 %collective-permute-start.23 = (bf16[16,16,128]{2,1,0:T(8,128)(2,1)S(1)}, bf16[16,16,128]{2,1,0:T(8,128)(2,1)S(1)}, u32[]{:S(2)}, u32[]{:S(2)}) collective-permute-start(bf16[16,16,128]{2,1,0:T(8,128)(2,1)S(1)} %all_to_all.10.mine), channel_id=1, source_target_pairs={{0,8},{8,0},{16,24},{24,16},{32,40},{40,32},{48,56},{56,48},{64,72... | collective-permute-start | bytes 196616 | tf_op jit(solution)/shard_map/ppermute | solution.py:34
  134.7 0.6 copy-start.13

commit v3 on v2

--- a/solution.py
+++ b/solution.py
@@ -18,12 +18,11 @@
 
 
 PLACES = [(x, z, c) for x in range(SIDE) for z in range(SIDE) for c in range(2)]
-SAME_CORE = [[dp_id(x, z, c) for x in range(SIDE) for z in range(SIDE)] for c in range(2)]
 
 
 FROM = (0, -1, 1, -2)
 X_ORDER = [
-    (1, 0), (2, 0), (3, 0), (1, 1), (2, 1), (1, 2), (2, 2), (3, 1), (1, 3), (3, 2), (2, 3), (3, 3),
+    (1, 0), (2, 0), (3, 0), (1, 1), (2, 1), (1, 2), (2, 2), (3, 1), (1, 3), (2, 3), (3, 3),
 ]
 IN_FLIGHT = 3
 ARRIVAL = [(0, 0), (0, 1), (0, 2), (1, 0), (2, 0), (3, 0), (1, 1), (2, 1), (1, 2), (2, 2), (3, 1), (0, 3)]
@@ -184,9 +183,7 @@
     return high, mid, low
 
 
-def send_kernel(parts_count, place, order, parts, *refs):
-    own_queries, other_queries = refs[:parts_count], refs[parts_count:2 * parts_count]
-    payload, raw_scores, wide, left = refs[2 * parts_count:]
+def send_kernel(place, parts, payload, wide):
     sketch = parts[0]
     for k in range(1, 8):
         sketch = sketch + parts[k]
@@ -194,14 +191,20 @@
     whole = wide[...]
     squares = jnp.sum(jnp.sum(whole * whole, axis=0, keepdims=True), axis=1, keepdims=True)
     parts = [v.astype(jnp.float32) for v in split3(jnp.broadcast_to(squares, (1, LANES)))]
-    tails = [[parts[0], parts[1]], [parts[2], jnp.zeros((1, LANES), jnp.float32)]]
+    zero = jnp.zeros((1, LANES), jnp.float32)
+    tails = [parts, [zero] * 3]
     first_col = place[0] * 4
     cols = [[wide[pl.ds(e * 32 + first_col + r, 1), :] for r in range(4)] for e in range(2)]
-    for p in range(16):
+    for p in range(32):
         rows = []
         for e in range(2):
-            rows += cols[e] + [wide[e * 32 + 2 * p:e * 32 + 2 * p + 2, :]] + tails[e]
+            rows += cols[e] + [wide[e * 32 + p:e * 32 + p + 1, :]] + tails[e]
         payload[p] = jnp.concatenate(rows, axis=0).astype(jnp.bfloat16)
+
+
+def scores_kernel(count, place, order, wide, *refs):
+    own_queries, other_queries = refs[:count], refs[count:2 * count]
+    raw_scores, left = refs[2 * count:]
     left[...] = jnp.zeros_like(left)
     raw = []
     for q, queries in enumerate((own_queries, other_queries)):
@@ -218,36 +221,45 @@
     )
 
 
-def send_part(place, sketches, own_queries, other_queries, order):
+def send_part(place, sketches):
     smem, vmem = pl.BlockSpec(memory_space=pltpu.SMEM), pl.BlockSpec(memory_space=pltpu.VMEM)
     return pl.pallas_call(
-        lambda *refs: send_kernel(len(own_queries), *refs),
+        send_kernel,
         out_shape=(
-            jax.ShapeDtypeStruct((16, 16, LANES), jnp.bfloat16),
-            jax.ShapeDtypeStruct((8, LANES), jnp.float32),
+            jax.ShapeDtypeStruct((32, 16, LANES), jnp.bfloat16),
+            jax.ShapeDtypeStruct((64, LANES), jnp.float32),
         ),
+        in_specs=[smem, vmem],
+        out_specs=(vmem, vmem),
+    )(place, sketches)
+
+
+def scores_part(place, order, wide, own_queries, other_queries):
+    smem, vmem = pl.BlockSpec(memory_space=pltpu.SMEM), pl.BlockSpec(memory_space=pltpu.VMEM)
+    return pl.pallas_call(
+        lambda *refs: scores_kernel(len(own_queries), *refs),
+        out_shape=jax.ShapeDtypeStruct((8, LANES), jnp.float32),
         in_specs=[smem, smem] + [vmem] * (1 + 2 * len(own_queries)),
-        out_specs=(vmem, vmem),
-        scratch_shapes=[pltpu.VMEM((64, LANES), jnp.float32), pltpu.VMEM((8, 4096), jnp.float32)],
-    )(place, order, sketches, *own_queries, *other_queries)
-
-
-def gram_kernel(place, mine, other, raw_scores, gram, scores):
+        out_specs=vmem,
+        scratch_shapes=[pltpu.VMEM((8, 4096), jnp.float32)],
+        cost_estimate=pl.CostEstimate(flops=2 * 8 * 4096 * 128, bytes_accessed=2 << 20, transcendentals=0),
+    )(place, order, wide, *own_queries, *other_queries)
+
+
+def gram_kernel(place, mine, raw_scores, gram, scores):
     t, dp = place[0], place[1]
-    odd = (dp % 2) == 1
-    blocks = [mine[...].astype(jnp.float32), other[...].astype(jnp.float32)]
+    wide = mine[...].astype(jnp.float32)
 
     def stack(r):
-        return jnp.concatenate([b[:, e * 8 + r, :] for b in blocks for e in range(2)], axis=0)
+        return jnp.concatenate([wide[:, r, :], wide[:, 8 + r, :]], axis=0).astype(jnp.bfloat16)
 
     trace = jnp.zeros((1, LANES), jnp.float32)
-    for b in blocks:
-        for r in (15, 14, 7, 6):
-            trace = trace + jnp.sum(b[:, r, :], axis=0, keepdims=True)
-    row_part = jnp.where(odd, stack(5), stack(4)).astype(jnp.bfloat16)
+    for r in (7, 6, 5):
+        trace = trace + jnp.sum(wide[:, r, :], axis=0, keepdims=True)
+    row_part = stack(4)
     for r in range(4):
         raw = lax.dot_general(
-            row_part, stack(r).astype(jnp.bfloat16), (((0,), (0,)), ((), ())),
+            row_part, stack(r), (((0,), (0,)), ((), ())),
             preferred_element_type=jnp.float32,
         )
         rows = dp * LANES + lax.broadcasted_iota(jnp.int32, raw.shape, 0)
@@ -256,7 +268,7 @@
     scores[...] = raw_scores[:2, :] / jnp.sqrt(trace / 64.0)
 
 
-def gram_part(place, mine, other, raw_scores):
+def gram_part(place, mine, raw_scores):
     smem, vmem = pl.BlockSpec(memory_space=pltpu.SMEM), pl.BlockSpec(memory_space=pltpu.VMEM)
     return pl.pallas_call(
         gram_kernel,
@@ -264,9 +276,9 @@
             jax.ShapeDtypeStruct((LANES, 512), jnp.float32),
             jax.ShapeDtypeStruct((2, LANES), jnp.float32),
         ),
-        in_specs=[smem, vmem, vmem, vmem],
+        in_specs=[smem, vmem, vmem],
         out_specs=(vmem, vmem),
-    )(place, mine, other, raw_scores)
+    )(place, mine, raw_scores)
 
 
 def halves(value, c, axis):
@@ -288,6 +300,8 @@
         if n >= IN_FLIGHT:
             source = after(source, held[X_ORDER[n - IN_FLIGHT]])
         held[a, b] = x_step(source, -1 if a == 2 else 1)
+        if (a, b) == (3, 0):
+            held[3, 2] = z_step(after(held[3, 0], held[0, 3]), -1)
     return held
 
 
@@ -319,12 +333,13 @@
     own_queries = [early_queries, late_queries]
     other_queries = [core_swap(part) for part in own_queries]
     order = jnp.concatenate([columns(ARRIVAL, c), columns(ARRIVAL, 1 - c)])
-    sketch = own_part + core_swap(other_part)
-    sketches = lax.all_to_all(jnp.broadcast_to(sketch[None], (8,) + sketch.shape), "tensor", 0, 0)
+    eight = lax.optimization_barrier(jnp.broadcast_to(own_part[None], (8,) + own_part.shape))
+    sketches = lax.all_to_all(eight + core_swap(other_part)[None], "tensor", 0, 0)
     place = jnp.stack([tensor, dp]).astype(jnp.int32)
-    payload, raw_scores = send_part(place, sketches, own_queries, other_queries, order)
-    mine = lax.all_to_all(payload, "dp", 0, 0, axis_index_groups=SAME_CORE)
-    return gram_part(place, mine, core_swap(mine), raw_scores)
+    payload, wide = send_part(place, sketches)
+    mine = lax.all_to_all(payload, "dp", 0, 0)
+    raw_scores = scores_part(place, order, wide, own_queries, other_queries)
+    return gram_part(place, mine, raw_scores)
 
 
 def solution(mesh):

time: 138 us -> 132 us (0.957)
  blocking collectives: 17.3 us -> 0 us
  starting transfers between devices: 43.5 us -> 50.1 us
  waiting for transfers between devices: 32 us -> 34.9 us
  Pallas kernels: 24.9 us -> 26.6 us
    all_to_all x1 -> x0, blocking collectives: 17.3 us -> none  [body(): mine = lax.all_to_all(payload, 'dp', 0, 0, axis_index_groups=SAME_CORE)]
    all_to_all x1 -> x2, starting transfers between devices: 6.75 us -> 15.4 us  [the longest x1 8.65 us: body(): mine = lax.all_to_all(payload, 'dp', 0, 0)]
    all_to_all x1 -> x2, waiting for transfers between devices: 3.73 us -> 10.9 us  [the longest x1 5.96 us: body(): mine = lax.all_to_all(payload, 'dp', 0, 0)]
    ppermute x24 -> x23, waiting for transfers between devices: 28.2 us -> 24 us  [dp_move(): lax.ppermute(value, 'dp', [(dp_id(*s), dp_id(*where(*s))) for s in PLACES])]
    ppermute x24 -> x23, starting transfers between devices: 36.8 us -> 34.7 us  [dp_move(): lax.ppermute(value, 'dp', [(dp_id(*s), dp_id(*where(*s))) for s in PLACES])]
    pallas_call x1 -> x2, Pallas kernels: 2.36 us -> 4.03 us  [the longest x1 2.29 us: scores_part(): pl.pallas_call(lambda *refs: scores_kernel(len(own_queries), *refs), out_...]
    unnamed x43 -> x41, local copies, waits for them, and re-layouts: 5.17 us -> 5.77 us
  transfers between devices with their start and end apart: 25 -> 25, of which waited for: 8 -> 7; matrix products, arithmetic and copies ran while one was open for 10% -> 11% of each run, Pallas kernels for 9% -> 12%
where the time goes in v3:
time: 132 us
  starting transfers between devices  50.1 us (38%)
  waiting for transfers between devices  34.9 us (26%)
  Pallas kernels  26.6 us (20%)
  local copies, waits for them, and re-layouts  13.5 us (10%)
  matrix products  3.58 us (3%)
  other arithmetic  2.01 us (2%)
    ppermute x23, starting transfers between devices, dp_move(): lax.ppermute(value, 'dp', [(dp_id(*s), dp_id(*where(*s))) for s in PLACES])  34.7 us
    ppermute x23, waiting for transfers between devices, dp_move(): lax.ppermute(value, 'dp', [(dp_id(*s), dp_id(*where(*s))) for s in PLACES])  24 us
    pallas_call x2, Pallas kernels, grad_part(): pl.pallas_call(lambda *refs: kernel(count, *refs), out_shape=shapes + [qu...  20.7 us
    all_to_all x1, starting transfers between devices, body(): mine = lax.all_to_all(payload, 'dp', 0, 0)  8.65 us
    all_to_all x1, starting transfers between devices, body(): lax.all_to_all(eight + core_swap(other_part)[None], 'tensor', 0, 0)  6.79 us
    all_to_all x1, waiting for transfers between devices, body(): mine = lax.all_to_all(payload, 'dp', 0, 0)  5.96 us
    unnamed x41, local copies, waits for them, and re-layouts  5.77 us
    all_to_all x1, waiting for transfers between devices, body(): lax.all_to_all(eight + core_swap(other_part)[None], 'tensor', 0, 0)  4.93 us
  transfers between devices with their start and end apart: 25, of which 7 were waited for; matrix products, arithmetic and copies ran while one was open for 11% of the time, Pallas kernels for 12%

profile of v3, /device:TPU:1, one launch (start us, length us, event | category | flops | bytes accessed | tf_op | source)
XLA Modules:
  0.0 131.6 jit_solution(685847073501739438)
XLA Ops:
  0.6 0.0 copy-start
  0.6 3.3 %collective-permute-start = (bf16[1792,128]{1,0:T(8,128)(2,1)}, bf16[1792,128]{1,0:T(8,128)(2,1)S(1)}, u32[]{:S(2)}, u32[]{:S(2)}) collective-permute-start(bf16[1792,128]{1,0:T(8,128)(2,1)} %param.10), channel_id=1, source_target_pairs={{0,8},{8,0},{16,24},{24,16},{32,40},{40,32},{48,56},{56,48},{64,72... | collective-permute-start | bytes 1376264 | tf_op jit(solution)/shard_map/ppermute | solution.py:33
  4.0 0.1 collective-permute-start.1
  4.1 0.7 constant_dynamic-slice_fusion.5
  4.8 1.0 constant_dynamic-slice_fusion.6
  5.8 0.0 collective-permute-done.1
  5.9 0.5 collective-permute-start.2
  6.4 0.7 collective-permute-start.6
  7.2 6.0 %collective-permute-start.3 = (bf16[2,960,128]{2,1,0:T(8,128)(2,1)S(1)}, bf16[2,960,128]{2,1,0:T(8,128)(2,1)S(1)}, u32[]{:S(2)}, u32[]{:S(2)}) collective-permute-start(bf16[2,960,128]{2,1,0:T(8,128)(2,1)S(1)} %pad_maximum_fusion.refs_3_), channel_id=1, source_target_pairs={{0,16},{8,56},{16,32},{24,8},{32,48},{40,24},{48,0},{56,40},{64,80... | collective-permute-start | bytes 1474568 | tf_op jit(solution)/shard_map/ppermute | solution.py:33
  13.2 0.0 collective-permute-start.5
  13.2 2.8 %collective-permute-done.6.refs_6_ = bf16[2,960,128]{2,1,0:T(8,128)(2,1)S(1)} collective-permute-done((bf16[2,960,128]{2,1,0:T(8,128)(2,1)S(1)}, bf16[2,960,128]{2,1,0:T(8,128)(2,1)S(1)}, u32[]{:S(2)}, u32[]{:S(2)}) %collective-permute-start.6) | collective-permute-done | bytes 491552 | tf_op jit(solution)/shard_map/ppermute | solution.py:33
  16.0 1.2 collective-permute-start.7
  17.3 14.3 %collective-permute-done.3.refs_4_ = bf16[2,960,128]{2,1,0:T(8,128)(2,1)S(1)} collective-permute-done((bf16[2,960,128]{2,1,0:T(8,128)(2,1)S(1)}, bf16[2,960,128]{2,1,0:T(8,128)(2,1)S(1)}, u32[]{:S(2)}, u32[]{:S(2)}) %collective-permute-start.3) | collective-permute-done | bytes 491552 | tf_op jit(solution)/shard_map/ppermute | solution.py:33
  31.5 0.1 collective-permute-start.11
  31.6 0.0 collective-permute-done.14.refs_7_
  31.6 1.3 %collective-permute-start.15 = (bf16[2,960,128]{2,1,0:T(8,128)(2,1)S(1)}, bf16[2,960,128]{2,1,0:T(8,128)(2,1)S(1)}, u32[]{:S(2)}, u32[]{:S(2)}) collective-permute-start(bf16[2,960,128]{2,1,0:T(8,128)(2,1)S(1)} %collective-permute-done.3.refs_4_), channel_id=1, source_target_pairs={{0,192},{8,72},{16,208},{24,88},{32,224},{40,104},{48,240},{56,120... | collective-permute-start | bytes 1474568 | tf_op jit(solution)/shard_map/ppermute | solution.py:33
  33.0 4.6 %collective-permute-start.4 = (bf16[2,960,128]{2,1,0:T(8,128)(2,1)S(1)}, bf16[2,960,128]{2,1,0:T(8,128)(2,1)}, u32[]{:S(2)}, u32[]{:S(2)}) collective-permute-start(bf16[2,960,128]{2,1,0:T(8,128)(2,1)S(1)} %collective-permute-done.3.refs_4_), channel_id=1, source_target_pairs={{0,16},{8,56},{16,32},{24,8},{32,48},{40,24},{48,0},{56,40},{64,80... | collective-permute-start | bytes 1474568 | tf_op jit(solution)/shard_map/ppermute | solution.py:33
  37.6 0.8 copy-done.14
  38.4 1.5 %collective-permute-start.8 = (bf16[2,960,128]{2,1,0:T(8,128)(2,1)}, bf16[2,960,128]{2,1,0:T(8,128)(2,1)S(1)}, u32[]{:S(2)}, u32[]{:S(2)}) collective-permute-start(bf16[2,960,128]{2,1,0:T(8,128)(2,1)} %collective-permute-done.5.refs_5_), channel_id=1, source_target_pairs={{0,64},{8,200},{16,80},{24,216},{32,96},{40,232},{48,112},{56,248}... | collective-permute-start | bytes 1474568 | tf_op jit(solution)/shard_map/ppermute | solution.py:33
  39.9 0.9 constant_dynamic-slice_fusion
  40.8 0.2 fusion
  41.1 1.1 collective-permute-start.16
  42.2 0.4 collective-permute-start.12
  42.6 5.6 %collective-permute-done.4.refs_14_ = bf16[2,960,128]{2,1,0:T(8,128)(2,1)} collective-permute-done((bf16[2,960,128]{2,1,0:T(8,128)(2,1)S(1)}, bf16[2,960,128]{2,1,0:T(8,128)(2,1)}, u32[]{:S(2)}, u32[]{:S(2)}) %collective-permute-start.4) | collective-permute-done | bytes 491552 | tf_op jit(solution)/shard_map/ppermute | solution.py:33
  48.2 1.5 %collective-permute-start.9 = (bf16[2,960,128]{2,1,0:T(8,128)(2,1)}, bf16[2,960,128]{2,1,0:T(8,128)(2,1)}, u32[]{:S(2)}, u32[]{:S(2)}) collective-permute-start(bf16[2,960,128]{2,1,0:T(8,128)(2,1)} %collective-permute-done.4.refs_14_), channel_id=1, source_target_pairs={{0,64},{8,200},{16,80},{24,216},{32,96},{40,232},{48,112},{56,248}... | collective-permute-start | bytes 1474568 | tf_op jit(solution)/shard_map/ppermute | solution.py:33
  49.8 1.6 %constant_dynamic-slice_fusion.1 = (bf16[512,896]{1,0:T(8,128)(2,1)S(1)}, bf16[512,896]{1,0:T(8,128)(2,1)S(1)}) fusion(bf16[512,1792]{1,0:T(8,128)(2,1)} %param.9, s32[]{:T(128)S(6)} %select_n.457, s32[]{:T(128)S(6)} %select_n.452), kind=kLoop, calls=%fused_computation.8 | loop fusion | bytes 3670024 | tf_op jit(solution)/shard_map/dynamic_slice | solution.py:286
  51.4 0.5 copy.16
  51.9 4.4 %collective-permute-start.18 = (bf16[512,896]{0,1:T(8,128)(2,1)S(1)}, bf16[512,896]{0,1:T(8,128)(2,1)S(1)}, u32[]{:S(2)}, u32[]{:S(2)}) collective-permute-start(bf16[512,896]{0,1:T(8,128)(2,1)S(1)} %copy.16), channel_id=1, source_target_pairs={{0,8},{8,0},{16,24},{24,16},{32,40},{40,32},{48,56},{56,48},{64,72... | collective-permute-start | bytes 2752520 | tf_op jit(solution)/shard_map/ppermute | solution.py:33
  56.3 0.6 pad_maximum_fusion.1.refs_10_
  56.9 1.4 %copy.15 = bf16[512,896]{0,1:T(8,128)(2,1)} copy(bf16[512,896]{1,0:T(8,128)(2,1)S(1)} %get-tuple-element.39) | data formatting | bytes 1835008
  58.3 0.6 stack.255.refs_0_
  58.9 0.7 stack.283.refs_0_
  59.6 3.6 %fusion.1.refs_11_ = f32[64,512]{1,0:T(8,128)S(1)} fusion(bf16[64,4096]{1,0:T(8,128)(2,1)S(1)} %copy-done, bf16[512,4096]{1,0:T(8,128)(2,1)} %param.7), kind=kOutput, calls=%fused_computation.16 | convolution fusion | flops 268435456 | bytes 4849664 | tf_op jit(solution)/shard_map/dot_general | solution.py:317
  63.2 0.1 collective-permute-start.19
  63.3 3.9 %collective-permute-start.10 = (bf16[2,960,128]{2,1,0:T(8,128)(2,1)S(1)}, bf16[2,960,128]{2,1,0:T(8,128)(2,1)S(1)}, u32[]{:S(2)}, u32[]{:S(2)}) collective-permute-start(bf16[2,960,128]{2,1,0:T(8,128)(2,1)S(1)} %copy-done.15), channel_id=1, source_target_pairs={{0,48},{8,24},{16,0},{24,40},{32,16},{40,56},{48,32},{56,8},{64,11... | collective-permute-start | bytes 1474568 | tf_op jit(solution)/shard_map/ppermute | solution.py:33
  67.2 0.7 collective-permute-start.13
  67.9 2.0 %collective-permute-start.17 = (bf16[2,960,128]{2,1,0:T(8,128)(2,1)}, bf16[2,960,128]{2,1,0:T(8,128)(2,1)S(1)}, u32[]{:S(2)}, u32[]{:S(2)}) collective-permute-start(bf16[2,960,128]{2,1,0:T(8,128)(2,1)} %collective-permute-done.9.refs_3_), channel_id=1, source_target_pairs={{0,64},{8,200},{16,80},{24,216},{32,96},{40,232},{48,112},{56,248}... | collective-permute-start | bytes 1474568 | tf_op jit(solution)/shard_map/ppermute | solution.py:33
  69.9 11.7 %shard_map.86 = (f32[4,896,256]{2,1,0:T(8,128)}, bf16[24,64,128]{2,1,0:T(8,128)(2,1)}) custom-call(s32[24]{0:T(128)} %stack.283.refs_0_, bf16[512,4096]{1,0:T(8,128)(2,1)} %refs_1_.3, bf16[512,4096]{1,0:T(8,128)(2,1)} %collective-permute-done.2.refs_2_, bf16[2,960,128]{2,1,0:T(8,128)(2,1)} %copy-done.5, bf16[2,960,128]{2,1,0:T(8,128)(2,1)} %copy-done.16, ...), custom_call_target="tpu_custom_call" | custom-call | flops 5637144576 | bytes 12582912 | tf_op jit(solution)/shard_map/pallas_call | solution.py:165
  81.7 0.6 copy-done.11
  82.3 0.3 copy-done.2
  82.6 0.2 copy-done.6
  82.8 0.2 copy-done.7
  82.9 0.2 copy-done.8
  83.1 9.0 %shard_map.87 = (f32[64,128]{1,0:T(8,128)}, f32[64,128]{1,0:T(8,128)}, bf16[8,64,128]{2,1,0:T(8,128)(2,1)}) custom-call(s32[8]{0:T(128)} %stack.255.refs_0_, bf16[512,4096]{1,0:T(8,128)(2,1)} %refs_1_.3, bf16[512,4096]{1,0:T(8,128)(2,1)} %collective-permute-done.2.refs_2_, bf16[2,960,128]{2,1,0:T(8,128)(2,1)} %collective-permute-done.9.refs_3_, ...), custom_call_target="tpu_custom_call" | custom-call | flops 1879048192 | bytes 4194304 | tf_op jit(solution)/shard_map/pallas_call | solution.py:165
  92.1 0.1 collective-permute-start.20
  92.2 0.8 broadcast_in_dim.2
  93.0 0.6 collective-permute-done.20
  93.6 0.7 broadcast_add_fusion
  94.3 6.8 %all-to-all-start = ((f32[8,64,128]{2,1,0:T(8,128)}), f32[8,64,128]{2,1,0:T(8,128)S(1)}, u32[]{:S(2)}, u32[]{:S(2)}) async-start(f32[8,64,128]{2,1,0:T(8,128)} %broadcast_add_fusion), calls=%async_computation | async-start | bytes 524288 | tf_op jit(solution)/shard_map/all_to_all | solution.py:337
  101.1 0.7 collective-permute-start.21
  101.8 0.6 pad_add_fusion.place.refs_0_
  102.4 4.9 %all-to-all-done.parts = f32[8,64,128]{2,1,0:T(8,128)S(1)} async-done(((f32[8,64,128]{2,1,0:T(8,128)}), f32[8,64,128]{2,1,0:T(8,128)S(1)}, u32[]{:S(2)}, u32[]{:S(2)}) %all-to-all-start) | async-done | bytes 262176 | tf_op jit(solution)/shard_map/all_to_all | solution.py:337
  107.3 0.7 copy-done.1
  108.0 1.7 %shard_map.88 = (bf16[32,16,128]{2,1,0:T(8,128)(2,1)}, f32[64,128]{1,0:T(8,128)}) custom-call(s32[2]{0:T(128)} %pad_add_fusion.place.refs_0_, f32[8,64,128]{2,1,0:T(8,128)} %copy-done.1), custom_call_target="tpu_custom_call" | custom-call | tf_op jit(solution)/shard_map/pallas_call | solution.py:226
  109.8 8.7 %all-to-all-start.1 = ((bf16[32,16,128]{2,1,0:T(8,128)(2,1)}), bf16[32,16,128]{2,1,0:T(8,128)(2,1)S(1)}, u32[]{:S(2)}, u32[]{:S(2)}) async-start(bf16[32,16,128]{2,1,0:T(8,128)(2,1)} %get-tuple-element.34), calls=%async_computation.1 | async-start | bytes 262144 | tf_op jit(solution)/shard_map/all_to_all | solution.py:340
  118.4 0.3 collective-permute-start.22
  118.8 0.7 concatenate.15.refs_1_
  119.4 0.6 collective-permute-done.22.refs_6_
  120.1 0.6 copy-done.12
  120.7 0.2 copy-done.10
  120.9 2.3 %shard_map.89.raw_scores = f32[8,128]{1,0:T(8,128)} custom-call(s32[2]{0:T(128)} %pad_add_fusion.place.refs_0_, s32[64]{0:T(128)} %concatenate.15.refs_1_, f32[64,128]{1,0:T(8,128)} %get-tuple-element.35.refs_2_, bf16[24,64,128]{2,1,0:T(8,128)(2,1)} %get-tuple-element.36.refs_3_, bf16[8,64,128]{2,1,0:T(8,128)(2,1)} %get-tuple-element.37.refs_4_, ...), custom_call_target="tpu_custom_call" | custom-call | flops 8388608 | bytes 2097152 | tf_op jit(solution)/shard_map/pallas_call | solution.py:239
  123.2 6.0 %all-to-all-done.1.mine = bf16[32,16,128]{2,1,0:T(8,128)(2,1)S(1)} async-done(((bf16[32,16,128]{2,1,0:T(8,128)(2,1)}), bf16[32,16,128]{2,1,0:T(8,128)(2,1)S(1)}, u32[]{:S(2)}, u32[]{:S(2)}) %all-to-all-start.1) | async-done | bytes 131104 | tf_op jit(solution)/shard_map/all_to_all | solution.py:340
  129.1 0.6 copy-done.4
  129.8 1.9 %shard_map.90 = (f32[128,512]{1,0:T(8,128)}, f32[2,128]{1,0:T(2,128)}) custom-call(s32[2]{0:T(128)} %pad_add_fusion.place.refs_0_, bf16[32,16,128]{2,1,0:T(8,128)(2,1)} %copy-done.4, f32[8,128]{1,0:T(8,128)} %shard_map.89.raw_scores), custom_call_target="tpu_custom_call" | custom-call | tf_op jit(solution)/shard_map/pallas_call | solution.py:273
  (53 shorter events, 0.3 us)
Async XLA Ops:
  0.6 59.0 %copy-start = (bf16[64,4096]{1,0:T(8,128)(2,1)S(1)}, bf16[64,4096]{1,0:T(8,128)(2,1)}, u32[]{:S(2)}) copy-start(bf16[64,4096]{1,0:T(8,128)(2,1)} %param.11) | copy-start | bytes 1572868
  0.6 5.2 %collective-permute-start = (bf16[1792,128]{1,0:T(8,128)(2,1)}, bf16[1792,128]{1,0:T(8,128)(2,1)S(1)}, u32[]{:S(2)}, u32[]{:S(2)}) collective-permute-start(bf16[1792,128]{1,0:T(8,128)(2,1)} %param.10), channel_id=1, source_target_pairs={{0,8},{8,0},{16,24},{24,16},{32,40},{40,32},{48,56},{56,48},{64,72... | collective-permute-start | bytes 1376264 | tf_op jit(solution)/shard_map/ppermute | solution.py:33
  4.0 1.8 %collective-permute-start.1 = (bf16[128,128]{1,0:T(8,128)(2,1)}, bf16[128,128]{1,0:T(8,128)(2,1)S(1)}, u32[]{:S(2)}, u32[]{:S(2)}) collective-permute-start(bf16[128,128]{1,0:T(8,128)(2,1)} %param.13), channel_id=1, source_target_pairs={{0,8},{8,0},{16,24},{24,16},{32,40},{40,32},{48,56},{56,48},{64,72... | collective-permute-start | bytes 98312 | tf_op jit(solution)/shard_map/ppermute | solution.py:33
  5.9 7.3 %copy-start.5 = (bf16[2,960,128]{2,1,0:T(8,128)(2,1)}, bf16[2,960,128]{2,1,0:T(8,128)(2,1)S(1)}, u32[]{:S(2)}) copy-start(bf16[2,960,128]{2,1,0:T(8,128)(2,1)S(1)} %pad_maximum_fusion.refs_3_) | copy-start | bytes 1474564
  5.9 61.9 %collective-permute-start.2 = (bf16[512,4096]{1,0:T(8,128)(2,1)}, bf16[512,4096]{1,0:T(8,128)(2,1)}, u32[]{:S(2)}, u32[]{:S(2)}) collective-permute-start(bf16[512,4096]{1,0:T(8,128)(2,1)} %refs_1_.3), channel_id=1, source_target_pairs={{0,8},{8,0},{16,24},{24,16},{32,40},{40,32},{48,56},{56,48},{64,72... | collective-permute-start | bytes 12582920 | tf_op jit(solution)/shard_map/ppermute | solution.py:33
  6.4 9.6 %collective-permute-start.6 = (bf16[2,960,128]{2,1,0:T(8,128)(2,1)S(1)}, bf16[2,960,128]{2,1,0:T(8,128)(2,1)S(1)}, u32[]{:S(2)}, u32[]{:S(2)}) collective-permute-start(bf16[2,960,128]{2,1,0:T(8,128)(2,1)S(1)} %pad_maximum_fusion.refs_3_), channel_id=1, source_target_pairs={{0,64},{8,200},{16,80},{24,216},{32,96},{40,232},{48,112},{56,248}... | collective-permute-start | bytes 1474568 | tf_op jit(solution)/shard_map/ppermute | solution.py:33
  7.2 24.3 %collective-permute-start.3 = (bf16[2,960,128]{2,1,0:T(8,128)(2,1)S(1)}, bf16[2,960,128]{2,1,0:T(8,128)(2,1)S(1)}, u32[]{:S(2)}, u32[]{:S(2)}) collective-permute-start(bf16[2,960,128]{2,1,0:T(8,128)(2,1)S(1)} %pad_maximum_fusion.refs_3_), channel_id=1, source_target_pairs={{0,16},{8,56},{16,32},{24,8},{32,48},{40,24},{48,0},{56,40},{64,80... | collective-permute-start | bytes 1474568 | tf_op jit(solution)/shard_map/ppermute | solution.py:33
  13.2 18.4 %collective-permute-start.14 = (bf16[2,960,128]{2,1,0:T(8,128)(2,1)S(1)}, bf16[2,960,128]{2,1,0:T(8,128)(2,1)S(1)}, u32[]{:S(2)}, u32[]{:S(2)}) collective-permute-start(bf16[2,960,128]{2,1,0:T(8,128)(2,1)S(1)} %pad_maximum_fusion.refs_3_), channel_id=1, source_target_pairs={{0,192},{8,72},{16,208},{24,88},{32,224},{40,104},{48,240},{56,120... | collective-permute-start | bytes 1474568 | tf_op jit(solution)/shard_map/ppermute | solution.py:33
  13.2 19.8 %collective-permute-start.5 = (bf16[2,960,128]{2,1,0:T(8,128)(2,1)S(1)}, bf16[2,960,128]{2,1,0:T(8,128)(2,1)}, u32[]{:S(2)}, u32[]{:S(2)}) collective-permute-start(bf16[2,960,128]{2,1,0:T(8,128)(2,1)S(1)} %pad_maximum_fusion.refs_3_), channel_id=1, source_target_pairs={{0,48},{8,24},{16,0},{24,40},{32,16},{40,56},{48,32},{56,8},{64,11... | collective-permute-start | bytes 1474568 | tf_op jit(solution)/shard_map/ppermute | solution.py:33
  16.0 21.6 %copy-start.13 = (bf16[2,960,128]{2,1,0:T(8,128)(2,1)}, bf16[2,960,128]{2,1,0:T(8,128)(2,1)S(1)}, u32[]{:S(2)}) copy-start(bf16[2,960,128]{2,1,0:T(8,128)(2,1)S(1)} %collective-permute-done.6.refs_6_) | copy-start | bytes 1474564
  16.0 21.6 %collective-permute-start.7 = (bf16[2,960,128]{2,1,0:T(8,128)(2,1)S(1)}, bf16[2,960,128]{2,1,0:T(8,128)(2,1)S(1)}, u32[]{:S(2)}, u32[]{:S(2)}) collective-permute-start(bf16[2,960,128]{2,1,0:T(8,128)(2,1)S(1)} %collective-permute-done.6.refs_6_), channel_id=1, source_target_pairs={{0,64},{8,200},{16,80},{24,216},{32,96},{40,232},{48,112},{56,248}... | collective-permute-start | bytes 1474568 | tf_op jit(solution)/shard_map/ppermute | solution.py:33
  31.5 16.7 %copy-start.16 = (bf16[2,960,128]{2,1,0:T(8,128)(2,1)}, bf16[2,960,128]{2,1,0:T(8,128)(2,1)S(1)}, u32[]{:S(2)}) copy-start(bf16[2,960,128]{2,1,0:T(8,128)(2,1)S(1)} %collective-permute-done.3.refs_4_) | copy-start | bytes 1474564
  31.5 9.5 %collective-permute-start.11 = (bf16[2,960,128]{2,1,0:T(8,128)(2,1)S(1)}, bf16[2,960,128]{2,1,0:T(8,128)(2,1)}, u32[]{:S(2)}, u32[]{:S(2)}) collective-permute-start(bf16[2,960,128]{2,1,0:T(8,128)(2,1)S(1)} %collective-permute-done.3.refs_4_), channel_id=1, source_target_pairs={{0,64},{8,200},{16,80},{24,216},{32,96},{40,232},{48,112},{56,248}... | collective-permute-start | bytes 1474568 | tf_op jit(solution)/shard_map/ppermute | solution.py:33
  31.6 6.0 %copy-start.17 = (bf16[2,960,128]{2,1,0:T(8,128)(2,1)}, bf16[2,960,128]{2,1,0:T(8,128)(2,1)S(1)}, u32[]{:S(2)}) copy-start(bf16[2,960,128]{2,1,0:T(8,128)(2,1)S(1)} %collective-permute-done.14.refs_7_) | copy-start | bytes 1474564
  31.6 9.4 %collective-permute-start.15 = (bf16[2,960,128]{2,1,0:T(8,128)(2,1)S(1)}, bf16[2,960,128]{2,1,0:T(8,128)(2,1)S(1)}, u32[]{:S(2)}, u32[]{:S(2)}) collective-permute-start(bf16[2,960,128]{2,1,0:T(8,128)(2,1)S(1)} %collective-permute-done.3.refs_4_), channel_id=1, source_target_pairs={{0,192},{8,72},{16,208},{24,88},{32,224},{40,104},{48,240},{56,120... | collective-permute-start | bytes 1474568 | tf_op jit(solution)/shard_map/ppermute | solution.py:33
  33.0 15.2 %collective-permute-start.4 = (bf16[2,960,128]{2,1,0:T(8,128)(2,1)S(1)}, bf16[2,960,128]{2,1,0:T(8,128)(2,1)}, u32[]{:S(2)}, u32[]{:S(2)}) collective-permute-start(bf16[2,960,128]{2,1,0:T(8,128)(2,1)S(1)} %collective-permute-done.3.refs_4_), channel_id=1, source_target_pairs={{0,16},{8,56},{16,32},{24,8},{32,48},{40,24},{48,0},{56,40},{64,80... | collective-permute-start | bytes 1474568 | tf_op jit(solution)/shard_map/ppermute | solution.py:33
  37.6 0.8 copy-start.14
  38.4 9.8 %collective-permute-start.8 = (bf16[2,960,128]{2,1,0:T(8,128)(2,1)}, bf16[2,960,128]{2,1,0:T(8,128)(2,1)S(1)}, u32[]{:S(2)}, u32[]{:S(2)}) collective-permute-start(bf16[2,960,128]{2,1,0:T(8,128)(2,1)} %collective-permute-done.5.refs_5_), channel_id=1, source_target_pairs={{0,64},{8,200},{16,80},{24,216},{32,96},{40,232},{48,112},{56,248}... | collective-permute-start | bytes 1474568 | tf_op jit(solution)/shard_map/ppermute | solution.py:33
  41.1 7.2 %copy-start.18 = (bf16[2,960,128]{2,1,0:T(8,128)(2,1)}, bf16[2,960,128]{2,1,0:T(8,128)(2,1)S(1)}, u32[]{:S(2)}) copy-start(bf16[2,960,128]{2,1,0:T(8,128)(2,1)S(1)} %collective-permute-done.15.refs_10_) | copy-start | bytes 1474564
  41.1 22.2 %collective-permute-start.16 = (bf16[2,960,128]{2,1,0:T(8,128)(2,1)}, bf16[2,960,128]{2,1,0:T(8,128)(2,1)}, u32[]{:S(2)}, u32[]{:S(2)}) collective-permute-start(bf16[2,960,128]{2,1,0:T(8,128)(2,1)} %collective-permute-done.11.refs_9_), channel_id=1, source_target_pairs={{0,64},{8,200},{16,80},{24,216},{32,96},{40,232},{48,112},{56,248}... | collective-permute-start | bytes 1474568 | tf_op jit(solution)/shard_map/ppermute | solution.py:33
  42.2 21.0 %collective-permute-start.12 = (bf16[2,960,128]{2,1,0:T(8,128)(2,1)}, bf16[2,960,128]{2,1,0:T(8,128)(2,1)}, u32[]{:S(2)}, u32[]{:S(2)}) collective-permute-start(bf16[2,960,128]{2,1,0:T(8,128)(2,1)} %collective-permute-done.5.refs_5_), channel_id=1, source_target_pairs={{0,192},{8,72},{16,208},{24,88},{32,224},{40,104},{48,240},{56,120... | collective-permute-start | bytes 1474568 | tf_op jit(solution)/shard_map/ppermute | solution.py:33
  48.2 3.1 %copy-start.19 = (bf16[2,960,128]{2,1,0:T(8,128)(2,1)}, bf16[2,960,128]{2,1,0:T(8,128)(2,1)S(1)}, u32[]{:S(2)}) copy-start(bf16[2,960,128]{2,1,0:T(8,128)(2,1)S(1)} %collective-permute-done.8.refs_11_) | copy-start | bytes 1474564
  48.2 19.0 %collective-permute-start.9 = (bf16[2,960,128]{2,1,0:T(8,128)(2,1)}, bf16[2,960,128]{2,1,0:T(8,128)(2,1)}, u32[]{:S(2)}, u32[]{:S(2)}) collective-permute-start(bf16[2,960,128]{2,1,0:T(8,128)(2,1)} %collective-permute-done.4.refs_14_), channel_id=1, source_target_pairs={{0,64},{8,200},{16,80},{24,216},{32,96},{40,232},{48,112},{56,248}... | collective-permute-start | bytes 1474568 | tf_op jit(solution)/shard_map/ppermute | solution.py:33
  51.9 29.7 %collective-permute-start.18 = (bf16[512,896]{0,1:T(8,128)(2,1)S(1)}, bf16[512,896]{0,1:T(8,128)(2,1)S(1)}, u32[]{:S(2)}, u32[]{:S(2)}) collective-permute-start(bf16[512,896]{0,1:T(8,128)(2,1)S(1)} %copy.16), channel_id=1, source_target_pairs={{0,8},{8,0},{16,24},{24,16},{32,40},{40,32},{48,56},{56,48},{64,72... | collective-permute-start | bytes 2752520 | tf_op jit(solution)/shard_map/ppermute | solution.py:33
  58.3 5.0 %copy-start.15 = (bf16[2,960,128]{2,1,0:T(8,128)(2,1)S(1)}, bf16[2,960,128]{2,1,0:T(8,128)(2,1)}, u32[]{:S(2)}) copy-start(bf16[2,960,128]{2,1,0:T(8,128)(2,1)} %copy-done.14) | copy-start | bytes 1474564
  63.2 18.4 %copy-start.3 = (f32[64,512]{1,0:T(8,128)}, f32[64,512]{1,0:T(8,128)S(1)}, u32[]{:S(2)}) copy-start(f32[64,512]{1,0:T(8,128)S(1)} %fusion.1.refs_11_) | copy-start | bytes 393220
  63.2 18.4 %collective-permute-start.19 = (f32[64,512]{1,0:T(8,128)S(1)}, f32[64,512]{1,0:T(8,128)S(1)}, u32[]{:S(2)}, u32[]{:S(2)}) collective-permute-start(f32[64,512]{1,0:T(8,128)S(1)} %fusion.1.refs_11_), channel_id=1, source_target_pairs={{0,8},{8,0},{16,24},{24,16},{32,40},{40,32},{48,56},{56,48},{64,72... | collective-permute-start | bytes 393224 | tf_op jit(solution)/shard_map/ppermute | solution.py:33
  63.3 18.3 %collective-permute-start.10 = (bf16[2,960,128]{2,1,0:T(8,128)(2,1)S(1)}, bf16[2,960,128]{2,1,0:T(8,128)(2,1)S(1)}, u32[]{:S(2)}, u32[]{:S(2)}) collective-permute-start(bf16[2,960,128]{2,1,0:T(8,128)(2,1)S(1)} %copy-done.15), channel_id=1, source_target_pairs={{0,48},{8,24},{16,0},{24,40},{32,16},{40,56},{48,32},{56,8},{64,11... | collective-permute-start | bytes 1474568 | tf_op jit(solution)/shard_map/ppermute | solution.py:33
  67.2 14.5 %collective-permute-start.13 = (bf16[2,960,128]{2,1,0:T(8,128)(2,1)}, bf16[2,960,128]{2,1,0:T(8,128)(2,1)S(1)}, u32[]{:S(2)}, u32[]{:S(2)}) collective-permute-start(bf16[2,960,128]{2,1,0:T(8,128)(2,1)} %collective-permute-done.4.refs_14_), channel_id=1, source_target_pairs={{0,192},{8,72},{16,208},{24,88},{32,224},{40,104},{48,240},{56,120... | collective-permute-start | bytes 1474568 | tf_op jit(solution)/shard_map/ppermute | solution.py:33
  67.9 13.8 %collective-permute-start.17 = (bf16[2,960,128]{2,1,0:T(8,128)(2,1)}, bf16[2,960,128]{2,1,0:T(8,128)(2,1)S(1)}, u32[]{:S(2)}, u32[]{:S(2)}) collective-permute-start(bf16[2,960,128]{2,1,0:T(8,128)(2,1)} %collective-permute-done.9.refs_3_), channel_id=1, source_target_pairs={{0,64},{8,200},{16,80},{24,216},{32,96},{40,232},{48,112},{56,248}... | collective-permute-start | bytes 1474568 | tf_op jit(solution)/shard_map/ppermute | solution.py:33
  81.6 0.7 copy-start.11
  81.6 1.0 copy-start.2
  81.7 1.1 copy-start.6
  81.7 1.3 copy-start.7
  81.7 1.4 %copy-start.8 = (bf16[2,960,128]{2,1,0:T(8,128)(2,1)}, bf16[2,960,128]{2,1,0:T(8,128)(2,1)S(1)}, u32[]{:S(2)}) copy-start(bf16[2,960,128]{2,1,0:T(8,128)(2,1)S(1)} %collective-permute-done.17.refs_6_) | copy-start | bytes 1474564
  83.1 18.0 %copy-start.9 = (bf16[24,64,128]{2,1,0:T(8,128)(2,1)S(1)}, bf16[24,64,128]{2,1,0:T(8,128)(2,1)}, u32[]{:S(2)}) copy-start(bf16[24,64,128]{2,1,0:T(8,128)(2,1)} %get-tuple-element.36.refs_3_) | copy-start | bytes 1179652
  92.1 1.5 %collective-permute-start.20 = (f32[64,128]{1,0:T(8,128)}, f32[64,128]{1,0:T(8,128)S(1)}, u32[]{:S(2)}, u32[]{:S(2)}) collective-permute-start(f32[64,128]{1,0:T(8,128)} %get-tuple-element.33), channel_id=1, source_target_pairs={{0,8},{8,0},{16,24},{24,16},{32,40},{40,32},{48,56},{56,48},{64,72... | collective-permute-start | bytes 98312 | tf_op jit(solution)/shard_map/ppermute | solution.py:33
  94.3 13.0 %all-to-all-start = ((f32[8,64,128]{2,1,0:T(8,128)}), f32[8,64,128]{2,1,0:T(8,128)S(1)}, u32[]{:S(2)}, u32[]{:S(2)}) async-start(f32[8,64,128]{2,1,0:T(8,128)} %broadcast_add_fusion), calls=%async_computation | async-start | bytes 524288 | tf_op jit(solution)/shard_map/all_to_all | solution.py:337
  101.1 19.0 %collective-permute-start.21 = (bf16[24,64,128]{2,1,0:T(8,128)(2,1)S(1)}, bf16[24,64,128]{2,1,0:T(8,128)(2,1)S(1)}, u32[]{:S(2)}, u32[]{:S(2)}) collective-permute-start(bf16[24,64,128]{2,1,0:T(8,128)(2,1)S(1)} %copy-done.9), channel_id=1, source_target_pairs={{0,8},{8,0},{16,24},{24,16},{32,40},{40,32},{48,56},{56,48},{64,72... | collective-permute-start | bytes 1179656 | tf_op jit(solution)/shard_map/ppermute | solution.py:33
  107.3 0.7 copy-start.1
  109.8 19.4 %all-to-all-start.1 = ((bf16[32,16,128]{2,1,0:T(8,128)(2,1)}), bf16[32,16,128]{2,1,0:T(8,128)(2,1)S(1)}, u32[]{:S(2)}, u32[]{:S(2)}) async-start(bf16[32,16,128]{2,1,0:T(8,128)(2,1)} %get-tuple-element.34), calls=%async_computation.1 | async-start | bytes 262144 | tf_op jit(solution)/shard_map/all_to_all | solution.py:340
  118.4 1.6 %collective-permute-start.22 = (bf16[8,64,128]{2,1,0:T(8,128)(2,1)}, bf16[8,64,128]{2,1,0:T(8,128)(2,1)S(1)}, u32[]{:S(2)}, u32[]{:S(2)}) collective-permute-start(bf16[8,64,128]{2,1,0:T(8,128)(2,1)} %get-tuple-element.37.refs_4_), channel_id=1, source_target_pairs={{0,8},{8,0},{16,24},{24,16},{32,40},{40,32},{48,56},{56,48},{64,72... | collective-permute-start | bytes 393224 | tf_op jit(solution)/shard_map/ppermute | solution.py:33
  120.1 0.7 copy-start.12
  120.1 0.8 copy-start.10
  129.1 0.7 copy-start.4

commit v4 on v3

--- a/solution.py
+++ b/solution.py
@@ -9,7 +9,7 @@
 SIDE = 4
 LANES = 128
 HALF = 896
-VMEM_BYTES = 56 << 20
+VMEM_BYTES = 36 << 20
 LAST = (((1,), (1,)), ((), ()))
 
 
@@ -86,10 +86,9 @@
     grads, pieces = refs[:2], refs[2:2 + count]
     out, queries, weight, grad, total, sems, out_sem = refs[2 + count:]
     groups = count // SIDE
+    bounds = [SIDE * b for b in range(groups)] + [count]
     moving = [
-        piece_copies(
-            table, grads, pieces[SIDE * b:SIDE * b + SIDE], 2 * SIDE * b, weight, grad, queries, sems.at[b]
-        )
+        piece_copies(table, grads, pieces[bounds[b]:bounds[b + 1]], 2 * bounds[b], weight, grad, queries, sems.at[b])
         for b in range(groups)
     ]
     start(moving[0])
@@ -102,7 +101,7 @@
         @pl.when(table[0] >= 0)
         def _():
             for e in range(4):
-                value = product(weight, grad, range(2 * SIDE * b, 2 * SIDE * (b + 1)), e)
+                value = product(weight, grad, range(2 * bounds[b], 2 * bounds[b + 1]), e)
                 total[e] = value if b == 0 else value + total[e]
     write = pltpu.make_async_copy(total, out, out_sem)
     write.start()
@@ -301,7 +300,7 @@
             source = after(source, held[X_ORDER[n - IN_FLIGHT]])
         held[a, b] = x_step(source, -1 if a == 2 else 1)
         if (a, b) == (3, 0):
-            held[3, 2] = z_step(after(held[3, 0], held[0, 3]), -1)
+            held[3, 2] = z_step(after(held[3, 0], held[0, 2]), -1)
     return held
 
 
@@ -325,7 +324,7 @@
             dp_id(x + sign * FROM[a], z + sign * FROM[b], k) for a, b in keys for k in (core, 1 - core)
         ]).astype(jnp.int32)
 
-    early, late = ARRIVAL[:12], ARRIVAL[12:]
+    early, late = ARRIVAL[:13], ARRIVAL[13:]
     total, early_queries = grad_part(columns(early, c), grads, [held[key] for key in early])
     own_part, other_part, late_queries = grad_part(
         columns(late, c), grads, [held[key] for key in late], (total, *gates, proj_half, *in_projs)

time: 132 us -> 129 us (0.977)
  Pallas kernels: 26.6 us -> 21.6 us
  waiting for transfers between devices: 34.9 us -> 36.7 us
    pallas_call x2, Pallas kernels: 20.7 us -> 15.7 us  [grad_part(): pl.pallas_call(lambda *refs: kernel(count, *refs), out_shape=shapes + [qu...]
    all_to_all x1, starting transfers between devices: 6.79 us -> 4.39 us  [body(): lax.all_to_all(eight + core_swap(other_part)[None], 'tensor', 0, 0)]
    ppermute x23, waiting for transfers between devices: 24 us -> 25.6 us  [dp_move(): lax.ppermute(value, 'dp', [(dp_id(*s), dp_id(*where(*s))) for s in PLACES])]
    ppermute x23, starting transfers between devices: 34.7 us -> 36 us  [dp_move(): lax.ppermute(value, 'dp', [(dp_id(*s), dp_id(*where(*s))) for s in PLACES])]
    all_to_all x1, starting transfers between devices: 8.65 us -> 10 us  [body(): mine = lax.all_to_all(payload, 'dp', 0, 0)]
    unnamed x41 -> x25, local copies, waits for them, and re-layouts: 5.77 us -> 5.48 us
  transfers between devices with their start and end apart: 25 -> 25, of which waited for: 7 -> 9; matrix products, arithmetic and copies ran while one was open for 11% -> 11% of each run, Pallas kernels for 12% -> 11%
where the time goes in v4:
time: 129 us; the launch traced here: 128 us
  starting transfers between devices  50.5 us (39%)
  waiting for transfers between devices  36.7 us (28%)
  Pallas kernels  21.6 us (17%)
  local copies, waits for them, and re-layouts  13.1 us (10%)
  matrix products  3.73 us (3%)
  other arithmetic  1.43 us (1%)
    ppermute x23, starting transfers between devices, dp_move(): lax.ppermute(value, 'dp', [(dp_id(*s), dp_id(*where(*s))) for s in PLACES])  36 us
    ppermute x23, waiting for transfers between devices, dp_move(): lax.ppermute(value, 'dp', [(dp_id(*s), dp_id(*where(*s))) for s in PLACES])  25.6 us
    pallas_call x2, Pallas kernels, grad_part(): pl.pallas_call(lambda *refs: kernel(count, *refs), out_shape=shapes + [qu...  15.7 us
    all_to_all x1, starting transfers between devices, body(): mine = lax.all_to_all(payload, 'dp', 0, 0)  10 us
    all_to_all x1, waiting for transfers between devices, body(): mine = lax.all_to_all(payload, 'dp', 0, 0)  6.23 us
    unnamed x25, local copies, waits for them, and re-layouts  5.48 us
    dynamic_slice x6, local copies, waits for them, and re-layouts, halves(): lax.dynamic_slice_in_dim(value, h * size, size, axis)  5.19 us
    all_to_all x1, waiting for transfers between devices, body(): lax.all_to_all(eight + core_swap(other_part)[None], 'tensor', 0, 0)  4.88 us
  transfers between devices with their start and end apart: 25, of which 9 were waited for; matrix products, arithmetic and copies ran while one was open for 11% of the time, Pallas kernels for 11%

profile of v4, /device:TPU:1, one launch (start us, length us, event | category | flops | bytes accessed | tf_op | source)
XLA Modules:
  0.0 128.0 jit_solution(3300856300711307858)
XLA Ops:
  0.6 0.0 copy-start
  0.6 3.3 %collective-permute-start = (bf16[1792,128]{1,0:T(8,128)(2,1)}, bf16[1792,128]{1,0:T(8,128)(2,1)S(1)}, u32[]{:S(2)}, u32[]{:S(2)}) collective-permute-start(bf16[1792,128]{1,0:T(8,128)(2,1)} %param.10), channel_id=1, source_target_pairs={{0,8},{8,0},{16,24},{24,16},{32,40},{40,32},{48,56},{56,48},{64,72... | collective-permute-start | bytes 1376264 | tf_op jit(solution)/shard_map/ppermute | solution.py:33
  4.0 0.1 collective-permute-start.1
  4.1 0.7 constant_dynamic-slice_fusion.5
  4.8 1.0 constant_dynamic-slice_fusion.6
  5.8 0.0 collective-permute-done.1
  5.9 0.5 collective-permute-start.2
  6.4 0.7 collective-permute-start.3
  7.2 0.7 collective-permute-start.14
  7.9 5.3 %collective-permute-start.7 = (bf16[2,960,128]{2,1,0:T(8,128)(2,1)S(1)}, bf16[2,960,128]{2,1,0:T(8,128)(2,1)S(1)}, u32[]{:S(2)}, u32[]{:S(2)}) collective-permute-start(bf16[2,960,128]{2,1,0:T(8,128)(2,1)S(1)} %pad_maximum_fusion.refs_3_), channel_id=1, source_target_pairs={{0,16},{8,56},{16,32},{24,8},{32,48},{40,24},{48,0},{56,40},{64,80... | collective-permute-start | bytes 1474568 | tf_op jit(solution)/shard_map/ppermute | solution.py:33
  13.2 6.0 %collective-permute-done.3.refs_6_ = bf16[2,960,128]{2,1,0:T(8,128)(2,1)S(1)} collective-permute-done((bf16[2,960,128]{2,1,0:T(8,128)(2,1)S(1)}, bf16[2,960,128]{2,1,0:T(8,128)(2,1)S(1)}, u32[]{:S(2)}, u32[]{:S(2)}) %collective-permute-start.3) | collective-permute-done | bytes 491552 | tf_op jit(solution)/shard_map/ppermute | solution.py:33
  19.2 0.0 collective-permute-start.4
  19.2 2.3 %collective-permute-done.14.refs_7_ = bf16[2,960,128]{2,1,0:T(8,128)(2,1)S(1)} collective-permute-done((bf16[2,960,128]{2,1,0:T(8,128)(2,1)S(1)}, bf16[2,960,128]{2,1,0:T(8,128)(2,1)S(1)}, u32[]{:S(2)}, u32[]{:S(2)}) %collective-permute-start.14) | collective-permute-done | bytes 491552 | tf_op jit(solution)/shard_map/ppermute | solution.py:33
  21.4 0.8 copy-done.4
  22.3 9.2 %collective-permute-done.7.refs_4_ = bf16[2,960,128]{2,1,0:T(8,128)(2,1)S(1)} collective-permute-done((bf16[2,960,128]{2,1,0:T(8,128)(2,1)S(1)}, bf16[2,960,128]{2,1,0:T(8,128)(2,1)S(1)}, u32[]{:S(2)}, u32[]{:S(2)}) %collective-permute-start.7) | collective-permute-done | bytes 491552 | tf_op jit(solution)/shard_map/ppermute | solution.py:33
  31.5 0.4 collective-permute-start.15
  31.9 5.5 %collective-permute-start.9 = (bf16[2,960,128]{2,1,0:T(8,128)(2,1)S(1)}, bf16[2,960,128]{2,1,0:T(8,128)(2,1)}, u32[]{:S(2)}, u32[]{:S(2)}) collective-permute-start(bf16[2,960,128]{2,1,0:T(8,128)(2,1)S(1)} %collective-permute-done.7.refs_4_), channel_id=1, source_target_pairs={{0,64},{8,200},{16,80},{24,216},{32,96},{40,232},{48,112},{56,248}... | collective-permute-start | bytes 1474568 | tf_op jit(solution)/shard_map/ppermute | solution.py:33
  37.4 0.0 collective-permute-done.5.refs_5_
  37.4 4.3 %collective-permute-start.8 = (bf16[2,960,128]{2,1,0:T(8,128)(2,1)S(1)}, bf16[2,960,128]{2,1,0:T(8,128)(2,1)}, u32[]{:S(2)}, u32[]{:S(2)}) collective-permute-start(bf16[2,960,128]{2,1,0:T(8,128)(2,1)S(1)} %collective-permute-done.7.refs_4_), channel_id=1, source_target_pairs={{0,16},{8,56},{16,32},{24,8},{32,48},{40,24},{48,0},{56,40},{64,80... | collective-permute-start | bytes 1474568 | tf_op jit(solution)/shard_map/ppermute | solution.py:33
  41.7 0.0 collective-permute-done.4.refs_8_
  41.7 1.5 %collective-permute-start.12 = (bf16[2,960,128]{2,1,0:T(8,128)(2,1)}, bf16[2,960,128]{2,1,0:T(8,128)(2,1)}, u32[]{:S(2)}, u32[]{:S(2)}) collective-permute-start(bf16[2,960,128]{2,1,0:T(8,128)(2,1)} %collective-permute-done.5.refs_5_), channel_id=1, source_target_pairs={{0,64},{8,200},{16,80},{24,216},{32,96},{40,232},{48,112},{56,248}... | collective-permute-start | bytes 1474568 | tf_op jit(solution)/shard_map/ppermute | solution.py:33
  43.2 0.9 constant_dynamic-slice_fusion
  44.1 0.2 fusion
  44.3 0.0 collective-permute-done.15.refs_10_
  44.3 0.0 collective-permute-done.9.refs_9_
  44.4 2.3 %collective-permute-start.16 = (bf16[2,960,128]{2,1,0:T(8,128)(2,1)}, bf16[2,960,128]{2,1,0:T(8,128)(2,1)}, u32[]{:S(2)}, u32[]{:S(2)}) collective-permute-start(bf16[2,960,128]{2,1,0:T(8,128)(2,1)} %collective-permute-done.9.refs_9_), channel_id=1, source_target_pairs={{0,64},{8,200},{16,80},{24,216},{32,96},{40,232},{48,112},{56,248}... | collective-permute-start | bytes 1474568 | tf_op jit(solution)/shard_map/ppermute | solution.py:33
  46.7 0.0 collective-permute-start.10
  46.7 4.4 %collective-permute-done.8.refs_14_ = bf16[2,960,128]{2,1,0:T(8,128)(2,1)} collective-permute-done((bf16[2,960,128]{2,1,0:T(8,128)(2,1)S(1)}, bf16[2,960,128]{2,1,0:T(8,128)(2,1)}, u32[]{:S(2)}, u32[]{:S(2)}) %collective-permute-start.8) | collective-permute-done | bytes 491552 | tf_op jit(solution)/shard_map/ppermute | solution.py:33
  51.1 2.5 %collective-permute-done.12.refs_11_ = bf16[2,960,128]{2,1,0:T(8,128)(2,1)} collective-permute-done((bf16[2,960,128]{2,1,0:T(8,128)(2,1)}, bf16[2,960,128]{2,1,0:T(8,128)(2,1)}, u32[]{:S(2)}, u32[]{:S(2)}) %collective-permute-start.12) | collective-permute-done | bytes 491552 | tf_op jit(solution)/shard_map/ppermute | solution.py:33
  53.6 3.4 %collective-permute-start.13 = (bf16[2,960,128]{2,1,0:T(8,128)(2,1)}, bf16[2,960,128]{2,1,0:T(8,128)(2,1)}, u32[]{:S(2)}, u32[]{:S(2)}) collective-permute-start(bf16[2,960,128]{2,1,0:T(8,128)(2,1)} %collective-permute-done.8.refs_14_), channel_id=1, source_target_pairs={{0,64},{8,200},{16,80},{24,216},{32,96},{40,232},{48,112},{56,248}... | collective-permute-start | bytes 1474568 | tf_op jit(solution)/shard_map/ppermute | solution.py:33
  57.0 2.6 %constant_dynamic-slice_fusion.1 = (bf16[512,896]{1,0:T(8,128)(2,1)S(1)}, bf16[512,896]{1,0:T(8,128)(2,1)}) fusion(bf16[512,1792]{1,0:T(8,128)(2,1)} %param.9, s32[]{:T(128)S(6)} %select_n.457, s32[]{:T(128)S(6)} %select_n.451), kind=kLoop, calls=%fused_computation.8 | loop fusion | bytes 3670024 | tf_op jit(solution)/shard_map/dynamic_slice | solution.py:285
  59.6 1.3 %copy.16 = bf16[512,896]{0,1:T(8,128)(2,1)} copy(bf16[512,896]{1,0:T(8,128)(2,1)S(1)} %get-tuple-element.38) | data formatting | bytes 1835008 | tf_op jit(solution)/shard_map/optimization_barrier | solution.py:53
  60.9 1.5 %copy.15 = bf16[512,896]{0,1:T(8,128)(2,1)S(1)} copy(bf16[512,896]{1,0:T(8,128)(2,1)} %get-tuple-element.39) | data formatting | bytes 1835008
  62.4 0.1 stack.253.refs_0_
  62.5 0.1 stack.283.refs_0_
  62.6 0.0 copy-start.1
  62.6 0.1 collective-permute-start.18
  62.7 3.7 %fusion.1.refs_10_ = f32[64,512]{1,0:T(8,128)S(1)} fusion(bf16[64,4096]{1,0:T(8,128)(2,1)S(1)} %copy-done, bf16[512,4096]{1,0:T(8,128)(2,1)} %param.7), kind=kOutput, calls=%fused_computation.16 | convolution fusion | flops 268435456 | bytes 4849664 | tf_op jit(solution)/shard_map/dot_general | solution.py:316
  66.4 0.4 collective-permute-start.19
  66.9 0.6 collective-permute-start.6
  67.5 0.6 collective-permute-start.11
  68.0 2.1 %collective-permute-start.17 = (bf16[2,960,128]{2,1,0:T(8,128)(2,1)}, bf16[2,960,128]{2,1,0:T(8,128)(2,1)S(1)}, u32[]{:S(2)}, u32[]{:S(2)}) collective-permute-start(bf16[2,960,128]{2,1,0:T(8,128)(2,1)} %collective-permute-done.13.refs_15_), channel_id=1, source_target_pairs={{0,64},{8,200},{16,80},{24,216},{32,96},{40,232},{48,112},{56,248}... | collective-permute-start | bytes 1474568 | tf_op jit(solution)/shard_map/ppermute | solution.py:33
  70.2 1.0 copy-done.5
  71.2 9.9 %shard_map.86 = (f32[4,896,256]{2,1,0:T(8,128)S(1)}, bf16[26,64,128]{2,1,0:T(8,128)(2,1)S(1)}) custom-call(s32[26]{0:T(128)S(1)} %stack.283.refs_0_, bf16[512,4096]{1,0:T(8,128)(2,1)S(1)} %copy-done.1, bf16[512,4096]{1,0:T(8,128)(2,1)} %collective-permute-done.2.refs_2_, bf16[2,960,128]{2,1,0:T(8,128)(2,1)S(1)} %pad_maximum_fusion.refs_3_, ...), custom_call_target="tpu_custom_call" | custom-call | flops 6106906624 | bytes 13631488 | tf_op jit(solution)/shard_map/pallas_call | solution.py:164
  81.2 5.8 %shard_map.87 = (f32[64,128]{1,0:T(8,128)S(1)}, f32[64,128]{1,0:T(8,128)S(1)}, bf16[6,64,128]{2,1,0:T(8,128)(2,1)S(1)}) custom-call(s32[6]{0:T(128)S(1)} %stack.253.refs_0_, bf16[512,4096]{1,0:T(8,128)(2,1)S(1)} %copy-done.1, bf16[512,4096]{1,0:T(8,128)(2,1)} %collective-permute-done.2.refs_2_, bf16[2,960,128]{2,1,0:T(8,128)(2,1)S(1)} %collective-permute-done.6.refs_3_, ...), custom_call_target="tpu_custom_call" | custom-call | flops 1409286144 | bytes 3145728 | tf_op jit(solution)/shard_map/pallas_call | solution.py:164
  87.0 3.1 %collective-permute-start.20 = (f32[64,128]{1,0:T(8,128)S(1)}, f32[64,128]{1,0:T(8,128)S(1)}, u32[]{:S(2)}, u32[]{:S(2)}) collective-permute-start(f32[64,128]{1,0:T(8,128)S(1)} %get-tuple-element.33), channel_id=1, source_target_pairs={{0,8},{8,0},{16,24},{24,16},{32,40},{40,32},{48,56},{56,48},{64,72... | collective-permute-start | bytes 98312 | tf_op jit(solution)/shard_map/ppermute | solution.py:33
  90.2 0.8 collective-permute-done.20
  91.0 0.7 broadcast_add_fusion
  91.7 4.4 %all-to-all-start = ((f32[8,64,128]{2,1,0:T(8,128)}), f32[8,64,128]{2,1,0:T(8,128)S(1)}, u32[]{:S(2)}, u32[]{:S(2)}) async-start(f32[8,64,128]{2,1,0:T(8,128)} %broadcast_add_fusion), calls=%async_computation | async-start | bytes 524288 | tf_op jit(solution)/shard_map/all_to_all | solution.py:336
  96.1 0.7 collective-permute-start.21
  96.8 0.6 pad_add_fusion.place.refs_0_
  97.4 4.9 %all-to-all-done.parts = f32[8,64,128]{2,1,0:T(8,128)S(1)} async-done(((f32[8,64,128]{2,1,0:T(8,128)}), f32[8,64,128]{2,1,0:T(8,128)S(1)}, u32[]{:S(2)}, u32[]{:S(2)}) %all-to-all-start) | async-done | bytes 262176 | tf_op jit(solution)/shard_map/all_to_all | solution.py:336
  102.3 0.7 copy-done.8
  103.0 1.7 %shard_map.88 = (bf16[32,16,128]{2,1,0:T(8,128)(2,1)}, f32[64,128]{1,0:T(8,128)}) custom-call(s32[2]{0:T(128)} %pad_add_fusion.place.refs_0_, f32[8,64,128]{2,1,0:T(8,128)} %copy-done.8), custom_call_target="tpu_custom_call" | custom-call | tf_op jit(solution)/shard_map/pallas_call | solution.py:225
  104.8 10.0 %all-to-all-start.1 = ((bf16[32,16,128]{2,1,0:T(8,128)(2,1)}), bf16[32,16,128]{2,1,0:T(8,128)(2,1)S(1)}, u32[]{:S(2)}, u32[]{:S(2)}) async-start(bf16[32,16,128]{2,1,0:T(8,128)(2,1)} %get-tuple-element.34), calls=%async_computation.1 | async-start | bytes 262144 | tf_op jit(solution)/shard_map/all_to_all | solution.py:339
  114.8 0.3 collective-permute-start.22
  115.1 0.7 concatenate.15.refs_1_
  115.8 0.3 collective-permute-done.22.refs_6_
  116.2 0.6 copy-done.11
  116.8 0.2 copy-done.10
  117.0 2.3 %shard_map.89.raw_scores = f32[8,128]{1,0:T(8,128)} custom-call(s32[2]{0:T(128)} %pad_add_fusion.place.refs_0_, s32[64]{0:T(128)} %concatenate.15.refs_1_, f32[64,128]{1,0:T(8,128)} %get-tuple-element.35.refs_2_, bf16[26,64,128]{2,1,0:T(8,128)(2,1)} %copy-done.2, bf16[6,64,128]{2,1,0:T(8,128)(2,1)} %copy-done.3, bf16[26,64,128]{2,1,0:T(8,128)(2,1)} %copy-done.10, ...), custom_call_target="tpu_custom_call" | custom-call | flops 8388608 | bytes 2097152 | tf_op jit(solution)/shard_map/pallas_call | solution.py:238
  119.3 6.2 %all-to-all-done.1.mine = bf16[32,16,128]{2,1,0:T(8,128)(2,1)S(1)} async-done(((bf16[32,16,128]{2,1,0:T(8,128)(2,1)}), bf16[32,16,128]{2,1,0:T(8,128)(2,1)S(1)}, u32[]{:S(2)}, u32[]{:S(2)}) %all-to-all-start.1) | async-done | bytes 131104 | tf_op jit(solution)/shard_map/all_to_all | solution.py:339
  125.5 0.7 copy-done.9
  126.1 1.9 %shard_map.90 = (f32[128,512]{1,0:T(8,128)}, f32[2,128]{1,0:T(2,128)}) custom-call(s32[2]{0:T(128)} %pad_add_fusion.place.refs_0_, bf16[32,16,128]{2,1,0:T(8,128)(2,1)} %copy-done.9, f32[8,128]{1,0:T(8,128)} %shard_map.89.raw_scores), custom_call_target="tpu_custom_call" | custom-call | tf_op jit(solution)/shard_map/pallas_call | solution.py:272
  (37 shorter events, 0.3 us)
Async XLA Ops:
  0.6 62.1 %copy-start = (bf16[64,4096]{1,0:T(8,128)(2,1)S(1)}, bf16[64,4096]{1,0:T(8,128)(2,1)}, u32[]{:S(2)}) copy-start(bf16[64,4096]{1,0:T(8,128)(2,1)} %param.11) | copy-start | bytes 1572868
  0.6 5.2 %collective-permute-start = (bf16[1792,128]{1,0:T(8,128)(2,1)}, bf16[1792,128]{1,0:T(8,128)(2,1)S(1)}, u32[]{:S(2)}, u32[]{:S(2)}) collective-permute-start(bf16[1792,128]{1,0:T(8,128)(2,1)} %param.10), channel_id=1, source_target_pairs={{0,8},{8,0},{16,24},{24,16},{32,40},{40,32},{48,56},{56,48},{64,72... | collective-permute-start | bytes 1376264 | tf_op jit(solution)/shard_map/ppermute | solution.py:33
  4.0 1.8 %collective-permute-start.1 = (bf16[128,128]{1,0:T(8,128)(2,1)}, bf16[128,128]{1,0:T(8,128)(2,1)S(1)}, u32[]{:S(2)}, u32[]{:S(2)}) collective-permute-start(bf16[128,128]{1,0:T(8,128)(2,1)} %param.13), channel_id=1, source_target_pairs={{0,8},{8,0},{16,24},{24,16},{32,40},{40,32},{48,56},{56,48},{64,72... | collective-permute-start | bytes 98312 | tf_op jit(solution)/shard_map/ppermute | solution.py:33
  5.9 62.1 %collective-permute-start.2 = (bf16[512,4096]{1,0:T(8,128)(2,1)}, bf16[512,4096]{1,0:T(8,128)(2,1)}, u32[]{:S(2)}, u32[]{:S(2)}) collective-permute-start(bf16[512,4096]{1,0:T(8,128)(2,1)} %refs_1_.3), channel_id=1, source_target_pairs={{0,8},{8,0},{16,24},{24,16},{32,40},{40,32},{48,56},{56,48},{64,72... | collective-permute-start | bytes 12582920 | tf_op jit(solution)/shard_map/ppermute | solution.py:33
  6.4 12.7 %collective-permute-start.3 = (bf16[2,960,128]{2,1,0:T(8,128)(2,1)S(1)}, bf16[2,960,128]{2,1,0:T(8,128)(2,1)S(1)}, u32[]{:S(2)}, u32[]{:S(2)}) collective-permute-start(bf16[2,960,128]{2,1,0:T(8,128)(2,1)S(1)} %pad_maximum_fusion.refs_3_), channel_id=1, source_target_pairs={{0,64},{8,200},{16,80},{24,216},{32,96},{40,232},{48,112},{56,248}... | collective-permute-start | bytes 1474568 | tf_op jit(solution)/shard_map/ppermute | solution.py:33
  7.2 14.3 %collective-permute-start.14 = (bf16[2,960,128]{2,1,0:T(8,128)(2,1)S(1)}, bf16[2,960,128]{2,1,0:T(8,128)(2,1)S(1)}, u32[]{:S(2)}, u32[]{:S(2)}) collective-permute-start(bf16[2,960,128]{2,1,0:T(8,128)(2,1)S(1)} %pad_maximum_fusion.refs_3_), channel_id=1, source_target_pairs={{0,192},{8,72},{16,208},{24,88},{32,224},{40,104},{48,240},{56,120... | collective-permute-start | bytes 1474568 | tf_op jit(solution)/shard_map/ppermute | solution.py:33
  7.9 23.6 %collective-permute-start.7 = (bf16[2,960,128]{2,1,0:T(8,128)(2,1)S(1)}, bf16[2,960,128]{2,1,0:T(8,128)(2,1)S(1)}, u32[]{:S(2)}, u32[]{:S(2)}) collective-permute-start(bf16[2,960,128]{2,1,0:T(8,128)(2,1)S(1)} %pad_maximum_fusion.refs_3_), channel_id=1, source_target_pairs={{0,16},{8,56},{16,32},{24,8},{32,48},{40,24},{48,0},{56,40},{64,80... | collective-permute-start | bytes 1474568 | tf_op jit(solution)/shard_map/ppermute | solution.py:33
  13.2 24.2 %collective-permute-start.5 = (bf16[2,960,128]{2,1,0:T(8,128)(2,1)S(1)}, bf16[2,960,128]{2,1,0:T(8,128)(2,1)}, u32[]{:S(2)}, u32[]{:S(2)}) collective-permute-start(bf16[2,960,128]{2,1,0:T(8,128)(2,1)S(1)} %pad_maximum_fusion.refs_3_), channel_id=1, source_target_pairs={{0,48},{8,24},{16,0},{24,40},{32,16},{40,56},{48,32},{56,8},{64,11... | collective-permute-start | bytes 1474568 | tf_op jit(solution)/shard_map/ppermute | solution.py:33
  19.2 22.5 %collective-permute-start.4 = (bf16[2,960,128]{2,1,0:T(8,128)(2,1)S(1)}, bf16[2,960,128]{2,1,0:T(8,128)(2,1)S(1)}, u32[]{:S(2)}, u32[]{:S(2)}) collective-permute-start(bf16[2,960,128]{2,1,0:T(8,128)(2,1)S(1)} %collective-permute-done.3.refs_6_), channel_id=1, source_target_pairs={{0,64},{8,200},{16,80},{24,216},{32,96},{40,232},{48,112},{56,248}... | collective-permute-start | bytes 1474568 | tf_op jit(solution)/shard_map/ppermute | solution.py:33
  21.4 0.8 copy-start.4
  31.5 29.4 %copy-start.6 = (bf16[2,960,128]{2,1,0:T(8,128)(2,1)}, bf16[2,960,128]{2,1,0:T(8,128)(2,1)S(1)}, u32[]{:S(2)}) copy-start(bf16[2,960,128]{2,1,0:T(8,128)(2,1)S(1)} %collective-permute-done.7.refs_4_) | copy-start | bytes 1474564
  31.5 12.8 %collective-permute-start.15 = (bf16[2,960,128]{2,1,0:T(8,128)(2,1)S(1)}, bf16[2,960,128]{2,1,0:T(8,128)(2,1)}, u32[]{:S(2)}, u32[]{:S(2)}) collective-permute-start(bf16[2,960,128]{2,1,0:T(8,128)(2,1)S(1)} %collective-permute-done.7.refs_4_), channel_id=1, source_target_pairs={{0,192},{8,72},{16,208},{24,88},{32,224},{40,104},{48,240},{56,120... | collective-permute-start | bytes 1474568 | tf_op jit(solution)/shard_map/ppermute | solution.py:33
  31.9 12.5 %collective-permute-start.9 = (bf16[2,960,128]{2,1,0:T(8,128)(2,1)S(1)}, bf16[2,960,128]{2,1,0:T(8,128)(2,1)}, u32[]{:S(2)}, u32[]{:S(2)}) collective-permute-start(bf16[2,960,128]{2,1,0:T(8,128)(2,1)S(1)} %collective-permute-done.7.refs_4_), channel_id=1, source_target_pairs={{0,64},{8,200},{16,80},{24,216},{32,96},{40,232},{48,112},{56,248}... | collective-permute-start | bytes 1474568 | tf_op jit(solution)/shard_map/ppermute | solution.py:33
  37.4 13.7 %collective-permute-start.8 = (bf16[2,960,128]{2,1,0:T(8,128)(2,1)S(1)}, bf16[2,960,128]{2,1,0:T(8,128)(2,1)}, u32[]{:S(2)}, u32[]{:S(2)}) collective-permute-start(bf16[2,960,128]{2,1,0:T(8,128)(2,1)S(1)} %collective-permute-done.7.refs_4_), channel_id=1, source_target_pairs={{0,16},{8,56},{16,32},{24,8},{32,48},{40,24},{48,0},{56,40},{64,80... | collective-permute-start | bytes 1474568 | tf_op jit(solution)/shard_map/ppermute | solution.py:33
  41.7 11.9 %collective-permute-start.12 = (bf16[2,960,128]{2,1,0:T(8,128)(2,1)}, bf16[2,960,128]{2,1,0:T(8,128)(2,1)}, u32[]{:S(2)}, u32[]{:S(2)}) collective-permute-start(bf16[2,960,128]{2,1,0:T(8,128)(2,1)} %collective-permute-done.5.refs_5_), channel_id=1, source_target_pairs={{0,64},{8,200},{16,80},{24,216},{32,96},{40,232},{48,112},{56,248}... | collective-permute-start | bytes 1474568 | tf_op jit(solution)/shard_map/ppermute | solution.py:33
  44.4 22.5 %collective-permute-start.16 = (bf16[2,960,128]{2,1,0:T(8,128)(2,1)}, bf16[2,960,128]{2,1,0:T(8,128)(2,1)}, u32[]{:S(2)}, u32[]{:S(2)}) collective-permute-start(bf16[2,960,128]{2,1,0:T(8,128)(2,1)} %collective-permute-done.9.refs_9_), channel_id=1, source_target_pairs={{0,64},{8,200},{16,80},{24,216},{32,96},{40,232},{48,112},{56,248}... | collective-permute-start | bytes 1474568 | tf_op jit(solution)/shard_map/ppermute | solution.py:33
  46.7 19.8 %collective-permute-start.10 = (bf16[2,960,128]{2,1,0:T(8,128)(2,1)}, bf16[2,960,128]{2,1,0:T(8,128)(2,1)}, u32[]{:S(2)}, u32[]{:S(2)}) collective-permute-start(bf16[2,960,128]{2,1,0:T(8,128)(2,1)} %collective-permute-done.5.refs_5_), channel_id=1, source_target_pairs={{0,192},{8,72},{16,208},{24,88},{32,224},{40,104},{48,240},{56,120... | collective-permute-start | bytes 1474568 | tf_op jit(solution)/shard_map/ppermute | solution.py:33
  53.6 13.9 %collective-permute-start.13 = (bf16[2,960,128]{2,1,0:T(8,128)(2,1)}, bf16[2,960,128]{2,1,0:T(8,128)(2,1)}, u32[]{:S(2)}, u32[]{:S(2)}) collective-permute-start(bf16[2,960,128]{2,1,0:T(8,128)(2,1)} %collective-permute-done.8.refs_14_), channel_id=1, source_target_pairs={{0,64},{8,200},{16,80},{24,216},{32,96},{40,232},{48,112},{56,248}... | collective-permute-start | bytes 1474568 | tf_op jit(solution)/shard_map/ppermute | solution.py:33
  62.6 7.6 %copy-start.1 = (bf16[512,4096]{1,0:T(8,128)(2,1)S(1)}, bf16[512,4096]{1,0:T(8,128)(2,1)}, u32[]{:S(2)}) copy-start(bf16[512,4096]{1,0:T(8,128)(2,1)} %refs_1_.3) | copy-start | bytes 12582916
  62.6 7.6 %copy-start.7 = (bf16[2,960,128]{2,1,0:T(8,128)(2,1)S(1)}, bf16[2,960,128]{2,1,0:T(8,128)(2,1)}, u32[]{:S(2)}) copy-start(bf16[2,960,128]{2,1,0:T(8,128)(2,1)} %copy-done.6) | copy-start | bytes 1474564
  62.6 18.5 %collective-permute-start.18 = (bf16[512,896]{0,1:T(8,128)(2,1)}, bf16[512,896]{0,1:T(8,128)(2,1)S(1)}, u32[]{:S(2)}, u32[]{:S(2)}) collective-permute-start(bf16[512,896]{0,1:T(8,128)(2,1)} %copy.16), channel_id=1, source_target_pairs={{0,8},{8,0},{16,24},{24,16},{32,40},{40,32},{48,56},{56,48},{64,72... | collective-permute-start | bytes 2752520 | tf_op jit(solution)/shard_map/ppermute | solution.py:33
  66.4 14.7 %collective-permute-start.19 = (f32[64,512]{1,0:T(8,128)S(1)}, f32[64,512]{1,0:T(8,128)S(1)}, u32[]{:S(2)}, u32[]{:S(2)}) collective-permute-start(f32[64,512]{1,0:T(8,128)S(1)} %fusion.1.refs_10_), channel_id=1, source_target_pairs={{0,8},{8,0},{16,24},{24,16},{32,40},{40,32},{48,56},{56,48},{64,72... | collective-permute-start | bytes 393224 | tf_op jit(solution)/shard_map/ppermute | solution.py:33
  66.9 14.2 %collective-permute-start.6 = (bf16[2,960,128]{2,1,0:T(8,128)(2,1)S(1)}, bf16[2,960,128]{2,1,0:T(8,128)(2,1)S(1)}, u32[]{:S(2)}, u32[]{:S(2)}) collective-permute-start(bf16[2,960,128]{2,1,0:T(8,128)(2,1)S(1)} %collective-permute-done.4.refs_8_), channel_id=1, source_target_pairs={{0,48},{8,24},{16,0},{24,40},{32,16},{40,56},{48,32},{56,8},{64,11... | collective-permute-start | bytes 1474568 | tf_op jit(solution)/shard_map/ppermute | solution.py:33
  67.5 13.7 %collective-permute-start.11 = (bf16[2,960,128]{2,1,0:T(8,128)(2,1)}, bf16[2,960,128]{2,1,0:T(8,128)(2,1)S(1)}, u32[]{:S(2)}, u32[]{:S(2)}) collective-permute-start(bf16[2,960,128]{2,1,0:T(8,128)(2,1)} %collective-permute-done.8.refs_14_), channel_id=1, source_target_pairs={{0,192},{8,72},{16,208},{24,88},{32,224},{40,104},{48,240},{56,120... | collective-permute-start | bytes 1474568 | tf_op jit(solution)/shard_map/ppermute | solution.py:33
  68.0 13.1 %collective-permute-start.17 = (bf16[2,960,128]{2,1,0:T(8,128)(2,1)}, bf16[2,960,128]{2,1,0:T(8,128)(2,1)S(1)}, u32[]{:S(2)}, u32[]{:S(2)}) collective-permute-start(bf16[2,960,128]{2,1,0:T(8,128)(2,1)} %collective-permute-done.13.refs_15_), channel_id=1, source_target_pairs={{0,64},{8,200},{16,80},{24,216},{32,96},{40,232},{48,112},{56,248}... | collective-permute-start | bytes 1474568 | tf_op jit(solution)/shard_map/ppermute | solution.py:33
  70.2 1.0 copy-start.5
  81.1 15.0 %copy-start.2 = (bf16[26,64,128]{2,1,0:T(8,128)(2,1)}, bf16[26,64,128]{2,1,0:T(8,128)(2,1)S(1)}, u32[]{:S(2)}) copy-start(bf16[26,64,128]{2,1,0:T(8,128)(2,1)S(1)} %get-tuple-element.36.refs_3_) | copy-start | bytes 1277956
  87.0 29.2 %copy-start.3 = (bf16[6,64,128]{2,1,0:T(8,128)(2,1)}, bf16[6,64,128]{2,1,0:T(8,128)(2,1)S(1)}, u32[]{:S(2)}) copy-start(bf16[6,64,128]{2,1,0:T(8,128)(2,1)S(1)} %get-tuple-element.37.refs_4_) | copy-start | bytes 294916
  87.0 4.0 %collective-permute-start.20 = (f32[64,128]{1,0:T(8,128)S(1)}, f32[64,128]{1,0:T(8,128)S(1)}, u32[]{:S(2)}, u32[]{:S(2)}) collective-permute-start(f32[64,128]{1,0:T(8,128)S(1)} %get-tuple-element.33), channel_id=1, source_target_pairs={{0,8},{8,0},{16,24},{24,16},{32,40},{40,32},{48,56},{56,48},{64,72... | collective-permute-start | bytes 98312 | tf_op jit(solution)/shard_map/ppermute | solution.py:33
  91.7 10.6 %all-to-all-start = ((f32[8,64,128]{2,1,0:T(8,128)}), f32[8,64,128]{2,1,0:T(8,128)S(1)}, u32[]{:S(2)}, u32[]{:S(2)}) async-start(f32[8,64,128]{2,1,0:T(8,128)} %broadcast_add_fusion), calls=%async_computation | async-start | bytes 524288 | tf_op jit(solution)/shard_map/all_to_all | solution.py:336
  96.1 20.1 %collective-permute-start.21 = (bf16[26,64,128]{2,1,0:T(8,128)(2,1)S(1)}, bf16[26,64,128]{2,1,0:T(8,128)(2,1)S(1)}, u32[]{:S(2)}, u32[]{:S(2)}) collective-permute-start(bf16[26,64,128]{2,1,0:T(8,128)(2,1)S(1)} %get-tuple-element.36.refs_3_), channel_id=1, source_target_pairs={{0,8},{8,0},{16,24},{24,16},{32,40},{40,32},{48,56},{56,48},{64,72... | collective-permute-start | bytes 1277960 | tf_op jit(solution)/shard_map/ppermute | solution.py:33
  102.3 0.7 copy-start.8
  104.8 20.7 %all-to-all-start.1 = ((bf16[32,16,128]{2,1,0:T(8,128)(2,1)}), bf16[32,16,128]{2,1,0:T(8,128)(2,1)S(1)}, u32[]{:S(2)}, u32[]{:S(2)}) async-start(bf16[32,16,128]{2,1,0:T(8,128)(2,1)} %get-tuple-element.34), calls=%async_computation.1 | async-start | bytes 262144 | tf_op jit(solution)/shard_map/all_to_all | solution.py:339
  114.8 1.4 %collective-permute-start.22 = (bf16[6,64,128]{2,1,0:T(8,128)(2,1)S(1)}, bf16[6,64,128]{2,1,0:T(8,128)(2,1)S(1)}, u32[]{:S(2)}, u32[]{:S(2)}) collective-permute-start(bf16[6,64,128]{2,1,0:T(8,128)(2,1)S(1)} %get-tuple-element.37.refs_4_), channel_id=1, source_target_pairs={{0,8},{8,0},{16,24},{24,16},{32,40},{40,32},{48,56},{56,48},{64,72... | collective-permute-start | bytes 294920 | tf_op jit(solution)/shard_map/ppermute | solution.py:33
  116.2 0.6 copy-start.11
  116.2 0.8 copy-start.10
  125.5 0.7 copy-start.9

commit v5 on v4

--- a/solution.py
+++ b/solution.py
@@ -135,8 +135,12 @@
         sketch = lax.dot_general(
             out_side, in_side, LAST, preferred_element_type=jnp.float32, precision=lax.Precision.HIGHEST
         )
-        out = (out_own, out_other)[e // 2]
-        out[(e % 2) * 32:(e % 2 + 1) * 32, :] = jnp.concatenate([sketch[:32], sketch[32:]], axis=1)
+        rows, block = slice((e % 2) * 32, (e % 2 + 1) * 32), jnp.concatenate([sketch[:32], sketch[32:]], axis=1)
+        if e < 2:
+            for peer in range(8):
+                out_own[peer, rows, :] = block
+        else:
+            out_other[rows, :] = block
 
 
 def grad_part(table, grads, pieces, tail=None):
@@ -152,7 +156,7 @@
     ]
     if tail:
         kernel = late_kernel
-        shapes, out_specs = [jax.ShapeDtypeStruct((64, LANES), jnp.float32)] * 2, [vmem] * 3
+        shapes, out_specs = [jax.ShapeDtypeStruct(s, jnp.float32) for s in ((8, 64, LANES), (64, LANES))], [vmem] * 3
         in_specs = [anywhere] * (5 + count) + [vmem] * 3
         scratch += [pltpu.VMEM(*total), pltpu.VMEM((2, HALF, rows), jnp.bfloat16)]
         scratch += [pltpu.SemaphoreType.DMA, pltpu.SemaphoreType.DMA]
@@ -332,8 +336,7 @@
     own_queries = [early_queries, late_queries]
     other_queries = [core_swap(part) for part in own_queries]
     order = jnp.concatenate([columns(ARRIVAL, c), columns(ARRIVAL, 1 - c)])
-    eight = lax.optimization_barrier(jnp.broadcast_to(own_part[None], (8,) + own_part.shape))
-    sketches = lax.all_to_all(eight + core_swap(other_part)[None], "tensor", 0, 0)
+    sketches = lax.all_to_all(own_part + core_swap(other_part)[None], "tensor", 0, 0)
     place = jnp.stack([tensor, dp]).astype(jnp.int32)
     payload, wide = send_part(place, sketches)
     mine = lax.all_to_all(payload, "dp", 0, 0)

time: 129 us -> 129 us (level)
  no operation moved by 1% of the time
where the time goes in v5:
time: 129 us; the launch traced here: 128 us
  starting transfers between devices  50.5 us (39%)
  waiting for transfers between devices  36.7 us (28%)
  Pallas kernels  21.6 us (17%)
  local copies, waits for them, and re-layouts  13.1 us (10%)
  matrix products  3.73 us (3%)
  other arithmetic  1.43 us (1%)
    ppermute x23, starting transfers between devices, dp_move(): lax.ppermute(value, 'dp', [(dp_id(*s), dp_id(*where(*s))) for s in PLACES])  36 us
    ppermute x23, waiting for transfers between devices, dp_move(): lax.ppermute(value, 'dp', [(dp_id(*s), dp_id(*where(*s))) for s in PLACES])  25.6 us
    pallas_call x2, Pallas kernels, grad_part(): pl.pallas_call(lambda *refs: kernel(count, *refs), out_shape=shapes + [qu...  15.7 us
    all_to_all x1, starting transfers between devices, body(): mine = lax.all_to_all(payload, 'dp', 0, 0)  10 us
    all_to_all x1, waiting for transfers between devices, body(): mine = lax.all_to_all(payload, 'dp', 0, 0)  6.23 us
    unnamed x25, local copies, waits for them, and re-layouts  5.48 us
    dynamic_slice x6, local copies, waits for them, and re-layouts, halves(): lax.dynamic_slice_in_dim(value, h * size, size, axis)  5.19 us
    all_to_all x1, waiting for transfers between devices, body(): lax.all_to_all(own_part + core_swap(other_part)[None], 'tensor', 0, 0)  4.88 us
  transfers between devices with their start and end apart: 25, of which 9 were waited for; matrix products, arithmetic and copies ran while one was open for 11% of the time, Pallas kernels for 11%

profile of v5, /device:TPU:1, one launch (start us, length us, event | category | flops | bytes accessed | tf_op | source)
XLA Modules:
  0.0 128.0 jit_solution(11914224197727218789)
XLA Ops:
  0.6 0.0 copy-start
  0.6 3.3 %collective-permute-start = (bf16[1792,128]{1,0:T(8,128)(2,1)}, bf16[1792,128]{1,0:T(8,128)(2,1)S(1)}, u32[]{:S(2)}, u32[]{:S(2)}) collective-permute-start(bf16[1792,128]{1,0:T(8,128)(2,1)} %param.10), channel_id=1, source_target_pairs={{0,8},{8,0},{16,24},{24,16},{32,40},{40,32},{48,56},{56,48},{64,72... | collective-permute-start | bytes 1376264 | tf_op jit(solution)/shard_map/ppermute | solution.py:33
  4.0 0.1 collective-permute-start.1
  4.1 0.7 constant_dynamic-slice_fusion.5
  4.8 1.0 constant_dynamic-slice_fusion.6
  5.8 0.0 collective-permute-done.1
  5.9 0.5 collective-permute-start.2
  6.4 0.7 collective-permute-start.3
  7.2 0.7 collective-permute-start.14
  7.9 5.3 %collective-permute-start.7 = (bf16[2,960,128]{2,1,0:T(8,128)(2,1)S(1)}, bf16[2,960,128]{2,1,0:T(8,128)(2,1)S(1)}, u32[]{:S(2)}, u32[]{:S(2)}) collective-permute-start(bf16[2,960,128]{2,1,0:T(8,128)(2,1)S(1)} %pad_maximum_fusion.refs_3_), channel_id=1, source_target_pairs={{0,16},{8,56},{16,32},{24,8},{32,48},{40,24},{48,0},{56,40},{64,80... | collective-permute-start | bytes 1474568 | tf_op jit(solution)/shard_map/ppermute | solution.py:33
  13.2 6.0 %collective-permute-done.3.refs_6_ = bf16[2,960,128]{2,1,0:T(8,128)(2,1)S(1)} collective-permute-done((bf16[2,960,128]{2,1,0:T(8,128)(2,1)S(1)}, bf16[2,960,128]{2,1,0:T(8,128)(2,1)S(1)}, u32[]{:S(2)}, u32[]{:S(2)}) %collective-permute-start.3) | collective-permute-done | bytes 491552 | tf_op jit(solution)/shard_map/ppermute | solution.py:33
  19.2 0.0 collective-permute-start.4
  19.2 2.3 %collective-permute-done.14.refs_7_ = bf16[2,960,128]{2,1,0:T(8,128)(2,1)S(1)} collective-permute-done((bf16[2,960,128]{2,1,0:T(8,128)(2,1)S(1)}, bf16[2,960,128]{2,1,0:T(8,128)(2,1)S(1)}, u32[]{:S(2)}, u32[]{:S(2)}) %collective-permute-start.14) | collective-permute-done | bytes 491552 | tf_op jit(solution)/shard_map/ppermute | solution.py:33
  21.4 0.8 copy-done.4
  22.3 9.2 %collective-permute-done.7.refs_4_ = bf16[2,960,128]{2,1,0:T(8,128)(2,1)S(1)} collective-permute-done((bf16[2,960,128]{2,1,0:T(8,128)(2,1)S(1)}, bf16[2,960,128]{2,1,0:T(8,128)(2,1)S(1)}, u32[]{:S(2)}, u32[]{:S(2)}) %collective-permute-start.7) | collective-permute-done | bytes 491552 | tf_op jit(solution)/shard_map/ppermute | solution.py:33
  31.5 0.4 collective-permute-start.15
  31.9 5.5 %collective-permute-start.9 = (bf16[2,960,128]{2,1,0:T(8,128)(2,1)S(1)}, bf16[2,960,128]{2,1,0:T(8,128)(2,1)}, u32[]{:S(2)}, u32[]{:S(2)}) collective-permute-start(bf16[2,960,128]{2,1,0:T(8,128)(2,1)S(1)} %collective-permute-done.7.refs_4_), channel_id=1, source_target_pairs={{0,64},{8,200},{16,80},{24,216},{32,96},{40,232},{48,112},{56,248}... | collective-permute-start | bytes 1474568 | tf_op jit(solution)/shard_map/ppermute | solution.py:33
  37.4 0.0 collective-permute-done.5.refs_5_
  37.4 4.3 %collective-permute-start.8 = (bf16[2,960,128]{2,1,0:T(8,128)(2,1)S(1)}, bf16[2,960,128]{2,1,0:T(8,128)(2,1)}, u32[]{:S(2)}, u32[]{:S(2)}) collective-permute-start(bf16[2,960,128]{2,1,0:T(8,128)(2,1)S(1)} %collective-permute-done.7.refs_4_), channel_id=1, source_target_pairs={{0,16},{8,56},{16,32},{24,8},{32,48},{40,24},{48,0},{56,40},{64,80... | collective-permute-start | bytes 1474568 | tf_op jit(solution)/shard_map/ppermute | solution.py:33
  41.7 0.0 collective-permute-done.4.refs_8_
  41.7 1.5 %collective-permute-start.12 = (bf16[2,960,128]{2,1,0:T(8,128)(2,1)}, bf16[2,960,128]{2,1,0:T(8,128)(2,1)}, u32[]{:S(2)}, u32[]{:S(2)}) collective-permute-start(bf16[2,960,128]{2,1,0:T(8,128)(2,1)} %collective-permute-done.5.refs_5_), channel_id=1, source_target_pairs={{0,64},{8,200},{16,80},{24,216},{32,96},{40,232},{48,112},{56,248}... | collective-permute-start | bytes 1474568 | tf_op jit(solution)/shard_map/ppermute | solution.py:33
  43.2 0.9 constant_dynamic-slice_fusion
  44.1 0.2 fusion
  44.3 0.0 collective-permute-done.15.refs_10_
  44.3 0.0 collective-permute-done.9.refs_9_
  44.4 2.3 %collective-permute-start.16 = (bf16[2,960,128]{2,1,0:T(8,128)(2,1)}, bf16[2,960,128]{2,1,0:T(8,128)(2,1)}, u32[]{:S(2)}, u32[]{:S(2)}) collective-permute-start(bf16[2,960,128]{2,1,0:T(8,128)(2,1)} %collective-permute-done.9.refs_9_), channel_id=1, source_target_pairs={{0,64},{8,200},{16,80},{24,216},{32,96},{40,232},{48,112},{56,248}... | collective-permute-start | bytes 1474568 | tf_op jit(solution)/shard_map/ppermute | solution.py:33
  46.7 0.0 collective-permute-start.10
  46.7 4.4 %collective-permute-done.8.refs_14_ = bf16[2,960,128]{2,1,0:T(8,128)(2,1)} collective-permute-done((bf16[2,960,128]{2,1,0:T(8,128)(2,1)S(1)}, bf16[2,960,128]{2,1,0:T(8,128)(2,1)}, u32[]{:S(2)}, u32[]{:S(2)}) %collective-permute-start.8) | collective-permute-done | bytes 491552 | tf_op jit(solution)/shard_map/ppermute | solution.py:33
  51.1 2.5 %collective-permute-done.12.refs_11_ = bf16[2,960,128]{2,1,0:T(8,128)(2,1)} collective-permute-done((bf16[2,960,128]{2,1,0:T(8,128)(2,1)}, bf16[2,960,128]{2,1,0:T(8,128)(2,1)}, u32[]{:S(2)}, u32[]{:S(2)}) %collective-permute-start.12) | collective-permute-done | bytes 491552 | tf_op jit(solution)/shard_map/ppermute | solution.py:33
  53.6 3.4 %collective-permute-start.13 = (bf16[2,960,128]{2,1,0:T(8,128)(2,1)}, bf16[2,960,128]{2,1,0:T(8,128)(2,1)}, u32[]{:S(2)}, u32[]{:S(2)}) collective-permute-start(bf16[2,960,128]{2,1,0:T(8,128)(2,1)} %collective-permute-done.8.refs_14_), channel_id=1, source_target_pairs={{0,64},{8,200},{16,80},{24,216},{32,96},{40,232},{48,112},{56,248}... | collective-permute-start | bytes 1474568 | tf_op jit(solution)/shard_map/ppermute | solution.py:33
  57.0 2.6 %constant_dynamic-slice_fusion.1 = (bf16[512,896]{1,0:T(8,128)(2,1)S(1)}, bf16[512,896]{1,0:T(8,128)(2,1)}) fusion(bf16[512,1792]{1,0:T(8,128)(2,1)} %param.9, s32[]{:T(128)S(6)} %select_n.457, s32[]{:T(128)S(6)} %select_n.451), kind=kLoop, calls=%fused_computation.8 | loop fusion | bytes 3670024 | tf_op jit(solution)/shard_map/dynamic_slice | solution.py:289
  59.6 1.3 %copy.16 = bf16[512,896]{0,1:T(8,128)(2,1)} copy(bf16[512,896]{1,0:T(8,128)(2,1)S(1)} %get-tuple-element.38) | data formatting | bytes 1835008 | tf_op jit(solution)/shard_map/optimization_barrier | solution.py:53
  60.9 1.5 %copy.15 = bf16[512,896]{0,1:T(8,128)(2,1)S(1)} copy(bf16[512,896]{1,0:T(8,128)(2,1)} %get-tuple-element.39) | data formatting | bytes 1835008
  62.4 0.1 stack.253.refs_0_
  62.5 0.1 stack.283.refs_0_
  62.6 0.0 copy-start.1
  62.6 0.1 collective-permute-start.18
  62.7 3.7 %fusion.1.refs_10_ = f32[64,512]{1,0:T(8,128)S(1)} fusion(bf16[64,4096]{1,0:T(8,128)(2,1)S(1)} %copy-done, bf16[512,4096]{1,0:T(8,128)(2,1)} %param.7), kind=kOutput, calls=%fused_computation.16 | convolution fusion | flops 268435456 | bytes 4849664 | tf_op jit(solution)/shard_map/dot_general | solution.py:320
  66.4 0.4 collective-permute-start.19
  66.9 0.6 collective-permute-start.6
  67.5 0.6 collective-permute-start.11
  68.0 2.1 %collective-permute-start.17 = (bf16[2,960,128]{2,1,0:T(8,128)(2,1)}, bf16[2,960,128]{2,1,0:T(8,128)(2,1)S(1)}, u32[]{:S(2)}, u32[]{:S(2)}) collective-permute-start(bf16[2,960,128]{2,1,0:T(8,128)(2,1)} %collective-permute-done.13.refs_15_), channel_id=1, source_target_pairs={{0,64},{8,200},{16,80},{24,216},{32,96},{40,232},{48,112},{56,248}... | collective-permute-start | bytes 1474568 | tf_op jit(solution)/shard_map/ppermute | solution.py:33
  70.2 1.0 copy-done.5
  71.2 9.9 %shard_map.86 = (f32[4,896,256]{2,1,0:T(8,128)S(1)}, bf16[26,64,128]{2,1,0:T(8,128)(2,1)S(1)}) custom-call(s32[26]{0:T(128)S(1)} %stack.283.refs_0_, bf16[512,4096]{1,0:T(8,128)(2,1)S(1)} %copy-done.1, bf16[512,4096]{1,0:T(8,128)(2,1)} %collective-permute-done.2.refs_2_, bf16[2,960,128]{2,1,0:T(8,128)(2,1)S(1)} %pad_maximum_fusion.refs_3_, ...), custom_call_target="tpu_custom_call" | custom-call | flops 6106906624 | bytes 13631488 | tf_op jit(solution)/shard_map/pallas_call | solution.py:168
  81.2 5.8 %shard_map.87 = (f32[8,64,128]{2,1,0:T(8,128)S(1)}, f32[64,128]{1,0:T(8,128)S(1)}, bf16[6,64,128]{2,1,0:T(8,128)(2,1)S(1)}) custom-call(s32[6]{0:T(128)S(1)} %stack.253.refs_0_, bf16[512,4096]{1,0:T(8,128)(2,1)S(1)} %copy-done.1, bf16[512,4096]{1,0:T(8,128)(2,1)} %collective-permute-done.2.refs_2_, bf16[2,960,128]{2,1,0:T(8,128)(2,1)S(1)} %collective-permute-done.6.refs_3_, ...), custom_call_target="tpu_custom_call" | custom-call | flops 1409286144 | bytes 3145728 | tf_op jit(solution)/shard_map/pallas_call | solution.py:168
  87.0 3.1 %collective-permute-start.20 = (f32[64,128]{1,0:T(8,128)S(1)}, f32[64,128]{1,0:T(8,128)S(1)}, u32[]{:S(2)}, u32[]{:S(2)}) collective-permute-start(f32[64,128]{1,0:T(8,128)S(1)} %get-tuple-element.33), channel_id=1, source_target_pairs={{0,8},{8,0},{16,24},{24,16},{32,40},{40,32},{48,56},{56,48},{64,72... | collective-permute-start | bytes 98312 | tf_op jit(solution)/shard_map/ppermute | solution.py:33
  90.1 0.9 collective-permute-done.20
  91.0 0.7 broadcast_add_fusion
  91.7 4.4 %all-to-all-start = ((f32[8,64,128]{2,1,0:T(8,128)}), f32[8,64,128]{2,1,0:T(8,128)S(1)}, u32[]{:S(2)}, u32[]{:S(2)}) async-start(f32[8,64,128]{2,1,0:T(8,128)} %broadcast_add_fusion), calls=%async_computation | async-start | bytes 524288 | tf_op jit(solution)/shard_map/all_to_all | solution.py:339
  96.1 0.7 collective-permute-start.21
  96.8 0.6 pad_add_fusion.place.refs_0_
  97.4 4.9 %all-to-all-done.parts = f32[8,64,128]{2,1,0:T(8,128)S(1)} async-done(((f32[8,64,128]{2,1,0:T(8,128)}), f32[8,64,128]{2,1,0:T(8,128)S(1)}, u32[]{:S(2)}, u32[]{:S(2)}) %all-to-all-start) | async-done | bytes 262176 | tf_op jit(solution)/shard_map/all_to_all | solution.py:339
  102.3 0.7 copy-done.8
  103.0 1.7 %shard_map.88 = (bf16[32,16,128]{2,1,0:T(8,128)(2,1)}, f32[64,128]{1,0:T(8,128)}) custom-call(s32[2]{0:T(128)} %pad_add_fusion.place.refs_0_, f32[8,64,128]{2,1,0:T(8,128)} %copy-done.8), custom_call_target="tpu_custom_call" | custom-call | tf_op jit(solution)/shard_map/pallas_call | solution.py:229
  104.8 10.0 %all-to-all-start.1 = ((bf16[32,16,128]{2,1,0:T(8,128)(2,1)}), bf16[32,16,128]{2,1,0:T(8,128)(2,1)S(1)}, u32[]{:S(2)}, u32[]{:S(2)}) async-start(bf16[32,16,128]{2,1,0:T(8,128)(2,1)} %get-tuple-element.34), calls=%async_computation.1 | async-start | bytes 262144 | tf_op jit(solution)/shard_map/all_to_all | solution.py:342
  114.8 0.3 collective-permute-start.22
  115.1 0.7 concatenate.15.refs_1_
  115.8 0.3 collective-permute-done.22.refs_6_
  116.2 0.6 copy-done.11
  116.8 0.2 copy-done.10
  117.0 2.3 %shard_map.89.raw_scores = f32[8,128]{1,0:T(8,128)} custom-call(s32[2]{0:T(128)} %pad_add_fusion.place.refs_0_, s32[64]{0:T(128)} %concatenate.15.refs_1_, f32[64,128]{1,0:T(8,128)} %get-tuple-element.35.refs_2_, bf16[26,64,128]{2,1,0:T(8,128)(2,1)} %copy-done.2, bf16[6,64,128]{2,1,0:T(8,128)(2,1)} %copy-done.3, bf16[26,64,128]{2,1,0:T(8,128)(2,1)} %copy-done.10, ...), custom_call_target="tpu_custom_call" | custom-call | flops 8388608 | bytes 2097152 | tf_op jit(solution)/shard_map/pallas_call | solution.py:242
  119.3 6.2 %all-to-all-done.1.mine = bf16[32,16,128]{2,1,0:T(8,128)(2,1)S(1)} async-done(((bf16[32,16,128]{2,1,0:T(8,128)(2,1)}), bf16[32,16,128]{2,1,0:T(8,128)(2,1)S(1)}, u32[]{:S(2)}, u32[]{:S(2)}) %all-to-all-start.1) | async-done | bytes 131104 | tf_op jit(solution)/shard_map/all_to_all | solution.py:342
  125.5 0.7 copy-done.9
  126.1 1.9 %shard_map.90 = (f32[128,512]{1,0:T(8,128)}, f32[2,128]{1,0:T(2,128)}) custom-call(s32[2]{0:T(128)} %pad_add_fusion.place.refs_0_, bf16[32,16,128]{2,1,0:T(8,128)(2,1)} %copy-done.9, f32[8,128]{1,0:T(8,128)} %shard_map.89.raw_scores), custom_call_target="tpu_custom_call" | custom-call | tf_op jit(solution)/shard_map/pallas_call | solution.py:276
  (36 shorter events, 0.3 us)
Async XLA Ops:
  0.6 62.1 %copy-start = (bf16[64,4096]{1,0:T(8,128)(2,1)S(1)}, bf16[64,4096]{1,0:T(8,128)(2,1)}, u32[]{:S(2)}) copy-start(bf16[64,4096]{1,0:T(8,128)(2,1)} %param.11) | copy-start | bytes 1572868
  0.6 5.2 %collective-permute-start = (bf16[1792,128]{1,0:T(8,128)(2,1)}, bf16[1792,128]{1,0:T(8,128)(2,1)S(1)}, u32[]{:S(2)}, u32[]{:S(2)}) collective-permute-start(bf16[1792,128]{1,0:T(8,128)(2,1)} %param.10), channel_id=1, source_target_pairs={{0,8},{8,0},{16,24},{24,16},{32,40},{40,32},{48,56},{56,48},{64,72... | collective-permute-start | bytes 1376264 | tf_op jit(solution)/shard_map/ppermute | solution.py:33
  4.0 1.8 %collective-permute-start.1 = (bf16[128,128]{1,0:T(8,128)(2,1)}, bf16[128,128]{1,0:T(8,128)(2,1)S(1)}, u32[]{:S(2)}, u32[]{:S(2)}) collective-permute-start(bf16[128,128]{1,0:T(8,128)(2,1)} %param.13), channel_id=1, source_target_pairs={{0,8},{8,0},{16,24},{24,16},{32,40},{40,32},{48,56},{56,48},{64,72... | collective-permute-start | bytes 98312 | tf_op jit(solution)/shard_map/ppermute | solution.py:33
  5.9 62.1 %collective-permute-start.2 = (bf16[512,4096]{1,0:T(8,128)(2,1)}, bf16[512,4096]{1,0:T(8,128)(2,1)}, u32[]{:S(2)}, u32[]{:S(2)}) collective-permute-start(bf16[512,4096]{1,0:T(8,128)(2,1)} %refs_1_.3), channel_id=1, source_target_pairs={{0,8},{8,0},{16,24},{24,16},{32,40},{40,32},{48,56},{56,48},{64,72... | collective-permute-start | bytes 12582920 | tf_op jit(solution)/shard_map/ppermute | solution.py:33
  6.4 12.7 %collective-permute-start.3 = (bf16[2,960,128]{2,1,0:T(8,128)(2,1)S(1)}, bf16[2,960,128]{2,1,0:T(8,128)(2,1)S(1)}, u32[]{:S(2)}, u32[]{:S(2)}) collective-permute-start(bf16[2,960,128]{2,1,0:T(8,128)(2,1)S(1)} %pad_maximum_fusion.refs_3_), channel_id=1, source_target_pairs={{0,64},{8,200},{16,80},{24,216},{32,96},{40,232},{48,112},{56,248}... | collective-permute-start | bytes 1474568 | tf_op jit(solution)/shard_map/ppermute | solution.py:33
  7.2 14.3 %collective-permute-start.14 = (bf16[2,960,128]{2,1,0:T(8,128)(2,1)S(1)}, bf16[2,960,128]{2,1,0:T(8,128)(2,1)S(1)}, u32[]{:S(2)}, u32[]{:S(2)}) collective-permute-start(bf16[2,960,128]{2,1,0:T(8,128)(2,1)S(1)} %pad_maximum_fusion.refs_3_), channel_id=1, source_target_pairs={{0,192},{8,72},{16,208},{24,88},{32,224},{40,104},{48,240},{56,120... | collective-permute-start | bytes 1474568 | tf_op jit(solution)/shard_map/ppermute | solution.py:33
  7.9 23.6 %collective-permute-start.7 = (bf16[2,960,128]{2,1,0:T(8,128)(2,1)S(1)}, bf16[2,960,128]{2,1,0:T(8,128)(2,1)S(1)}, u32[]{:S(2)}, u32[]{:S(2)}) collective-permute-start(bf16[2,960,128]{2,1,0:T(8,128)(2,1)S(1)} %pad_maximum_fusion.refs_3_), channel_id=1, source_target_pairs={{0,16},{8,56},{16,32},{24,8},{32,48},{40,24},{48,0},{56,40},{64,80... | collective-permute-start | bytes 1474568 | tf_op jit(solution)/shard_map/ppermute | solution.py:33
  13.2 24.2 %collective-permute-start.5 = (bf16[2,960,128]{2,1,0:T(8,128)(2,1)S(1)}, bf16[2,960,128]{2,1,0:T(8,128)(2,1)}, u32[]{:S(2)}, u32[]{:S(2)}) collective-permute-start(bf16[2,960,128]{2,1,0:T(8,128)(2,1)S(1)} %pad_maximum_fusion.refs_3_), channel_id=1, source_target_pairs={{0,48},{8,24},{16,0},{24,40},{32,16},{40,56},{48,32},{56,8},{64,11... | collective-permute-start | bytes 1474568 | tf_op jit(solution)/shard_map/ppermute | solution.py:33
  19.2 22.5 %collective-permute-start.4 = (bf16[2,960,128]{2,1,0:T(8,128)(2,1)S(1)}, bf16[2,960,128]{2,1,0:T(8,128)(2,1)S(1)}, u32[]{:S(2)}, u32[]{:S(2)}) collective-permute-start(bf16[2,960,128]{2,1,0:T(8,128)(2,1)S(1)} %collective-permute-done.3.refs_6_), channel_id=1, source_target_pairs={{0,64},{8,200},{16,80},{24,216},{32,96},{40,232},{48,112},{56,248}... | collective-permute-start | bytes 1474568 | tf_op jit(solution)/shard_map/ppermute | solution.py:33
  21.4 0.8 copy-start.4
  31.5 29.4 %copy-start.6 = (bf16[2,960,128]{2,1,0:T(8,128)(2,1)}, bf16[2,960,128]{2,1,0:T(8,128)(2,1)S(1)}, u32[]{:S(2)}) copy-start(bf16[2,960,128]{2,1,0:T(8,128)(2,1)S(1)} %collective-permute-done.7.refs_4_) | copy-start | bytes 1474564
  31.5 12.8 %collective-permute-start.15 = (bf16[2,960,128]{2,1,0:T(8,128)(2,1)S(1)}, bf16[2,960,128]{2,1,0:T(8,128)(2,1)}, u32[]{:S(2)}, u32[]{:S(2)}) collective-permute-start(bf16[2,960,128]{2,1,0:T(8,128)(2,1)S(1)} %collective-permute-done.7.refs_4_), channel_id=1, source_target_pairs={{0,192},{8,72},{16,208},{24,88},{32,224},{40,104},{48,240},{56,120... | collective-permute-start | bytes 1474568 | tf_op jit(solution)/shard_map/ppermute | solution.py:33
  31.9 12.5 %collective-permute-start.9 = (bf16[2,960,128]{2,1,0:T(8,128)(2,1)S(1)}, bf16[2,960,128]{2,1,0:T(8,128)(2,1)}, u32[]{:S(2)}, u32[]{:S(2)}) collective-permute-start(bf16[2,960,128]{2,1,0:T(8,128)(2,1)S(1)} %collective-permute-done.7.refs_4_), channel_id=1, source_target_pairs={{0,64},{8,200},{16,80},{24,216},{32,96},{40,232},{48,112},{56,248}... | collective-permute-start | bytes 1474568 | tf_op jit(solution)/shard_map/ppermute | solution.py:33
  37.4 13.7 %collective-permute-start.8 = (bf16[2,960,128]{2,1,0:T(8,128)(2,1)S(1)}, bf16[2,960,128]{2,1,0:T(8,128)(2,1)}, u32[]{:S(2)}, u32[]{:S(2)}) collective-permute-start(bf16[2,960,128]{2,1,0:T(8,128)(2,1)S(1)} %collective-permute-done.7.refs_4_), channel_id=1, source_target_pairs={{0,16},{8,56},{16,32},{24,8},{32,48},{40,24},{48,0},{56,40},{64,80... | collective-permute-start | bytes 1474568 | tf_op jit(solution)/shard_map/ppermute | solution.py:33
  41.7 11.9 %collective-permute-start.12 = (bf16[2,960,128]{2,1,0:T(8,128)(2,1)}, bf16[2,960,128]{2,1,0:T(8,128)(2,1)}, u32[]{:S(2)}, u32[]{:S(2)}) collective-permute-start(bf16[2,960,128]{2,1,0:T(8,128)(2,1)} %collective-permute-done.5.refs_5_), channel_id=1, source_target_pairs={{0,64},{8,200},{16,80},{24,216},{32,96},{40,232},{48,112},{56,248}... | collective-permute-start | bytes 1474568 | tf_op jit(solution)/shard_map/ppermute | solution.py:33
  44.4 22.5 %collective-permute-start.16 = (bf16[2,960,128]{2,1,0:T(8,128)(2,1)}, bf16[2,960,128]{2,1,0:T(8,128)(2,1)}, u32[]{:S(2)}, u32[]{:S(2)}) collective-permute-start(bf16[2,960,128]{2,1,0:T(8,128)(2,1)} %collective-permute-done.9.refs_9_), channel_id=1, source_target_pairs={{0,64},{8,200},{16,80},{24,216},{32,96},{40,232},{48,112},{56,248}... | collective-permute-start | bytes 1474568 | tf_op jit(solution)/shard_map/ppermute | solution.py:33
  46.7 19.8 %collective-permute-start.10 = (bf16[2,960,128]{2,1,0:T(8,128)(2,1)}, bf16[2,960,128]{2,1,0:T(8,128)(2,1)}, u32[]{:S(2)}, u32[]{:S(2)}) collective-permute-start(bf16[2,960,128]{2,1,0:T(8,128)(2,1)} %collective-permute-done.5.refs_5_), channel_id=1, source_target_pairs={{0,192},{8,72},{16,208},{24,88},{32,224},{40,104},{48,240},{56,120... | collective-permute-start | bytes 1474568 | tf_op jit(solution)/shard_map/ppermute | solution.py:33
  53.6 13.9 %collective-permute-start.13 = (bf16[2,960,128]{2,1,0:T(8,128)(2,1)}, bf16[2,960,128]{2,1,0:T(8,128)(2,1)}, u32[]{:S(2)}, u32[]{:S(2)}) collective-permute-start(bf16[2,960,128]{2,1,0:T(8,128)(2,1)} %collective-permute-done.8.refs_14_), channel_id=1, source_target_pairs={{0,64},{8,200},{16,80},{24,216},{32,96},{40,232},{48,112},{56,248}... | collective-permute-start | bytes 1474568 | tf_op jit(solution)/shard_map/ppermute | solution.py:33
  62.6 7.6 %copy-start.1 = (bf16[512,4096]{1,0:T(8,128)(2,1)S(1)}, bf16[512,4096]{1,0:T(8,128)(2,1)}, u32[]{:S(2)}) copy-start(bf16[512,4096]{1,0:T(8,128)(2,1)} %refs_1_.3) | copy-start | bytes 12582916
  62.6 7.6 %copy-start.7 = (bf16[2,960,128]{2,1,0:T(8,128)(2,1)S(1)}, bf16[2,960,128]{2,1,0:T(8,128)(2,1)}, u32[]{:S(2)}) copy-start(bf16[2,960,128]{2,1,0:T(8,128)(2,1)} %copy-done.6) | copy-start | bytes 1474564
  62.6 18.5 %collective-permute-start.18 = (bf16[512,896]{0,1:T(8,128)(2,1)}, bf16[512,896]{0,1:T(8,128)(2,1)S(1)}, u32[]{:S(2)}, u32[]{:S(2)}) collective-permute-start(bf16[512,896]{0,1:T(8,128)(2,1)} %copy.16), channel_id=1, source_target_pairs={{0,8},{8,0},{16,24},{24,16},{32,40},{40,32},{48,56},{56,48},{64,72... | collective-permute-start | bytes 2752520 | tf_op jit(solution)/shard_map/ppermute | solution.py:33
  66.4 14.7 %collective-permute-start.19 = (f32[64,512]{1,0:T(8,128)S(1)}, f32[64,512]{1,0:T(8,128)S(1)}, u32[]{:S(2)}, u32[]{:S(2)}) collective-permute-start(f32[64,512]{1,0:T(8,128)S(1)} %fusion.1.refs_10_), channel_id=1, source_target_pairs={{0,8},{8,0},{16,24},{24,16},{32,40},{40,32},{48,56},{56,48},{64,72... | collective-permute-start | bytes 393224 | tf_op jit(solution)/shard_map/ppermute | solution.py:33
  66.9 14.2 %collective-permute-start.6 = (bf16[2,960,128]{2,1,0:T(8,128)(2,1)S(1)}, bf16[2,960,128]{2,1,0:T(8,128)(2,1)S(1)}, u32[]{:S(2)}, u32[]{:S(2)}) collective-permute-start(bf16[2,960,128]{2,1,0:T(8,128)(2,1)S(1)} %collective-permute-done.4.refs_8_), channel_id=1, source_target_pairs={{0,48},{8,24},{16,0},{24,40},{32,16},{40,56},{48,32},{56,8},{64,11... | collective-permute-start | bytes 1474568 | tf_op jit(solution)/shard_map/ppermute | solution.py:33
  67.5 13.7 %collective-permute-start.11 = (bf16[2,960,128]{2,1,0:T(8,128)(2,1)}, bf16[2,960,128]{2,1,0:T(8,128)(2,1)S(1)}, u32[]{:S(2)}, u32[]{:S(2)}) collective-permute-start(bf16[2,960,128]{2,1,0:T(8,128)(2,1)} %collective-permute-done.8.refs_14_), channel_id=1, source_target_pairs={{0,192},{8,72},{16,208},{24,88},{32,224},{40,104},{48,240},{56,120... | collective-permute-start | bytes 1474568 | tf_op jit(solution)/shard_map/ppermute | solution.py:33
  68.0 13.1 %collective-permute-start.17 = (bf16[2,960,128]{2,1,0:T(8,128)(2,1)}, bf16[2,960,128]{2,1,0:T(8,128)(2,1)S(1)}, u32[]{:S(2)}, u32[]{:S(2)}) collective-permute-start(bf16[2,960,128]{2,1,0:T(8,128)(2,1)} %collective-permute-done.13.refs_15_), channel_id=1, source_target_pairs={{0,64},{8,200},{16,80},{24,216},{32,96},{40,232},{48,112},{56,248}... | collective-permute-start | bytes 1474568 | tf_op jit(solution)/shard_map/ppermute | solution.py:33
  70.2 1.0 copy-start.5
  81.1 15.0 %copy-start.2 = (bf16[26,64,128]{2,1,0:T(8,128)(2,1)}, bf16[26,64,128]{2,1,0:T(8,128)(2,1)S(1)}, u32[]{:S(2)}) copy-start(bf16[26,64,128]{2,1,0:T(8,128)(2,1)S(1)} %get-tuple-element.36.refs_3_) | copy-start | bytes 1277956
  87.0 29.2 %copy-start.3 = (bf16[6,64,128]{2,1,0:T(8,128)(2,1)}, bf16[6,64,128]{2,1,0:T(8,128)(2,1)S(1)}, u32[]{:S(2)}) copy-start(bf16[6,64,128]{2,1,0:T(8,128)(2,1)S(1)} %get-tuple-element.37.refs_4_) | copy-start | bytes 294916
  87.0 4.0 %collective-permute-start.20 = (f32[64,128]{1,0:T(8,128)S(1)}, f32[64,128]{1,0:T(8,128)S(1)}, u32[]{:S(2)}, u32[]{:S(2)}) collective-permute-start(f32[64,128]{1,0:T(8,128)S(1)} %get-tuple-element.33), channel_id=1, source_target_pairs={{0,8},{8,0},{16,24},{24,16},{32,40},{40,32},{48,56},{56,48},{64,72... | collective-permute-start | bytes 98312 | tf_op jit(solution)/shard_map/ppermute | solution.py:33
  91.7 10.6 %all-to-all-start = ((f32[8,64,128]{2,1,0:T(8,128)}), f32[8,64,128]{2,1,0:T(8,128)S(1)}, u32[]{:S(2)}, u32[]{:S(2)}) async-start(f32[8,64,128]{2,1,0:T(8,128)} %broadcast_add_fusion), calls=%async_computation | async-start | bytes 524288 | tf_op jit(solution)/shard_map/all_to_all | solution.py:339
  96.1 20.1 %collective-permute-start.21 = (bf16[26,64,128]{2,1,0:T(8,128)(2,1)S(1)}, bf16[26,64,128]{2,1,0:T(8,128)(2,1)S(1)}, u32[]{:S(2)}, u32[]{:S(2)}) collective-permute-start(bf16[26,64,128]{2,1,0:T(8,128)(2,1)S(1)} %get-tuple-element.36.refs_3_), channel_id=1, source_target_pairs={{0,8},{8,0},{16,24},{24,16},{32,40},{40,32},{48,56},{56,48},{64,72... | collective-permute-start | bytes 1277960 | tf_op jit(solution)/shard_map/ppermute | solution.py:33
  102.3 0.7 copy-start.8
  104.8 20.7 %all-to-all-start.1 = ((bf16[32,16,128]{2,1,0:T(8,128)(2,1)}), bf16[32,16,128]{2,1,0:T(8,128)(2,1)S(1)}, u32[]{:S(2)}, u32[]{:S(2)}) async-start(bf16[32,16,128]{2,1,0:T(8,128)(2,1)} %get-tuple-element.34), calls=%async_computation.1 | async-start | bytes 262144 | tf_op jit(solution)/shard_map/all_to_all | solution.py:342
  114.8 1.4 %collective-permute-start.22 = (bf16[6,64,128]{2,1,0:T(8,128)(2,1)S(1)}, bf16[6,64,128]{2,1,0:T(8,128)(2,1)S(1)}, u32[]{:S(2)}, u32[]{:S(2)}) collective-permute-start(bf16[6,64,128]{2,1,0:T(8,128)(2,1)S(1)} %get-tuple-element.37.refs_4_), channel_id=1, source_target_pairs={{0,8},{8,0},{16,24},{24,16},{32,40},{40,32},{48,56},{56,48},{64,72... | collective-permute-start | bytes 294920 | tf_op jit(solution)/shard_map/ppermute | solution.py:33
  116.2 0.6 copy-start.11
  116.2 0.8 copy-start.10
  125.5 0.7 copy-start.9
